TPU v7x, 256 devices: a whole 4x4x8 slice. The times are simulated.
256 devices in a mesh: tm: 128 (over x, y, z), head: 2 (over core).
Axes of the slice: x: 4, y: 4, z: 8, core: 2. Of those that a mesh axis runs over, the one named last changes fastest.
Arguments:
- video: bfloat16 [128, 128, 1024], P('tm'), may hold values from -12 to 12
- assign: int32 [128, 128], P('tm'), may hold values from 0 to 31, as said below
- w_query: bfloat16 [1024, 1024], replicated, may hold values from -0.1875 to 0.1875
- w_key: bfloat16 [1024, 1024], replicated, may hold values from -0.1875 to 0.1875
- w_value: bfloat16 [1024, 1024], replicated, may hold values from -0.1875 to 0.1875
- w_out: bfloat16 [1024, 1024], replicated, may hold values from -0.1875 to 0.1875
- cotangent: bfloat16 [128, 128, 1024], P('tm'), may hold values from -6 to 6
Outputs:
- attended: bfloat16 [128, 128, 1024], P('tm', None, 'head')
- video_grad: bfloat16 [128, 128, 1024], P('tm', None, 'head')
Inputs may be any that keep to these rules, and one draw needn't show every extreme that they name: `assign`: every memory row of every segment is named by at least one token.
All inputs are finite; a program needn't handle non-finite values.
Results may differ from a plain program's by a relative error of at most 0.013.
The roundings to bfloat16 on the way count: a program that leaves them out, or rounds other values in their place, can miss the bound.
Values may be sent and summed in bfloat16 or wider, within the bound.
No kernel may reach another device: no remote copies, remote signals or barrier semaphores. Data moves between devices by JAX's collectives and lax.ppermute only.
A program may use at most 128 MiB of HBM per device.

v0:
```python
import jax
import jax.numpy as jnp
from jax import lax
from jax.sharding import PartitionSpec as P

HEAD_DIM = 64
MEM = 32


def times_transposed(matrix, weight):
    return lax.dot_general(
        matrix, weight, (((1,), (1,)), ((), ())), preferred_element_type=jnp.float32
    )


def merge_heads(stacked):
    return jnp.transpose(stacked, (1, 0, 2)).reshape(stacked.shape[1], -1)


def shards(video, assign, w_query, w_key, w_value, w_out, cotangent):
    head_groups = lax.axis_size("head")
    head_index = lax.axis_index("head")
    segment_index = lax.axis_index("tm")
    tokens = video[0]
    token_count = tokens.shape[0]
    model_width = tokens.shape[1]
    local_width = model_width // head_groups
    local_heads = local_width // HEAD_DIM
    score_scale = HEAD_DIM ** (-0.5)

    def columns(weight):
        return lax.dynamic_slice_in_dim(weight, head_index * local_width, local_width, 1)

    wq_local = columns(w_query)
    wk_local = columns(w_key)
    wv_local = columns(w_value)
    wo_rows = lax.dynamic_slice_in_dim(w_out, head_index * local_width, local_width, 0)

    def project(weight):
        return jnp.dot(tokens, weight, preferred_element_type=jnp.float32).astype(jnp.bfloat16)

    queries = project(wq_local)
    own_keys = project(wk_local)
    own_values = project(wv_local)
    labels = assign[0]
    onehot = labels[:, None] == jnp.arange(MEM, dtype=jnp.int32)[None, :]
    counts = jnp.sum(onehot.astype(jnp.float32), axis=0)
    summed = lax.dot_general(
        onehot.astype(jnp.bfloat16),
        tokens,
        (((0,), (0,)), ((), ())),
        preferred_element_type=jnp.float32,
    )
    memory = (summed / counts[:, None]).astype(jnp.bfloat16)
    mem_keys = jnp.dot(memory, wk_local, preferred_element_type=jnp.float32).astype(jnp.bfloat16)
    mem_values = jnp.dot(memory, wv_local, preferred_element_type=jnp.float32).astype(jnp.bfloat16)
    all_mkeys, all_mvalues = (
        lax.all_gather(mem_keys, "tm", axis=0, tiled=True),
        lax.all_gather(mem_values, "tm", axis=0, tiled=True),
    )
    prior_rows = all_mkeys.shape[0]
    key_rows = jnp.concatenate([all_mkeys, own_keys], axis=0)
    value_rows = jnp.concatenate([all_mvalues, own_values], axis=0)
    key_index = jnp.arange(prior_rows + token_count, dtype=jnp.int32)
    visible = ((key_index < segment_index * MEM) | (key_index >= prior_rows))[None, :]

    def head_cols(matrix, head):
        return lax.dynamic_slice_in_dim(matrix, head * HEAD_DIM, HEAD_DIM, 1)

    def scores_of(head):
        query_head = head_cols(queries, head)
        key_head = head_cols(key_rows, head)
        scores = times_transposed(query_head, key_head) * score_scale
        return (query_head, key_head, scores)

    def forward_head(head):
        query_head, key_head, scores = scores_of(head)
        row_max = jnp.max(jnp.where(visible, scores, -jnp.inf), axis=1, keepdims=True)
        raised = jnp.where(visible, jnp.exp(scores - row_max), 0.0)
        row_total = jnp.sum(raised, axis=1, keepdims=True)
        weights = (raised / row_total).astype(jnp.bfloat16)
        out_head = jnp.dot(weights, head_cols(value_rows, head), preferred_element_type=jnp.float32)
        log_norm = row_max[:, 0] + jnp.log(row_total[:, 0])
        return (out_head.astype(jnp.bfloat16), log_norm)

    head_outs, log_norms = lax.map(forward_head, jnp.arange(local_heads, dtype=jnp.int32))
    heads_out = merge_heads(head_outs)
    partial_out = jnp.dot(heads_out, wo_rows, preferred_element_type=jnp.float32)
    attended = lax.psum_scatter(partial_out, "head", scatter_dimension=1, tiled=True).astype(
        jnp.bfloat16
    )
    grad_out = times_transposed(cotangent[0], wo_rows).astype(jnp.bfloat16)

    def backward_head(inputs):
        head, log_norm = inputs
        query_head, key_head, scores = scores_of(head)
        probs = jnp.where(visible, jnp.exp(scores - log_norm[:, None]), 0.0)
        weights = probs.astype(jnp.bfloat16)
        grad_head = head_cols(grad_out, head)
        out_head = head_cols(heads_out, head)
        row_delta = jnp.sum(grad_head.astype(jnp.float32) * out_head.astype(jnp.float32), axis=1)
        dprobs = times_transposed(grad_head, head_cols(value_rows, head))
        dscores = (probs * (dprobs - row_delta[:, None])).astype(jnp.bfloat16)
        query_grad = (
            jnp.dot(dscores, key_head, preferred_element_type=jnp.float32) * score_scale
        ).astype(jnp.bfloat16)
        key_grads = (
            lax.dot_general(
                dscores, query_head, (((0,), (0,)), ((), ())), preferred_element_type=jnp.float32
            )
            * score_scale
        )
        value_grads = lax.dot_general(
            weights, grad_head, (((0,), (0,)), ((), ())), preferred_element_type=jnp.float32
        )
        return (
            query_grad,
            key_grads[prior_rows:].astype(jnp.bfloat16),
            value_grads[prior_rows:].astype(jnp.bfloat16),
            key_grads[:prior_rows],
            value_grads[:prior_rows],
        )

    query_parts, key_parts, value_parts, mkey_parts, mvalue_parts = lax.map(
        backward_head, (jnp.arange(local_heads, dtype=jnp.int32), log_norms)
    )
    grad_terms = jnp.concatenate([merge_heads(mkey_parts), merge_heads(mvalue_parts)], axis=1)
    memory_sums = lax.psum_scatter(grad_terms, "tm", scatter_dimension=0, tiled=True)
    mem_key_grad = memory_sums[:, :local_width].astype(jnp.bfloat16)
    mem_value_grad = memory_sums[:, local_width:].astype(jnp.bfloat16)
    memory_grad = times_transposed(mem_key_grad, wk_local) + times_transposed(
        mem_value_grad, wv_local
    )
    mem_term = memory_grad / counts[:, None]
    partial_grad = times_transposed(merge_heads(query_parts), wq_local)
    partial_grad = partial_grad + times_transposed(merge_heads(key_parts), wk_local)
    partial_grad = partial_grad + times_transposed(merge_heads(value_parts), wv_local)
    partial_grad = partial_grad + jnp.dot(
        onehot.astype(jnp.float32),
        mem_term,
        precision=lax.Precision.HIGHEST,
        preferred_element_type=jnp.float32,
    )
    video_grad = lax.psum_scatter(partial_grad, "head", scatter_dimension=1, tiled=True).astype(
        jnp.bfloat16
    )
    return (attended[None], video_grad[None])


def solution(mesh):
    placed = (P("tm", None, None), P("tm", None), P(), P(), P(), P(), P("tm", None, None))
    return jax.shard_map(
        shards,
        mesh=mesh,
        in_specs=placed,
        out_specs=(P("tm", None, "head"), P("tm", None, "head")),
        check_vma=False,
    )
```

profile of v0, /device:TPU:1, one launch (start us, length us, event | category | flops | bytes accessed | tf_op | source)
XLA Modules:
  0.0 1179.9 jit_solution(10043554458171405214)
XLA Ops:
  9.3 2.1 convolution_convert_fusion.5
  17.0 112.4 %all-gather.5.cloned.1.call-done = bf16[4096,512]{1,0:T(8,128)(2,1)} async-done(((bf16[32,512]{1,0:T(8,128)(2,1)}), bf16[4096,512]{1,0:T(8,128)(2,1)}) %all-gather.5.cloned.1.call-update) | async-done | bytes 4194320 | tf_op jit(solution)/shard_map/all_gather | solution.py:59
  129.3 4.4 pad_maximum_fusion.2
  133.8 113.7 %all-gather.3.cloned.1.call-done = bf16[4096,512]{1,0:T(8,128)(2,1)} async-done(((bf16[32,512]{1,0:T(8,128)(2,1)}), bf16[4096,512]{1,0:T(8,128)(2,1)}) %all-gather.3.cloned.1.call-update) | async-done | bytes 4194320 | tf_op jit(solution)/shard_map/all_gather | solution.py:58
  247.5 4.5 pad_maximum_fusion.1
  252.0 49.8 %while.32 = (s32[]{:T(128)}, bf16[8,128,64]{1,2,0:T(8,128)(2,1)S(1)}, f32[8,128]{1,0:T(8,128)S(1)}, s32[8]{0:T(128)S(1)}, bf16[128,512]{1,0:T(8,128)(2,1)S(1)}, ...) while((s32[]{:T(128)}, ...), condition=%wide.region_4.5_spmd.clone, body=%wide.region_1.4_spmd.clone.sunk | while | flops 143839488 | bytes 8724935 | solution.py:86
  255.8 2.4 fusion.117
  259.6 1.9 select_reduce_fusion.2
  262.0 2.4 fusion.117
  265.8 1.9 select_reduce_fusion.2
  268.2 2.4 fusion.117
  274.5 2.4 fusion.117
  278.2 1.9 select_reduce_fusion.2
  280.7 2.4 fusion.117
  286.9 2.4 fusion.117
  293.1 2.4 fusion.117
  299.4 2.4 fusion.117
  301.9 82.8 %while.33 = (s32[]{:T(128)}, bf16[8,128,64]{1,2,0:T(8,128)(2,1)S(1)}, bf16[8,128,64]{1,2,0:T(8,128)(2,1)S(1)}, bf16[8,128,64]{1,2,0:T(8,128)(2,1)S(1)}, f32[8,40...) while((s32[]{:T(128)}, ...), condition=%wide.region_8.9_spmd.clone, body=%wide.region_6.8_spmd.clone.sunk | while | flops 350146816 | bytes 19690384 | solution.py:124
  303.7 2.0 fusion.129
  305.6 2.0 fusion.130
  307.9 2.3 fusion.131
  314.0 2.0 fusion.129
  316.0 2.0 fusion.130
  318.3 2.3 fusion.131
  324.4 2.0 fusion.129
  326.4 2.0 fusion.130
  328.7 2.3 fusion.131
  334.7 2.0 fusion.129
  336.7 2.0 fusion.130
  339.0 2.3 fusion.131
  345.1 2.0 fusion.129
  347.0 2.0 fusion.130
  349.3 2.3 fusion.131
  355.4 2.0 fusion.129
  357.3 2.0 fusion.130
  359.6 2.3 fusion.131
  365.7 2.0 fusion.129
  367.7 2.0 fusion.130
  370.0 2.3 fusion.131
  376.1 2.0 fusion.129
  378.1 2.0 fusion.130
  380.4 2.3 fusion.131
  384.7 11.8 %pad_maximum_fusion = f32[4096,1024]{0,1:T(8,128)} fusion(f32[4096,512]{0,1:T(8,128)} %bitcast.109, f32[4096,512]{0,1:T(8,128)} %bitcast.110), kind=kLoop, calls=%fused_computation.58 | loop fusion | flops 4194304 | bytes 33554432 | tf_op jit(solution)/shard_map/concatenate | solution.py:127
  396.5 17.5 %copy.25 = f32[4096,1024]{1,0:T(8,128)} copy(f32[4096,1024]{0,1:T(8,128)} %pad_maximum_fusion) | data formatting | bytes 33554432
  414.1 2.4 fusion.48
  418.7 636.1 %reduce-scatter.10.cloned.1.call-done = f32[32,1024]{1,0:T(8,128)} async-done(((f32[4096,1024]{1,0:T(8,128)}), f32[32,1024]{1,0:T(8,128)}) %reduce-scatter.10.cloned.1.call-update) | async-done | bytes 131088
  1060.0 94.7 %reduce-scatter.6.cloned.1.call-done = f32[128,512]{1,0:T(8,128)} async-done(((f32[128,1024]{1,0:T(8,128)}), f32[128,512]{1,0:T(8,128)}) %reduce-scatter.6.cloned.1.call-update) | async-done | bytes 262160 | tf_op jit(solution)/shard_map/reduce_scatter | solution.py:89
  1156.3 15.5 %reduce-scatter.8.cloned.1.call-done = f32[128,512]{1,0:T(8,128)} async-done(((f32[128,1024]{1,0:T(8,128)}), f32[128,512]{1,0:T(8,128)}) %reduce-scatter.8.cloned.1.call-update) | async-done | bytes 262160 | tf_op jit(solution)/shard_map/reduce_scatter | solution.py:144
  (189 shorter events, 64.4 us)
Async XLA Ops:
  7.2 4.4 copy-start
  7.2 5.4 copy-start.2
  7.2 122.1 %all-gather.5.cloned.1.call-start = ((), (), s32[]{:S(2)}) async-start(), calls=%async_computation.4 | async-start | bytes 4227072 | tf_op jit(solution)/shard_map/all_gather | solution.py:59
  11.5 236.1 %all-gather.3.cloned.1.call-start = ((), (), s32[]{:S(2)}) async-start(), calls=%async_computation.3 | async-start | bytes 4227072 | tf_op jit(solution)/shard_map/all_gather | solution.py:58
  12.5 1042.4 %reduce-scatter.10.cloned.1.call-start = ((), (), s32[]{:S(2)}) async-start(), calls=%async_computation.7 | async-start | bytes 16908288
  12.6 3.9 copy-start.4
  14.4 2.0 copy-start.3
  414.0 740.6 %reduce-scatter.6.cloned.1.call-start = ((), (), s32[]{:S(2)}) async-start(), calls=%async_computation.5 | async-start | bytes 786432 | tf_op jit(solution)/shard_map/reduce_scatter | solution.py:89
  418.2 753.6 %reduce-scatter.8.cloned.1.call-start = ((), (), s32[]{:S(2)}) async-start(), calls=%async_computation.6 | async-start | bytes 786432 | tf_op jit(solution)/shard_map/reduce_scatter | solution.py:144
  418.2 640.0 %copy-start.5 = (s32[1,128]{1,0:T(1,128)S(1)}, s32[1,128]{1,0:T(1,128)}, u32[]{:S(2)}) copy-start(s32[1,128]{1,0:T(1,128)} %param.12) | copy-start | bytes 1540
  1055.9 2.7 copy-start.1
Sparse Core Ops, SparseCore 0:
  12.2 117.0 all-gather.4
  133.5 113.9 all-gather.2
  414.1 640.6 reduce-scatter.9
  1057.2 97.3 reduce-scatter.5
  1157.1 14.5 reduce-scatter.7
where the time goes:
time: 1180 us
  waiting for transfers between devices  972 us (82%)
  matrix products  107 us (9%)
  local copies, waits for them, and re-layouts  43 us (4%)
  other arithmetic  31.5 us (3%)
  between operations  14 us (1%)
    unnamed x6, waiting for transfers between devices  636 us
    all_gather x1, waiting for transfers between devices, shards(): lax.all_gather(mem_keys, 'tm', axis=0, tiled=True)  114 us
    all_gather x1, waiting for transfers between devices, shards(): lax.all_gather(mem_values, 'tm', axis=0, tiled=True)  112 us
    reduce_scatter x1, waiting for transfers between devices, shards(): lax.psum_scatter(partial_out, 'head', scatter_dimension=1, tiled=True)  94.7 us
    dot_general x30, matrix products, times_transposed(): lax.dot_general(matrix, weight, (((1,), (1,)), ((), ())), preferred_eleme...  52.8 us
  transfers between devices with their start and end apart: 5, of which 5 were waited for; matrix products, arithmetic and copies ran while one was open for 2% of the time, Pallas kernels for 0%

commit v1 on v0

v1 whole, which is shorter than its diff:
```python
import functools

import jax
import jax.numpy as jnp
from jax import lax
from jax.experimental import pallas as pl
from jax.experimental.pallas import tpu as pltpu
from jax.sharding import PartitionSpec as P

HEAD_DIM = 64
MEM = 32
TOK = 128
D = 1024
HALF = 512
LOCAL_HEADS = 8
SPLITS = 16
CHIPS = 128
QROWS = TOK // SPLITS
ROWS = MEM + 2 * QROWS
LANES = 2 * HEAD_DIM
KEYS = CHIPS * MEM
BLOCK_SEGS = 16
QBLOCK = BLOCK_SEGS * QROWS
KBLOCK = BLOCK_SEGS * MEM
NBLOCKS = CHIPS // BLOCK_SEGS
SCALE = 0.125
MASKED = -3e38
VMEM_BYTES = 40 * 1024 * 1024
f32 = jnp.float32
bf16 = jnp.bfloat16


def dot(a, b):
    return jnp.dot(a, b, preferred_element_type=f32)


def dot_nt(a, b):
    return lax.dot_general(a, b, (((1,), (1,)), ((), ())), preferred_element_type=f32)


def dot_tn(a, b):
    return lax.dot_general(a, b, (((0,), (0,)), ((), ())), preferred_element_type=f32)


def three_parts(x):
    high = x.astype(bf16).astype(f32)
    rest = x - high
    middle = rest.astype(bf16).astype(f32)
    low = (rest - middle).astype(bf16).astype(f32)
    return high, middle, low


def low_lanes(shape):
    return lax.broadcasted_iota(jnp.int32, shape, 1) < HEAD_DIM


def split_pair(pair):
    low = low_lanes(pair.shape)
    zero = jnp.zeros_like(pair)
    return jnp.concatenate([jnp.where(low, pair, zero), jnp.where(low, zero, pair)], axis=0)


def head_cols(matrix, head):
    return matrix[:, head * HEAD_DIM : (head + 1) * HEAD_DIM]


def onehot_rows(assign_row):
    rows = lax.broadcasted_iota(jnp.int32, (MEM, TOK), 0)
    return (rows == assign_row).astype(f32)


def pre_kernel(tok_ref, asg_ref, cot_ref, wq_hbm, wk_hbm, wv_hbm, wo_hbm, msg_ref, qd_ref, kv_ref, wq, wk, wv, wo, sems):
    offset = pl.multiple_of(lax.axis_index("head") * HALF, HALF)
    copies = [
        pltpu.make_async_copy(wk_hbm.at[:, pl.ds(offset, HALF)], wk, sems.at[0]),
        pltpu.make_async_copy(wv_hbm.at[:, pl.ds(offset, HALF)], wv, sems.at[1]),
        pltpu.make_async_copy(wq_hbm.at[:, pl.ds(offset, HALF)], wq, sems.at[2]),
        pltpu.make_async_copy(wo_hbm.at[pl.ds(offset, HALF), :], wo, sems.at[3]),
    ]
    for copy in copies:
        copy.start()
    tokens = tok_ref[...]
    onehot = onehot_rows(asg_ref[...])
    counts = jnp.sum(onehot, axis=1, keepdims=True)
    memory = (dot(onehot.astype(bf16), tokens) / counts).astype(bf16)
    rows = jnp.concatenate([memory, tokens], axis=0)
    copies[0].wait()
    keys = dot(rows, wk[...]).astype(bf16)
    copies[1].wait()
    values = dot(rows, wv[...]).astype(bf16)
    copies[2].wait()
    queries = (dot(tokens, wq[...]).astype(bf16).astype(f32) * SCALE).astype(bf16)
    copies[3].wait()
    grad_out = dot_nt(cot_ref[...], wo[...]).astype(bf16)
    lane = lax.broadcasted_iota(jnp.int32, (TOK, LANES), 1)
    for head in range(LOCAL_HEADS):
        pair = jnp.concatenate([head_cols(keys, head), head_cols(values, head)], axis=1)
        query_pair = jnp.concatenate([head_cols(queries, head), head_cols(grad_out, head)], axis=1)
        own = pair[MEM:]
        kv_ref[head] = own
        qd_ref[head] = query_pair
        masked = jnp.where(low_lanes(query_pair.shape), query_pair, jnp.zeros_like(query_pair))
        scores = dot_nt(masked, own)
        row_max = jnp.max(scores, axis=1, keepdims=True)
        raised = jnp.exp(scores - row_max)
        row_sum = jnp.sum(raised, axis=1, keepdims=True)
        out = dot((raised / row_sum).astype(bf16), own)
        side = out
        for at, part in enumerate(three_parts(row_max) + three_parts(row_sum)):
            side = jnp.where(lane == at, part, side)
        both = jnp.concatenate(
            [query_pair.astype(f32).reshape(SPLITS, QROWS, LANES), side.reshape(SPLITS, QROWS, LANES)], axis=1
        ).astype(bf16)
        msg_ref[:, head, :MEM, :] = jnp.broadcast_to(pair[:MEM][None], (SPLITS, MEM, LANES))
        msg_ref[:, head, MEM:, :] = both


def attend_kernel(msg_ref, out_ref, kvt, scores, dprobs, pairs, accum):
    def block(j):
        return pl.ds(pl.multiple_of(j * KBLOCK, KBLOCK), KBLOCK)

    def kv_block(j):
        return msg_ref[pl.ds(j * BLOCK_SEGS, BLOCK_SEGS), :MEM, :].reshape(KBLOCK, LANES)

    eye = (
        lax.broadcasted_iota(jnp.int32, (LANES, LANES), 0) == lax.broadcasted_iota(jnp.int32, (LANES, LANES), 1)
    ).astype(bf16)

    for j in range(NBLOCKS):
        kvt[:, j * KBLOCK : (j + 1) * KBLOCK] = dot_nt(eye, kv_block(j)).astype(bf16)
        accum[j * KBLOCK : (j + 1) * KBLOCK, :] = jnp.zeros((KBLOCK, LANES), f32)

    visible = lax.broadcasted_iota(jnp.int32, (KBLOCK, QBLOCK), 0) // MEM < (
        lax.broadcasted_iota(jnp.int32, (KBLOCK, QBLOCK), 1) // QROWS
    )

    def fold(op, x):
        return op(x.reshape(KBLOCK // 8, 8, QBLOCK), axis=0)

    def query_block(i, carry):
        rows = msg_ref[pl.ds(i * BLOCK_SEGS, BLOCK_SEGS), MEM:, :].astype(f32)
        query_pair = rows[:, :QROWS].reshape(QBLOCK, LANES)
        side = rows[:, QROWS:].reshape(QBLOCK, LANES).T
        own_out = side[HEAD_DIM:]
        own_max = side[0:1] + side[1:2] + side[2:3]
        own_sum = side[3:4] + side[4:5] + side[5:6]
        grad_t = query_pair.T[HEAD_DIM:]
        pair_rows = split_pair(query_pair).astype(bf16)

        def first(j, top, mask):
            both = dot_nt(kv_block(j), pair_rows)
            score = both[:, :QBLOCK]
            if mask:
                score = jnp.where(visible, score, MASKED)
            scores[block(j), :] = score
            dprobs[block(j), :] = both[:, QBLOCK:]
            return jnp.maximum(top, fold(jnp.max, score))

        top = jnp.broadcast_to(own_max, (8, QBLOCK))
        top = lax.fori_loop(0, i, lambda j, t: first(j, t, False), top)
        top = first(i, top, True)
        row_max = jnp.max(top, axis=0, keepdims=True)

        def second(j, total):
            raised = jnp.exp(scores[block(j), :] - row_max)
            scores[block(j), :] = raised
            return total + fold(jnp.sum, raised)

        total = lax.fori_loop(0, i + 1, second, jnp.zeros((8, QBLOCK), f32))
        own_share = own_sum * jnp.exp(own_max - row_max)
        row_sum = own_share + jnp.sum(total, axis=0, keepdims=True)
        inverse = 1.0 / row_sum

        def third(j, out):
            probs = scores[block(j), :] * inverse
            scores[block(j), :] = probs
            weights = probs.astype(bf16)
            pairs[block(j), QBLOCK:] = weights
            return out + dot(kvt[:, block(j)], weights)

        out = lax.fori_loop(0, i + 1, third, jnp.zeros((LANES, QBLOCK), f32))
        heads_out = (own_out * (own_share * inverse) + out[HEAD_DIM:]).astype(bf16).astype(f32)
        delta = jnp.sum(grad_t * heads_out, axis=0, keepdims=True)

        def fourth(j, grad):
            dscores = (scores[block(j), :] * (dprobs[block(j), :] - delta)).astype(bf16)
            pairs[block(j), :QBLOCK] = dscores
            accum[block(j), :] += dot(pairs[block(j), :], pair_rows)
            return grad + dot(kvt[:, block(j)], dscores)

        query_grad = lax.fori_loop(0, i + 1, fourth, jnp.zeros((LANES, QBLOCK), f32))[:HEAD_DIM]
        grad_high = query_grad.astype(bf16).astype(f32)
        main = jnp.concatenate([grad_high, heads_out], axis=0).T
        row_at = lax.broadcasted_iota(jnp.int32, (HEAD_DIM, QBLOCK), 0)
        stats = jnp.zeros((HEAD_DIM, QBLOCK), f32)
        for at, part in enumerate(three_parts(row_max) + three_parts(row_sum)):
            stats = jnp.where(row_at == at, part, stats)
        extra = jnp.concatenate([query_grad - grad_high, stats], axis=0).T
        out_ref[pl.ds(i * BLOCK_SEGS, BLOCK_SEGS), MEM:, :] = jnp.concatenate(
            [main.reshape(BLOCK_SEGS, QROWS, LANES), extra.reshape(BLOCK_SEGS, QROWS, LANES)], axis=1
        ).astype(bf16)
        return carry

    lax.fori_loop(0, NBLOCKS, query_block, 0)
    for j in range(NBLOCKS):
        out_ref[j * BLOCK_SEGS : (j + 1) * BLOCK_SEGS, :MEM, :] = (
            accum[j * KBLOCK : (j + 1) * KBLOCK, :].astype(bf16).reshape(BLOCK_SEGS, MEM, LANES)
        )


def post_kernel(msg_ref, asg_ref, qd_ref, kv_ref, wq_hbm, wk_hbm, wv_hbm, wo_hbm, mine_ref, other_ref, wq, wk, wv, wo, sems):
    half = lax.axis_index("head")
    offset = pl.multiple_of(half * HALF, HALF)
    away = pl.multiple_of((1 - half) * HALF, HALF)
    copies = [
        pltpu.make_async_copy(wo_hbm.at[pl.ds(offset, HALF), :], wo, sems.at[0]),
        pltpu.make_async_copy(wq_hbm.at[:, pl.ds(offset, HALF)], wq, sems.at[1]),
        pltpu.make_async_copy(wk_hbm.at[:, pl.ds(offset, HALF)], wk, sems.at[2]),
        pltpu.make_async_copy(wv_hbm.at[:, pl.ds(offset, HALF)], wv, sems.at[3]),
    ]
    for copy in copies:
        copy.start()
    onehot = onehot_rows(asg_ref[...])
    counts = jnp.sum(onehot, axis=1, keepdims=True)
    heads_out, query_grads, key_grads, value_grads = [], [], [], []
    for head in range(LOCAL_HEADS):
        mem_pair = jnp.sum(msg_ref[:, head, :MEM, :].astype(f32), axis=0)
        rows = msg_ref[:, head, MEM:, :].astype(f32)
        main = rows[:, :QROWS].reshape(TOK, LANES)
        extra = rows[:, QROWS:].reshape(TOK, LANES)
        at = HEAD_DIM
        row_max = extra[:, at : at + 1] + extra[:, at + 1 : at + 2] + extra[:, at + 2 : at + 3]
        row_sum = extra[:, at + 3 : at + 4] + extra[:, at + 4 : at + 5] + extra[:, at + 5 : at + 6]
        query_pair = qd_ref[head]
        own = kv_ref[head]
        pair_rows = split_pair(query_pair)
        both = dot_nt(pair_rows, own)
        probs = jnp.exp(both[:TOK] - row_max) / row_sum
        weights = probs.astype(bf16)
        products = query_pair.astype(f32) * main
        delta = jnp.sum(jnp.where(low_lanes(products.shape), 0.0, products), axis=1, keepdims=True)
        dscores = (probs * (both[TOK:] - delta)).astype(bf16)
        query_grad = (main + extra + dot(dscores, own)) * SCALE
        own_pair = dot_tn(jnp.concatenate([dscores, weights], axis=0), pair_rows)
        grads = jnp.concatenate([own_pair, mem_pair], axis=0)
        heads_out.append(main[:, HEAD_DIM:])
        query_grads.append(query_grad[:, :HEAD_DIM])
        key_grads.append(grads[:, :HEAD_DIM])
        value_grads.append(grads[:, HEAD_DIM:])

    def merge(parts):
        return jnp.concatenate(parts, axis=1).astype(bf16)

    heads_out = merge(heads_out)
    query_grads = merge(query_grads)
    key_grads = merge(key_grads)
    value_grads = merge(value_grads)
    onehot = onehot.astype(bf16)
    for copy in copies:
        copy.wait()
    for ref, start in ((mine_ref, offset), (other_ref, away)):
        rows = pl.ds(start, HALF)
        ref[0] = dot(heads_out, wo[:, rows])
        total = dot_nt(key_grads, wk[rows, :]) + dot_nt(value_grads, wv[rows, :])
        high, middle, low = three_parts(total[TOK:] / counts)
        spread = dot_tn(onehot, high.astype(bf16)) + dot_tn(onehot, middle.astype(bf16)) + dot_tn(onehot, low.astype(bf16))
        ref[1] = total[:TOK] + dot_nt(query_grads, wq[rows, :]) + spread


def params():
    return pltpu.CompilerParams(vmem_limit_bytes=VMEM_BYTES)


def vmem():
    return pl.BlockSpec(memory_space=pltpu.VMEM)


def hbm():
    return pl.BlockSpec(memory_space=pl.ANY)


def weight_scratch():
    return [pltpu.VMEM((D, HALF), bf16)] * 3 + [pltpu.VMEM((HALF, D), bf16), pltpu.SemaphoreType.DMA((4,))]


def shards(video, assign, w_query, w_key, w_value, w_out, cotangent):
    pair_shape = jax.ShapeDtypeStruct((LOCAL_HEADS, TOK, LANES), bf16)
    message_shape = jax.ShapeDtypeStruct((SPLITS, LOCAL_HEADS, ROWS, LANES), bf16)
    message, query_pairs, own_pairs = pl.pallas_call(
        pre_kernel,
        out_shape=(message_shape, pair_shape, pair_shape),
        in_specs=[vmem()] * 3 + [hbm()] * 4,
        out_specs=(vmem(), vmem(), vmem()),
        scratch_shapes=weight_scratch(),
        compiler_params=params(),
        name="project",
    )(video[0], assign, cotangent[0], w_query, w_key, w_value, w_out)

    received = lax.all_to_all(message.reshape(CHIPS, ROWS, LANES), "tm", 0, 0, tiled=True)
    answer = pl.pallas_call(
        attend_kernel,
        out_shape=jax.ShapeDtypeStruct((CHIPS, ROWS, LANES), bf16),
        in_specs=[vmem()],
        out_specs=vmem(),
        scratch_shapes=[
            pltpu.VMEM((LANES, KEYS), bf16),
            pltpu.VMEM((KEYS, QBLOCK), f32),
            pltpu.VMEM((KEYS, QBLOCK), f32),
            pltpu.VMEM((KEYS, 2 * QBLOCK), bf16),
            pltpu.VMEM((KEYS, LANES), f32),
        ],
        compiler_params=params(),
        name="attend",
    )(received)
    returned = lax.all_to_all(answer, "tm", 0, 0, tiled=True).reshape(message_shape.shape)

    half_shape = jax.ShapeDtypeStruct((2, TOK, HALF), f32)
    mine, other = pl.pallas_call(
        post_kernel,
        out_shape=(half_shape, half_shape),
        in_specs=[vmem()] * 4 + [hbm()] * 4,
        out_specs=(vmem(), vmem()),
        scratch_shapes=weight_scratch(),
        compiler_params=params(),
        name="gradients",
    )(returned, assign, query_pairs, own_pairs, w_query, w_key, w_value, w_out)
    total = mine + lax.ppermute(other, "head", [(0, 1), (1, 0)])
    total = total.astype(bf16)
    return (total[0][None], total[1][None])


def solution(mesh):
    placed = (P("tm", None, None), P("tm", None), P(), P(), P(), P(), P("tm", None, None))
    return jax.shard_map(
        shards,
        mesh=mesh,
        in_specs=placed,
        out_specs=(P("tm", None, "head"), P("tm", None, "head")),
        check_vma=False,
    )
```

time: 1180 us -> 160 us (0.14)
  waiting for transfers between devices: 972 us -> 1.54 us
  matrix products: 107 us -> 0 us
  blocking collectives: 0 us -> 104 us
  Pallas kernels: 0 us -> 39.8 us
  local copies, waits for them, and re-layouts: 43 us -> 9.65 us
  other arithmetic: 31.5 us -> 0.09 us
  between operations: 14 us -> 0.72 us
    unnamed x6 -> x0, waiting for transfers between devices: 636 us -> none
    all_gather x2 -> x0, waiting for transfers between devices: 226 us -> none  [the longest x1 114 us: shards(): lax.all_gather(mem_keys, 'tm', axis=0, tiled=True)]
    reduce_scatter x2 -> x0, waiting for transfers between devices: 110 us -> none  [the longest x1 94.7 us: shards(): lax.psum_scatter(partial_out, 'head', scatter_dimension=1, tiled=True)]
    dot_general x70 -> x0, matrix products: 107 us -> none  [the longest x30 52.8 us: times_transposed(): lax.dot_general(matrix, weight, (((1,), (1,)), ((), ())), preferred_eleme...]
    all_to_all x0 -> x2, blocking collectives: none -> 104 us  [the longest x1 58 us: shards(): lax.all_to_all(message.reshape(CHIPS, ROWS, LANES), 'tm', 0, 0, tiled=True)]
    pallas_call x0 -> x3, Pallas kernels: none -> 39.8 us  [the longest x1 30.5 us: shards(): pl.pallas_call(attend_kernel, out_shape=jax.ShapeDtypeStruct((CHIPS, ROWS...]
    concatenate x3 -> x0, other arithmetic: 20.8 us -> none  [the longest x1 11.8 us: shards(): jnp.concatenate([merge_heads(mkey_parts), merge_heads(mvalue_parts)], axi...]
    dynamic_update_slice x24 -> x0, local copies, waits for them, and re-layouts: 12.8 us -> none  [the longest x8 12.3 us: shards(): lax.map(backward_head, (jnp.arange(local_heads, dtype=jnp.int32), log_nor...]
  transfers between devices with their start and end apart: 5 -> 1, of which waited for: 5 -> 1; matrix products, arithmetic and copies ran while one was open for 2% -> 0% of each run, Pallas kernels for 0% -> 0%
where the time goes in v1:
time: 160 us
  blocking collectives  104 us (65%)
  Pallas kernels  39.8 us (25%)
  local copies, waits for them, and re-layouts  9.65 us (6%)
  starting transfers between devices  4.24 us (3%)
    all_to_all x1, blocking collectives, shards(): lax.all_to_all(message.reshape(CHIPS, ROWS, LANES), 'tm', 0, 0, tiled=True)  58 us
    all_to_all x1, blocking collectives, shards(): lax.all_to_all(answer, 'tm', 0, 0, tiled=True).reshape(message_shape.shape)  45.6 us
    pallas_call x1, Pallas kernels, shards(): pl.pallas_call(attend_kernel, out_shape=jax.ShapeDtypeStruct((CHIPS, ROWS...  30.5 us
    unnamed x24, local copies, waits for them, and re-layouts  8.94 us
    pallas_call x1, Pallas kernels, shards(): pl.pallas_call(pre_kernel, out_shape=(message_shape, pair_shape, pair_sha...  4.75 us
    pallas_call x1, Pallas kernels, shards(): pl.pallas_call(post_kernel, out_shape=(half_shape, half_shape), in_specs=...  4.58 us
    ppermute x1, starting transfers between devices, shards(): total = mine + lax.ppermute(other, 'head', [(0, 1), (1, 0)])  4.24 us
  transfers between devices with their start and end apart: 1, of which 1 were waited for; matrix products, arithmetic and copies ran while one was open for 0% of the time, Pallas kernels for 0%

profile of v1, /device:TPU:1, one launch (start us, length us, event | category | flops | bytes accessed | tf_op | source)
XLA Modules:
  0.0 159.7 jit_solution(12310229568345685387)
XLA Ops:
  0.6 0.0 copy-start
  0.6 1.6 copy-done
  2.2 0.0 copy-start.2
  2.2 1.6 copy-done.2
  3.8 0.0 copy-start.4
  3.8 1.6 copy-done.4
  5.4 0.0 copy-start.6
  5.4 1.6 copy-done.6
  7.0 0.0 copy-start.8
  7.0 0.9 copy-done.8
  7.9 0.0 copy-start.9
  8.0 0.9 copy-done.9
  8.9 0.0 copy-start.10
  8.9 0.7 copy-done.10
  9.6 4.7 %project.1 = (bf16[16,8,48,128]{3,2,1,0:T(8,128)(2,1)S(1)}, bf16[8,128,128]{2,1,0:T(8,128)(2,1)S(1)}, bf16[8,128,128]{2,1,0:T(8,128)(2,1)S(1)}) custom-call(bf16[128,1024]{1,0:T(8,128)(2,1)S(1)} %bitcast.6, s32[1,128]{1,0:T(1,128)S(1)} %copy-done.10, bf16[128,1024]{1,0:T(8,128)(2,1)S(1)} %bitcast.7, bf16[1024,1024]{1,0:T(8,128)(2,1)S(1)} %copy-done, ...), custom_call_target="tpu_custom_call" | custom-call | tf_op jit(solution)/shard_map/project/pallas_call | solution.py:289
  14.3 0.0 copy-start.7
  14.3 58.0 %all_to_all.10.msg_ref = bf16[128,48,128]{2,1,0:T(8,128)(2,1)S(1)} all-to-all(bf16[128,48,128]{2,1,0:T(8,128)(2,1)S(1)} %bitcast.5), channel_id=1, replica_groups=mesh['tm'=128,'head'=2] {'tm'}, dimensions={0} | all-to-all | bytes 3145728 | tf_op jit(solution)/shard_map/all_to_all | solution.py:299
  72.3 0.0 copy-start.3
  72.3 0.0 copy-start.5
  72.3 30.5 %attend.1 = bf16[128,48,128]{2,1,0:T(8,128)(2,1)S(1)} custom-call(bf16[128,48,128]{2,1,0:T(8,128)(2,1)S(1)} %all_to_all.10.msg_ref), custom_call_target="tpu_custom_call" | custom-call | tf_op jit(solution)/shard_map/attend/pallas_call | solution.py:300
  102.8 0.0 copy-start.1
  102.8 0.0 copy-start.11
  102.8 45.6 %all_to_all.11 = bf16[128,48,128]{2,1,0:T(8,128)(2,1)S(1)} all-to-all(bf16[128,48,128]{2,1,0:T(8,128)(2,1)S(1)} %attend.1), channel_id=1, replica_groups=mesh['tm'=128,'head'=2] {'tm'}, dimensions={0} | all-to-all | bytes 3145728 | tf_op jit(solution)/shard_map/all_to_all | solution.py:315
  148.5 0.0 copy-done.7
  148.5 0.0 copy-done.3
  148.5 0.0 copy-done.5
  148.5 0.0 copy-done.1
  148.5 0.0 copy-done.11
  148.5 4.6 %gradients.1 = (f32[2,128,512]{2,1,0:T(8,128)S(1)}, f32[2,128,512]{2,1,0:T(8,128)S(1)}) custom-call(bf16[16,8,48,128]{3,2,1,0:T(8,128)(2,1)S(1)} %bitcast.4, s32[1,128]{1,0:T(1,128)S(1)} %copy-done.11, bf16[8,128,128]{2,1,0:T(8,128)(2,1)S(1)} %get-tuple-element.8.qd_ref, bf16[8,128,128]{2,1,0:T(8,128)(2,1)S(1)} %get-tuple-element.9.kv_ref, ...), custom_call_target="tpu_custom_call" | custom-call | tf_op jit(solution)/shard_map/gradients/pallas_call | solution.py:318
  153.1 4.2 %collective-permute-start = (f32[2,128,512]{2,1,0:T(8,128)S(1)}, f32[2,128,512]{2,1,0:T(8,128)S(1)}, u32[]{:S(2)}, u32[]{:S(2)}) collective-permute-start(f32[2,128,512]{2,1,0:T(8,128)S(1)} %get-tuple-element.11), channel_id=1, source_target_pairs={{0,1},{1,0},{2,3},{3,2},{4,5},{5,4},{6,7},{7,6},{8,9},{9,8},{10,11... | collective-permute-start | bytes 1572872 | tf_op jit(solution)/shard_map/ppermute | solution.py:327
  157.3 1.5 collective-permute-done
  158.9 0.1 add_convert_fusion
  159.0 0.7 fusion
Async XLA Ops:
  0.6 1.6 copy-start
  2.2 1.6 copy-start.2
  3.8 1.6 copy-start.4
  5.4 1.6 copy-start.6
  7.0 0.9 copy-start.8
  7.9 0.9 copy-start.9
  8.9 0.7 copy-start.10
  14.3 134.2 %copy-start.7 = (bf16[1024,1024]{1,0:T(8,128)(2,1)S(1)}, bf16[1024,1024]{1,0:T(8,128)(2,1)}, u32[]{:S(2)}) copy-start(bf16[1024,1024]{1,0:T(8,128)(2,1)} %wo_hbm.3) | copy-start | bytes 6291460
  72.3 76.2 %copy-start.3 = (bf16[1024,1024]{1,0:T(8,128)(2,1)S(1)}, bf16[1024,1024]{1,0:T(8,128)(2,1)}, u32[]{:S(2)}) copy-start(bf16[1024,1024]{1,0:T(8,128)(2,1)} %wk_hbm.3) | copy-start | bytes 6291460
  72.3 76.2 %copy-start.5 = (bf16[1024,1024]{1,0:T(8,128)(2,1)S(1)}, bf16[1024,1024]{1,0:T(8,128)(2,1)}, u32[]{:S(2)}) copy-start(bf16[1024,1024]{1,0:T(8,128)(2,1)} %wv_hbm.3) | copy-start | bytes 6291460
  102.8 45.7 %copy-start.1 = (bf16[1024,1024]{1,0:T(8,128)(2,1)S(1)}, bf16[1024,1024]{1,0:T(8,128)(2,1)}, u32[]{:S(2)}) copy-start(bf16[1024,1024]{1,0:T(8,128)(2,1)} %wq_hbm.3) | copy-start | bytes 6291460
  102.8 45.7 %copy-start.11 = (s32[1,128]{1,0:T(1,128)S(1)}, s32[1,128]{1,0:T(1,128)}, u32[]{:S(2)}) copy-start(s32[1,128]{1,0:T(1,128)} %asg_ref.3) | copy-start | bytes 1540
  153.1 5.8 %collective-permute-start = (f32[2,128,512]{2,1,0:T(8,128)S(1)}, f32[2,128,512]{2,1,0:T(8,128)S(1)}, u32[]{:S(2)}, u32[]{:S(2)}) collective-permute-start(f32[2,128,512]{2,1,0:T(8,128)S(1)} %get-tuple-element.11), channel_id=1, source_target_pairs={{0,1},{1,0},{2,3},{3,2},{4,5},{5,4},{6,7},{7,6},{8,9},{9,8},{10,11... | collective-permute-start | bytes 1572872 | tf_op jit(solution)/shard_map/ppermute | solution.py:327

commit v2 on v1

--- a/solution.py
+++ b/solution.py
@@ -1,5 +1,3 @@
-import functools
-
 import jax
 import jax.numpy as jnp
 from jax import lax
@@ -25,7 +23,9 @@
 NBLOCKS = CHIPS // BLOCK_SEGS
 SCALE = 0.125
 MASKED = -3e38
-VMEM_BYTES = 40 * 1024 * 1024
+FIRST_VMEM = 60 * 1024 * 1024
+MIDDLE_VMEM = 32 * 1024 * 1024
+LAST_VMEM = 32 * 1024 * 1024
 f32 = jnp.float32
 bf16 = jnp.bfloat16
 
@@ -69,30 +69,41 @@
     return (rows == assign_row).astype(f32)
 
 
-def pre_kernel(tok_ref, asg_ref, cot_ref, wq_hbm, wk_hbm, wv_hbm, wo_hbm, msg_ref, qd_ref, kv_ref, wq, wk, wv, wo, sems):
+def pre_kernel(
+    tok_hbm, asg_hbm, cot_hbm, wq_hbm, wk_hbm, wv_hbm, wo_hbm, msg_hbm, qd_ref, kv_ref,
+    tok_ref, asg_ref, cot_ref, wq, wk, wv, wo, msg_ref, sems, out_sems,
+):
     offset = pl.multiple_of(lax.axis_index("head") * HALF, HALF)
-    copies = [
-        pltpu.make_async_copy(wk_hbm.at[:, pl.ds(offset, HALF)], wk, sems.at[0]),
-        pltpu.make_async_copy(wv_hbm.at[:, pl.ds(offset, HALF)], wv, sems.at[1]),
-        pltpu.make_async_copy(wq_hbm.at[:, pl.ds(offset, HALF)], wq, sems.at[2]),
-        pltpu.make_async_copy(wo_hbm.at[pl.ds(offset, HALF), :], wo, sems.at[3]),
+    moves = [
+        (asg_hbm, asg_ref),
+        (tok_hbm, tok_ref),
+        (wk_hbm.at[:, pl.ds(offset, HALF)], wk),
+        (wv_hbm.at[:, pl.ds(offset, HALF)], wv),
+        (wq_hbm.at[:, pl.ds(offset, HALF)], wq),
+        (cot_hbm, cot_ref),
+        (wo_hbm.at[pl.ds(offset, HALF), :], wo),
     ]
+    copies = [pltpu.make_async_copy(source, target, sems.at[at]) for at, (source, target) in enumerate(moves)]
     for copy in copies:
         copy.start()
-    tokens = tok_ref[...]
+    copies[0].wait()
     onehot = onehot_rows(asg_ref[...])
     counts = jnp.sum(onehot, axis=1, keepdims=True)
+    copies[1].wait()
+    tokens = tok_ref[...]
     memory = (dot(onehot.astype(bf16), tokens) / counts).astype(bf16)
     rows = jnp.concatenate([memory, tokens], axis=0)
-    copies[0].wait()
+    copies[2].wait()
     keys = dot(rows, wk[...]).astype(bf16)
-    copies[1].wait()
+    copies[3].wait()
     values = dot(rows, wv[...]).astype(bf16)
-    copies[2].wait()
+    copies[4].wait()
     queries = (dot(tokens, wq[...]).astype(bf16).astype(f32) * SCALE).astype(bf16)
-    copies[3].wait()
+    copies[5].wait()
+    copies[6].wait()
     grad_out = dot_nt(cot_ref[...], wo[...]).astype(bf16)
     lane = lax.broadcasted_iota(jnp.int32, (TOK, LANES), 1)
+    sends = []
     for head in range(LOCAL_HEADS):
         pair = jnp.concatenate([head_cols(keys, head), head_cols(values, head)], axis=1)
         query_pair = jnp.concatenate([head_cols(queries, head), head_cols(grad_out, head)], axis=1)
@@ -113,23 +124,28 @@
         ).astype(bf16)
         msg_ref[:, head, :MEM, :] = jnp.broadcast_to(pair[:MEM][None], (SPLITS, MEM, LANES))
         msg_ref[:, head, MEM:, :] = both
-
-
-def attend_kernel(msg_ref, out_ref, kvt, scores, dprobs, pairs, accum):
+        sends.append(pltpu.make_async_copy(msg_ref.at[:, head], msg_hbm.at[:, head], out_sems.at[head]))
+        sends[-1].start()
+    for send in sends:
+        send.wait()
+
+
+def attend_kernel(msg_hbm, out_hbm, msg_ref, out_ref, kvt, scores, dprobs, accum, in_sems, out_sem):
+    def segs(j):
+        return slice(j * BLOCK_SEGS, (j + 1) * BLOCK_SEGS)
+
     def block(j):
-        return pl.ds(pl.multiple_of(j * KBLOCK, KBLOCK), KBLOCK)
+        return slice(j * KBLOCK, (j + 1) * KBLOCK)
 
     def kv_block(j):
-        return msg_ref[pl.ds(j * BLOCK_SEGS, BLOCK_SEGS), :MEM, :].reshape(KBLOCK, LANES)
-
+        return msg_ref[segs(j), :MEM, :].reshape(KBLOCK, LANES)
+
+    copies = [pltpu.make_async_copy(msg_hbm.at[segs(j)], msg_ref.at[segs(j)], in_sems.at[j]) for j in range(NBLOCKS)]
+    for copy in copies:
+        copy.start()
     eye = (
         lax.broadcasted_iota(jnp.int32, (LANES, LANES), 0) == lax.broadcasted_iota(jnp.int32, (LANES, LANES), 1)
     ).astype(bf16)
-
-    for j in range(NBLOCKS):
-        kvt[:, j * KBLOCK : (j + 1) * KBLOCK] = dot_nt(eye, kv_block(j)).astype(bf16)
-        accum[j * KBLOCK : (j + 1) * KBLOCK, :] = jnp.zeros((KBLOCK, LANES), f32)
-
     visible = lax.broadcasted_iota(jnp.int32, (KBLOCK, QBLOCK), 0) // MEM < (
         lax.broadcasted_iota(jnp.int32, (KBLOCK, QBLOCK), 1) // QROWS
     )
@@ -137,8 +153,11 @@
     def fold(op, x):
         return op(x.reshape(KBLOCK // 8, 8, QBLOCK), axis=0)
 
-    def query_block(i, carry):
-        rows = msg_ref[pl.ds(i * BLOCK_SEGS, BLOCK_SEGS), MEM:, :].astype(f32)
+    for i in range(NBLOCKS):
+        buf = i % 2
+        copies[i].wait()
+        kvt[:, block(i)] = dot_nt(eye, kv_block(i)).astype(bf16)
+        rows = msg_ref[segs(i), MEM:, :].astype(f32)
         query_pair = rows[:, :QROWS].reshape(QBLOCK, LANES)
         side = rows[:, QROWS:].reshape(QBLOCK, LANES).T
         own_out = side[HEAD_DIM:]
@@ -147,48 +166,42 @@
         grad_t = query_pair.T[HEAD_DIM:]
         pair_rows = split_pair(query_pair).astype(bf16)
 
-        def first(j, top, mask):
+        top = jnp.broadcast_to(own_max, (8, QBLOCK))
+        for j in range(i + 1):
             both = dot_nt(kv_block(j), pair_rows)
             score = both[:, :QBLOCK]
-            if mask:
+            if j == i:
                 score = jnp.where(visible, score, MASKED)
-            scores[block(j), :] = score
-            dprobs[block(j), :] = both[:, QBLOCK:]
-            return jnp.maximum(top, fold(jnp.max, score))
-
-        top = jnp.broadcast_to(own_max, (8, QBLOCK))
-        top = lax.fori_loop(0, i, lambda j, t: first(j, t, False), top)
-        top = first(i, top, True)
+            scores[buf, block(j), :] = score
+            dprobs[buf, block(j), :] = both[:, QBLOCK:]
+            top = jnp.maximum(top, fold(jnp.max, score))
         row_max = jnp.max(top, axis=0, keepdims=True)
 
-        def second(j, total):
-            raised = jnp.exp(scores[block(j), :] - row_max)
-            scores[block(j), :] = raised
-            return total + fold(jnp.sum, raised)
-
-        total = lax.fori_loop(0, i + 1, second, jnp.zeros((8, QBLOCK), f32))
+        total = jnp.zeros((8, QBLOCK), f32)
+        out = jnp.zeros((LANES, QBLOCK), f32)
+        for j in range(i + 1):
+            raised = jnp.exp(scores[buf, block(j), :] - row_max)
+            scores[buf, block(j), :] = raised
+            total = total + fold(jnp.sum, raised)
+            out = out + dot(kvt[:, block(j)], raised.astype(bf16))
         own_share = own_sum * jnp.exp(own_max - row_max)
         row_sum = own_share + jnp.sum(total, axis=0, keepdims=True)
         inverse = 1.0 / row_sum
-
-        def third(j, out):
-            probs = scores[block(j), :] * inverse
-            scores[block(j), :] = probs
-            weights = probs.astype(bf16)
-            pairs[block(j), QBLOCK:] = weights
-            return out + dot(kvt[:, block(j)], weights)
-
-        out = lax.fori_loop(0, i + 1, third, jnp.zeros((LANES, QBLOCK), f32))
-        heads_out = (own_out * (own_share * inverse) + out[HEAD_DIM:]).astype(bf16).astype(f32)
+        heads_out = ((own_out * own_share + out[HEAD_DIM:]) * inverse).astype(bf16).astype(f32)
         delta = jnp.sum(grad_t * heads_out, axis=0, keepdims=True)
 
-        def fourth(j, grad):
-            dscores = (scores[block(j), :] * (dprobs[block(j), :] - delta)).astype(bf16)
-            pairs[block(j), :QBLOCK] = dscores
-            accum[block(j), :] += dot(pairs[block(j), :], pair_rows)
-            return grad + dot(kvt[:, block(j)], dscores)
-
-        query_grad = lax.fori_loop(0, i + 1, fourth, jnp.zeros((LANES, QBLOCK), f32))[:HEAD_DIM]
+        grad = jnp.zeros((LANES, QBLOCK), f32)
+        for j in range(i + 1):
+            probs = scores[buf, block(j), :] * inverse
+            dscores = (probs * (dprobs[buf, block(j), :] - delta)).astype(bf16)
+            both = jnp.concatenate([dscores, probs.astype(bf16)], axis=1)
+            term = dot(both, pair_rows)
+            if j == i:
+                accum[block(j), :] = term
+            else:
+                accum[block(j), :] += term
+            grad = grad + dot(kvt[:, block(j)], dscores)
+        query_grad = grad[:HEAD_DIM]
         grad_high = query_grad.astype(bf16).astype(f32)
         main = jnp.concatenate([grad_high, heads_out], axis=0).T
         row_at = lax.broadcasted_iota(jnp.int32, (HEAD_DIM, QBLOCK), 0)
@@ -196,19 +209,21 @@
         for at, part in enumerate(three_parts(row_max) + three_parts(row_sum)):
             stats = jnp.where(row_at == at, part, stats)
         extra = jnp.concatenate([query_grad - grad_high, stats], axis=0).T
-        out_ref[pl.ds(i * BLOCK_SEGS, BLOCK_SEGS), MEM:, :] = jnp.concatenate(
+        out_ref[segs(i), MEM:, :] = jnp.concatenate(
             [main.reshape(BLOCK_SEGS, QROWS, LANES), extra.reshape(BLOCK_SEGS, QROWS, LANES)], axis=1
         ).astype(bf16)
-        return carry
-
-    lax.fori_loop(0, NBLOCKS, query_block, 0)
+
     for j in range(NBLOCKS):
-        out_ref[j * BLOCK_SEGS : (j + 1) * BLOCK_SEGS, :MEM, :] = (
-            accum[j * KBLOCK : (j + 1) * KBLOCK, :].astype(bf16).reshape(BLOCK_SEGS, MEM, LANES)
-        )
-
-
-def post_kernel(msg_ref, asg_ref, qd_ref, kv_ref, wq_hbm, wk_hbm, wv_hbm, wo_hbm, mine_ref, other_ref, wq, wk, wv, wo, sems):
+        out_ref[segs(j), :MEM, :] = accum[block(j), :].astype(bf16).reshape(BLOCK_SEGS, MEM, LANES)
+    copy = pltpu.make_async_copy(out_ref, out_hbm, out_sem)
+    copy.start()
+    copy.wait()
+
+
+def post_kernel(
+    msg_hbm, asg_ref, qd_ref, kv_ref, wq_hbm, wk_hbm, wv_hbm, wo_hbm, mine_ref, other_ref,
+    wq, wk, wv, wo, msg_ref, sems, in_sems,
+):
     half = lax.axis_index("head")
     offset = pl.multiple_of(half * HALF, HALF)
     away = pl.multiple_of((1 - half) * HALF, HALF)
@@ -218,12 +233,16 @@
         pltpu.make_async_copy(wk_hbm.at[:, pl.ds(offset, HALF)], wk, sems.at[2]),
         pltpu.make_async_copy(wv_hbm.at[:, pl.ds(offset, HALF)], wv, sems.at[3]),
     ]
-    for copy in copies:
+    parts = [
+        pltpu.make_async_copy(msg_hbm.at[:, head], msg_ref.at[:, head], in_sems.at[head]) for head in range(LOCAL_HEADS)
+    ]
+    for copy in parts + copies:
         copy.start()
     onehot = onehot_rows(asg_ref[...])
     counts = jnp.sum(onehot, axis=1, keepdims=True)
     heads_out, query_grads, key_grads, value_grads = [], [], [], []
     for head in range(LOCAL_HEADS):
+        parts[head].wait()
         mem_pair = jnp.sum(msg_ref[:, head, :MEM, :].astype(f32), axis=0)
         rows = msg_ref[:, head, MEM:, :].astype(f32)
         main = rows[:, :QROWS].reshape(TOK, LANES)
@@ -267,8 +286,8 @@
         ref[1] = total[:TOK] + dot_nt(query_grads, wq[rows, :]) + spread
 
 
-def params():
-    return pltpu.CompilerParams(vmem_limit_bytes=VMEM_BYTES)
+def params(vmem_bytes):
+    return pltpu.CompilerParams(vmem_limit_bytes=vmem_bytes)
 
 
 def vmem():
@@ -276,11 +295,15 @@
 
 
 def hbm():
+    return pl.BlockSpec(memory_space=pltpu.HBM)
+
+
+def anywhere():
     return pl.BlockSpec(memory_space=pl.ANY)
 
 
 def weight_scratch():
-    return [pltpu.VMEM((D, HALF), bf16)] * 3 + [pltpu.VMEM((HALF, D), bf16), pltpu.SemaphoreType.DMA((4,))]
+    return [pltpu.VMEM((D, HALF), bf16)] * 3 + [pltpu.VMEM((HALF, D), bf16)]
 
 
 def shards(video, assign, w_query, w_key, w_value, w_out, cotangent):
@@ -289,10 +312,18 @@
     message, query_pairs, own_pairs = pl.pallas_call(
         pre_kernel,
         out_shape=(message_shape, pair_shape, pair_shape),
-        in_specs=[vmem()] * 3 + [hbm()] * 4,
-        out_specs=(vmem(), vmem(), vmem()),
-        scratch_shapes=weight_scratch(),
-        compiler_params=params(),
+        in_specs=[anywhere()] * 7,
+        out_specs=(hbm(), vmem(), vmem()),
+        scratch_shapes=[
+            pltpu.VMEM((TOK, D), bf16),
+            pltpu.VMEM((1, TOK), jnp.int32),
+            pltpu.VMEM((TOK, D), bf16),
+            *weight_scratch(),
+            pltpu.VMEM(message_shape.shape, bf16),
+            pltpu.SemaphoreType.DMA((7,)),
+            pltpu.SemaphoreType.DMA((LOCAL_HEADS,)),
+        ],
+        compiler_params=params(FIRST_VMEM),
         name="project",
     )(video[0], assign, cotangent[0], w_query, w_key, w_value, w_out)
 
@@ -300,16 +331,19 @@
     answer = pl.pallas_call(
         attend_kernel,
         out_shape=jax.ShapeDtypeStruct((CHIPS, ROWS, LANES), bf16),
-        in_specs=[vmem()],
-        out_specs=vmem(),
+        in_specs=[hbm()],
+        out_specs=hbm(),
         scratch_shapes=[
+            pltpu.VMEM((CHIPS, ROWS, LANES), bf16),
+            pltpu.VMEM((CHIPS, ROWS, LANES), bf16),
             pltpu.VMEM((LANES, KEYS), bf16),
-            pltpu.VMEM((KEYS, QBLOCK), f32),
-            pltpu.VMEM((KEYS, QBLOCK), f32),
-            pltpu.VMEM((KEYS, 2 * QBLOCK), bf16),
+            pltpu.VMEM((2, KEYS, QBLOCK), f32),
+            pltpu.VMEM((2, KEYS, QBLOCK), f32),
             pltpu.VMEM((KEYS, LANES), f32),
+            pltpu.SemaphoreType.DMA((NBLOCKS,)),
+            pltpu.SemaphoreType.DMA,
         ],
-        compiler_params=params(),
+        compiler_params=params(MIDDLE_VMEM),
         name="attend",
     )(received)
     returned = lax.all_to_all(answer, "tm", 0, 0, tiled=True).reshape(message_shape.shape)
@@ -318,10 +352,15 @@
     mine, other = pl.pallas_call(
         post_kernel,
         out_shape=(half_shape, half_shape),
-        in_specs=[vmem()] * 4 + [hbm()] * 4,
+        in_specs=[hbm()] + [vmem()] * 3 + [anywhere()] * 4,
         out_specs=(vmem(), vmem()),
-        scratch_shapes=weight_scratch(),
-        compiler_params=params(),
+        scratch_shapes=[
+            *weight_scratch(),
+            pltpu.VMEM(message_shape.shape, bf16),
+            pltpu.SemaphoreType.DMA((4,)),
+            pltpu.SemaphoreType.DMA((LOCAL_HEADS,)),
+        ],
+        compiler_params=params(LAST_VMEM),
         name="gradients",
     )(returned, assign, query_pairs, own_pairs, w_query, w_key, w_value, w_out)
     total = mine + lax.ppermute(other, "head", [(0, 1), (1, 0)])

time: 160 us -> 143 us (0.89)
  local copies, waits for them, and re-layouts: 9.65 us -> 0.75 us
  Pallas kernels: 39.8 us -> 31.2 us
    pallas_call x1, Pallas kernels: 30.5 us -> 17.5 us  [shards(): pl.pallas_call(attend_kernel, out_shape=jax.ShapeDtypeStruct((CHIPS, ROWS...]
    unnamed x24 -> x14, local copies, waits for them, and re-layouts: 8.94 us -> 0.03 us
    pallas_call x1, Pallas kernels: 4.75 us -> 7.37 us  [shards(): pl.pallas_call(pre_kernel, out_shape=(message_shape, pair_shape, pair_sha...]
    pallas_call x1, Pallas kernels: 4.58 us -> 6.33 us  [shards(): pl.pallas_call(post_kernel, out_shape=(half_shape, half_shape), in_specs=...]
where the time goes in v2:
time: 143 us; the launch traced here: 142 us
  blocking collectives  104 us (73%)
  Pallas kernels  31.2 us (22%)
  starting transfers between devices  4.23 us (3%)
  waiting for transfers between devices  1.54 us (1%)
    all_to_all x1, blocking collectives, shards(): lax.all_to_all(message.reshape(CHIPS, ROWS, LANES), 'tm', 0, 0, tiled=True)  58.2 us
    all_to_all x1, blocking collectives, shards(): lax.all_to_all(answer, 'tm', 0, 0, tiled=True).reshape(message_shape.shape)  45.6 us
    pallas_call x1, Pallas kernels, shards(): pl.pallas_call(attend_kernel, out_shape=jax.ShapeDtypeStruct((CHIPS, ROWS...  17.5 us
    pallas_call x1, Pallas kernels, shards(): pl.pallas_call(pre_kernel, out_shape=(message_shape, pair_shape, pair_sha...  7.37 us
    pallas_call x1, Pallas kernels, shards(): pl.pallas_call(post_kernel, out_shape=(half_shape, half_shape), in_specs=...  6.33 us
    ppermute x1, starting transfers between devices, shards(): total = mine + lax.ppermute(other, 'head', [(0, 1), (1, 0)])  4.23 us
  transfers between devices with their start and end apart: 1, of which 1 were waited for; matrix products, arithmetic and copies ran while one was open for 0% of the time, Pallas kernels for 0%

profile of v2, /device:TPU:1, one launch (start us, length us, event | category | flops | bytes accessed | tf_op | source)
XLA Modules:
  0.0 142.4 jit_solution(5907413523401143952)
XLA Ops:
  0.6 7.4 %project.1 = (bf16[16,8,48,128]{3,2,1,0:T(8,128)(2,1)}, bf16[8,128,128]{2,1,0:T(8,128)(2,1)}, bf16[8,128,128]{2,1,0:T(8,128)(2,1)}) custom-call(bf16[128,1024]{1,0:T(8,128)(2,1)} %bitcast.6, s32[1,128]{1,0:T(1,128)} %asg_ref.1, bf16[128,1024]{1,0:T(8,128)(2,1)} %bitcast.7, bf16[1024,1024]{1,0:T(8,128)(2,1)} %wq_hbm.3, bf16[1024,1024]{1,0:T(8,128)(2,1)} %wk_hbm.3, ...), custom_call_target="tpu_custom_call" | custom-call | tf_op jit(solution)/shard_map/project/pallas_call | solution.py:312
  8.0 0.0 copy-start.3
  8.0 0.0 copy-start.4
  8.0 0.0 copy-start.5
  8.0 58.2 %all_to_all.10.msg_hbm = bf16[128,48,128]{2,1,0:T(8,128)(2,1)S(1)} all-to-all(bf16[128,48,128]{2,1,0:T(8,128)(2,1)} %bitcast.5), channel_id=1, replica_groups=mesh['tm'=128,'head'=2] {'tm'}, dimensions={0} | all-to-all | bytes 3145728 | tf_op jit(solution)/shard_map/all_to_all | solution.py:330
  66.2 0.0 copy-start.1
  66.2 0.0 copy-start.2
  66.2 17.5 %attend.1 = bf16[128,48,128]{2,1,0:T(8,128)(2,1)S(1)} custom-call(bf16[128,48,128]{2,1,0:T(8,128)(2,1)S(1)} %all_to_all.10.msg_hbm), custom_call_target="tpu_custom_call" | custom-call | tf_op jit(solution)/shard_map/attend/pallas_call | solution.py:331
  83.7 0.0 copy-start
  83.7 0.0 copy-start.6
  83.7 45.6 %all_to_all.11 = bf16[128,48,128]{2,1,0:T(8,128)(2,1)S(1)} all-to-all(bf16[128,48,128]{2,1,0:T(8,128)(2,1)S(1)} %attend.1), channel_id=1, replica_groups=mesh['tm'=128,'head'=2] {'tm'}, dimensions={0} | all-to-all | bytes 3145728 | tf_op jit(solution)/shard_map/all_to_all | solution.py:349
  129.4 0.0 copy-done.3
  129.4 0.0 copy-done.4
  129.4 0.0 copy-done.5
  129.4 0.0 copy-done.1
  129.4 0.0 copy-done.2
  129.4 0.0 copy-done
  129.4 0.0 copy-done.6
  129.4 6.3 %gradients.1 = (f32[2,128,512]{2,1,0:T(8,128)S(1)}, f32[2,128,512]{2,1,0:T(8,128)S(1)}) custom-call(bf16[16,8,48,128]{3,2,1,0:T(8,128)(2,1)S(1)} %bitcast.4, s32[1,128]{1,0:T(1,128)S(1)} %copy-done.6, bf16[8,128,128]{2,1,0:T(8,128)(2,1)S(1)} %copy-done.4, bf16[8,128,128]{2,1,0:T(8,128)(2,1)S(1)} %copy-done.5, bf16[1024,1024]{1,0:T(8,128)(2,1)S(1)} %copy-done, ...), custom_call_target="tpu_custom_call" | custom-call | tf_op jit(solution)/shard_map/gradients/pallas_call | solution.py:352
  135.8 4.2 %collective-permute-start = (f32[2,128,512]{2,1,0:T(8,128)S(1)}, f32[2,128,512]{2,1,0:T(8,128)S(1)}, u32[]{:S(2)}, u32[]{:S(2)}) collective-permute-start(f32[2,128,512]{2,1,0:T(8,128)S(1)} %get-tuple-element.11), channel_id=1, source_target_pairs={{0,1},{1,0},{2,3},{3,2},{4,5},{5,4},{6,7},{7,6},{8,9},{9,8},{10,11... | collective-permute-start | bytes 1572872 | tf_op jit(solution)/shard_map/ppermute | solution.py:366
  140.0 1.5 %collective-permute-done = f32[2,128,512]{2,1,0:T(8,128)S(1)} collective-permute-done((f32[2,128,512]{2,1,0:T(8,128)S(1)}, f32[2,128,512]{2,1,0:T(8,128)S(1)}, u32[]{:S(2)}, u32[]{:S(2)}) %collective-permute-start) | collective-permute-done | bytes 524320 | tf_op jit(solution)/shard_map/ppermute | solution.py:366
  141.5 0.1 add_convert_fusion
  141.6 0.7 fusion
Async XLA Ops:
  8.0 121.4 %copy-start.3 = (bf16[1024,1024]{1,0:T(8,128)(2,1)S(1)}, bf16[1024,1024]{1,0:T(8,128)(2,1)}, u32[]{:S(2)}) copy-start(bf16[1024,1024]{1,0:T(8,128)(2,1)} %wo_hbm.3) | copy-start | bytes 6291460
  8.0 121.4 %copy-start.4 = (bf16[8,128,128]{2,1,0:T(8,128)(2,1)S(1)}, bf16[8,128,128]{2,1,0:T(8,128)(2,1)}, u32[]{:S(2)}) copy-start(bf16[8,128,128]{2,1,0:T(8,128)(2,1)} %get-tuple-element.8.qd_ref) | copy-start | bytes 786436
  8.0 121.4 %copy-start.5 = (bf16[8,128,128]{2,1,0:T(8,128)(2,1)S(1)}, bf16[8,128,128]{2,1,0:T(8,128)(2,1)}, u32[]{:S(2)}) copy-start(bf16[8,128,128]{2,1,0:T(8,128)(2,1)} %get-tuple-element.9.kv_ref) | copy-start | bytes 786436
  66.2 63.2 %copy-start.1 = (bf16[1024,1024]{1,0:T(8,128)(2,1)S(1)}, bf16[1024,1024]{1,0:T(8,128)(2,1)}, u32[]{:S(2)}) copy-start(bf16[1024,1024]{1,0:T(8,128)(2,1)} %wk_hbm.3) | copy-start | bytes 6291460
  66.2 63.2 %copy-start.2 = (bf16[1024,1024]{1,0:T(8,128)(2,1)S(1)}, bf16[1024,1024]{1,0:T(8,128)(2,1)}, u32[]{:S(2)}) copy-start(bf16[1024,1024]{1,0:T(8,128)(2,1)} %wv_hbm.3) | copy-start | bytes 6291460
  83.7 45.7 %copy-start = (bf16[1024,1024]{1,0:T(8,128)(2,1)S(1)}, bf16[1024,1024]{1,0:T(8,128)(2,1)}, u32[]{:S(2)}) copy-start(bf16[1024,1024]{1,0:T(8,128)(2,1)} %wq_hbm.3) | copy-start | bytes 6291460
  83.7 45.7 %copy-start.6 = (s32[1,128]{1,0:T(1,128)S(1)}, s32[1,128]{1,0:T(1,128)}, u32[]{:S(2)}) copy-start(s32[1,128]{1,0:T(1,128)} %asg_ref.1) | copy-start | bytes 1540
  135.8 5.8 %collective-permute-start = (f32[2,128,512]{2,1,0:T(8,128)S(1)}, f32[2,128,512]{2,1,0:T(8,128)S(1)}, u32[]{:S(2)}, u32[]{:S(2)}) collective-permute-start(f32[2,128,512]{2,1,0:T(8,128)S(1)} %get-tuple-element.11), channel_id=1, source_target_pairs={{0,1},{1,0},{2,3},{3,2},{4,5},{5,4},{6,7},{7,6},{8,9},{9,8},{10,11... | collective-permute-start | bytes 1572872 | tf_op jit(solution)/shard_map/ppermute | solution.py:366

commit v3 on v2

v3 whole, which is shorter than its diff:
```python
import jax
import jax.numpy as jnp
from jax import lax
from jax.experimental import pallas as pl
from jax.experimental.pallas import tpu as pltpu
from jax.sharding import PartitionSpec as P

HEAD_DIM = 64
MEM = 32
TOK = 128
D = 1024
HALF = 512
HEADS = 16
CHIPS = 128
SPLITS = CHIPS // HEADS
OWN = TOK // 2
OWN_MEM = MEM // 2
QROWS = OWN // SPLITS
ROWS = OWN_MEM + 2 * QROWS
CHUNK_HEADS = 4
GROUP = 2
CHUNK = CHUNK_HEADS * HEAD_DIM
CHUNKS = HEADS // CHUNK_HEADS
LANES = 2 * HEAD_DIM
KEYS = CHIPS * MEM
BLOCK_SEGS = 16
QBLOCK = BLOCK_SEGS * QROWS
KBLOCK = BLOCK_SEGS * MEM
KHALF = KBLOCK // 2
NBLOCKS = CHIPS // BLOCK_SEGS
SCALE = 0.125
MASKED = -3e38
FIRST_VMEM = 60 * 1024 * 1024
MIDDLE_VMEM = 40 * 1024 * 1024
LAST_VMEM = 32 * 1024 * 1024
f32 = jnp.float32
bf16 = jnp.bfloat16


def dot(a, b):
    return jnp.dot(a, b, preferred_element_type=f32)


def dot_nt(a, b):
    return lax.dot_general(a, b, (((1,), (1,)), ((), ())), preferred_element_type=f32)


def dot_tn(a, b):
    return lax.dot_general(a, b, (((0,), (0,)), ((), ())), preferred_element_type=f32)


def three_parts(x):
    high = x.astype(bf16).astype(f32)
    rest = x - high
    middle = rest.astype(bf16).astype(f32)
    low = (rest - middle).astype(bf16).astype(f32)
    return high, middle, low


def low_lanes(shape):
    return lax.broadcasted_iota(jnp.int32, shape, 1) < HEAD_DIM


def split_pair(pair):
    low = low_lanes(pair.shape)
    zero = jnp.zeros_like(pair)
    return jnp.concatenate([jnp.where(low, pair, zero), jnp.where(low, zero, pair)], axis=0)


def head_cols(matrix, head):
    return matrix[:, head * HEAD_DIM : (head + 1) * HEAD_DIM]


def onehot_rows(assign_row, first):
    rows = lax.broadcasted_iota(jnp.int32, (OWN_MEM, TOK), 0) + first
    return (rows == assign_row).astype(f32)


def pre_kernel(
    tok_hbm, asg_hbm, cot_hbm, wq_hbm, wk_hbm, wv_hbm, wo_hbm, msg_hbm, qd_ref, kv_ref,
    tok_ref, asg_ref, cot_ref, wq, wk, wv, wo, msg_ref, sems, w_sems, out_sems,
):
    half = lax.axis_index("head")
    own_rows = pl.ds(pl.multiple_of(half * OWN, OWN), OWN)
    moves = [(asg_hbm, asg_ref), (tok_hbm, tok_ref), (cot_hbm.at[own_rows, :], cot_ref)]
    copies = [pltpu.make_async_copy(source, target, sems.at[at]) for at, (source, target) in enumerate(moves)]
    weights = []
    for chunk in range(CHUNKS):
        cols = slice(chunk * CHUNK, (chunk + 1) * CHUNK)
        pairs = [
            (wk_hbm.at[:, cols], wk.at[:, cols]),
            (wv_hbm.at[:, cols], wv.at[:, cols]),
            (wq_hbm.at[:, cols], wq.at[:, cols]),
            (wo_hbm.at[cols, :], wo.at[cols, :]),
        ]
        weights.append(
            [pltpu.make_async_copy(source, target, w_sems.at[chunk, at]) for at, (source, target) in enumerate(pairs)]
        )
    for copy in copies + weights[0] + weights[1]:
        copy.start()
    copies[0].wait()
    onehot = onehot_rows(asg_ref[...], half * OWN_MEM)
    counts = jnp.sum(onehot, axis=1, keepdims=True)
    copies[1].wait()
    tokens = tok_ref[...]
    memory = (dot(onehot.astype(bf16), tokens) / counts).astype(bf16)
    rows = jnp.concatenate([memory, tokens], axis=0)
    own_tokens = tok_ref[own_rows, :]
    copies[2].wait()
    own_cotangent = cot_ref[...]
    lane = lax.broadcasted_iota(jnp.int32, (OWN, LANES), 1)
    sends = []
    for chunk in range(CHUNKS):
        cols = slice(chunk * CHUNK, (chunk + 1) * CHUNK)
        for copy in weights[chunk]:
            copy.wait()
        if chunk + 2 < CHUNKS:
            for copy in weights[chunk + 2]:
                copy.start()
        keys = dot(rows, wk[:, cols]).astype(bf16)
        values = dot(rows, wv[:, cols]).astype(bf16)
        queries = (dot(own_tokens, wq[:, cols]).astype(bf16).astype(f32) * SCALE).astype(bf16)
        grad_out = dot_nt(own_cotangent, wo[cols, :]).astype(bf16)
        for at_head in range(CHUNK_HEADS):
            head = chunk * CHUNK_HEADS + at_head
            pair = jnp.concatenate([head_cols(keys, at_head), head_cols(values, at_head)], axis=1)
            query_pair = jnp.concatenate([head_cols(queries, at_head), head_cols(grad_out, at_head)], axis=1)
            kv_ref[head] = pair[OWN_MEM:]
            qd_ref[head] = query_pair
            msg_ref[:, head, :OWN_MEM, :] = jnp.broadcast_to(pair[:OWN_MEM][None], (SPLITS, OWN_MEM, LANES))
    for chunk in range(CHUNKS // GROUP):
        group = range(chunk * CHUNK_HEADS * GROUP, (chunk + 1) * CHUNK_HEADS * GROUP)
        query_pairs = [qd_ref[head] for head in group]
        low = low_lanes((OWN, LANES))
        scores = [dot_nt(jnp.where(low, q, jnp.zeros_like(q)), kv_ref[head]) for head, q in zip(group, query_pairs)]
        row_max = [jnp.max(x, axis=1, keepdims=True) for x in scores]
        raised = [jnp.exp(x - m) for x, m in zip(scores, row_max)]
        row_sum = [jnp.sum(x, axis=1, keepdims=True) for x in raised]
        sides = [dot((x / t).astype(bf16), kv_ref[head]) for head, x, t in zip(group, raised, row_sum)]
        for head, query_pair, top, total, side in zip(group, query_pairs, row_max, row_sum, sides):
            for at, part in enumerate(three_parts(top) + three_parts(total)):
                side = jnp.where(lane == at, part, side)
            msg_ref[:, head, OWN_MEM:, :] = jnp.concatenate(
                [query_pair.astype(f32).reshape(SPLITS, QROWS, LANES), side.reshape(SPLITS, QROWS, LANES)], axis=1
            ).astype(bf16)
        heads = slice(group[0], group[-1] + 1)
        sends.append(pltpu.make_async_copy(msg_ref.at[:, heads], msg_hbm.at[:, heads], out_sems.at[chunk]))
        sends[-1].start()
    for send in sends:
        send.wait()


def attend_kernel(
    msg_hbm, away_hbm, tail_hbm, mine_hbm, other_hbm,
    msg_ref, away_ref, tail_ref, mine_ref, other_ref, kvt, scores, dprobs, accum, in_sems, away_sems, out_sems,
):
    def segs(j):
        return slice(j * BLOCK_SEGS, (j + 1) * BLOCK_SEGS)

    def block(j):
        return slice(j * KBLOCK, (j + 1) * KBLOCK)

    def kv_block(j):
        near = msg_ref[segs(j), :OWN_MEM, :].reshape(KHALF, LANES)
        return jnp.concatenate([near, away_ref[segs(j)].reshape(KHALF, LANES)], axis=0)

    copies = []
    for j in range(NBLOCKS):
        copies.append(pltpu.make_async_copy(msg_hbm.at[segs(j)], msg_ref.at[segs(j)], in_sems.at[j]))
        copies.append(pltpu.make_async_copy(away_hbm.at[segs(j)], away_ref.at[segs(j)], away_sems.at[j]))
    for copy in copies:
        copy.start()
    eye = (
        lax.broadcasted_iota(jnp.int32, (LANES, LANES), 0) == lax.broadcasted_iota(jnp.int32, (LANES, LANES), 1)
    ).astype(bf16)
    visible = lax.broadcasted_iota(jnp.int32, (KBLOCK, QBLOCK), 0) % KHALF // OWN_MEM < (
        lax.broadcasted_iota(jnp.int32, (KBLOCK, QBLOCK), 1) // QROWS
    )

    def fold(op, x):
        return op(x.reshape(KBLOCK // 8, 8, QBLOCK), axis=0)

    state = [{} for _ in range(NBLOCKS)]

    def score_stage(i):
        buf, mine = i % 3, state[i]
        copies[2 * i].wait()
        copies[2 * i + 1].wait()
        kvt[:, block(i)] = dot_nt(eye, kv_block(i)).astype(bf16)
        rows = msg_ref[segs(i), OWN_MEM:, :].astype(f32)
        query_pair = rows[:, :QROWS].reshape(QBLOCK, LANES)
        side = rows[:, QROWS:].reshape(QBLOCK, LANES).T
        mine["own_out"] = side[HEAD_DIM:]
        mine["own_max"] = side[0:1] + side[1:2] + side[2:3]
        mine["own_sum"] = side[3:4] + side[4:5] + side[5:6]
        mine["grad_t"] = query_pair.T[HEAD_DIM:]
        mine["pair_rows"] = split_pair(query_pair).astype(bf16)
        top = jnp.broadcast_to(mine["own_max"], (8, QBLOCK))
        for j in range(i + 1):
            both = dot_nt(kv_block(j), mine["pair_rows"])
            score = both[:, :QBLOCK]
            if j == i:
                score = jnp.where(visible, score, MASKED)
            scores[buf, block(j), :] = score
            dprobs[buf, block(j), :] = both[:, QBLOCK:]
            top = jnp.maximum(top, fold(jnp.max, score))
            yield
        mine["row_max"] = jnp.max(top, axis=0, keepdims=True)

    def weight_stage(i):
        buf, mine = i % 3, state[i]
        row_max = mine["row_max"]
        total = jnp.zeros((8, QBLOCK), f32)
        out = jnp.zeros((LANES, QBLOCK), f32)
        for j in range(i + 1):
            raised = jnp.exp(scores[buf, block(j), :] - row_max)
            scores[buf, block(j), :] = raised
            total = total + fold(jnp.sum, raised)
            out = out + dot(kvt[:, block(j)], raised.astype(bf16))
            yield
        own_share = mine["own_sum"] * jnp.exp(mine["own_max"] - row_max)
        row_sum = own_share + jnp.sum(total, axis=0, keepdims=True)
        inverse = 1.0 / row_sum
        heads_out = ((mine["own_out"] * own_share + out[HEAD_DIM:]) * inverse).astype(bf16).astype(f32)
        mine.update(row_sum=row_sum, inverse=inverse, heads_out=heads_out)
        mine["delta"] = jnp.sum(mine["grad_t"] * heads_out, axis=0, keepdims=True)

    def grad_stage(i):
        buf, mine = i % 3, state[i]
        grad = jnp.zeros((LANES, QBLOCK), f32)
        for j in range(i + 1):
            probs = scores[buf, block(j), :] * mine["inverse"]
            dscores = (probs * (dprobs[buf, block(j), :] - mine["delta"])).astype(bf16)
            both = jnp.concatenate([dscores, probs.astype(bf16)], axis=1)
            term = dot(both, mine["pair_rows"])
            if j == i:
                accum[block(j), :] = term
            else:
                accum[block(j), :] += term
            grad = grad + dot(kvt[:, block(j)], dscores)
            yield
        query_grad = grad[:HEAD_DIM]
        grad_high = query_grad.astype(bf16).astype(f32)
        main = jnp.concatenate([grad_high, mine["heads_out"]], axis=0).T
        row_at = lax.broadcasted_iota(jnp.int32, (HEAD_DIM, QBLOCK), 0)
        stats = jnp.zeros((HEAD_DIM, QBLOCK), f32)
        for at, part in enumerate(three_parts(mine["row_max"]) + three_parts(mine["row_sum"])):
            stats = jnp.where(row_at == at, part, stats)
        extra = jnp.concatenate([query_grad - grad_high, stats], axis=0).T
        tail_ref[segs(i)] = jnp.concatenate(
            [main.reshape(BLOCK_SEGS, QROWS, LANES), extra.reshape(BLOCK_SEGS, QROWS, LANES)], axis=1
        ).astype(bf16)

    for step in range(NBLOCKS + 2):
        running = []
        for at, stage in ((step - 2, grad_stage), (step - 1, weight_stage), (step, score_stage)):
            if 0 <= at < NBLOCKS:
                running.append(stage(at))
        while running:
            for one in list(running):
                if next(one, one) is one:
                    running.remove(one)

    sends = [pltpu.make_async_copy(tail_ref, tail_hbm, out_sems.at[0])]
    sends[0].start()
    for j in range(NBLOCKS):
        total = accum[block(j), :]
        mine_ref[segs(j)] = total[:KHALF].reshape(BLOCK_SEGS, OWN_MEM, LANES)
        other_ref[segs(j)] = total[KHALF:].astype(bf16).reshape(BLOCK_SEGS, OWN_MEM, LANES)
    sends.append(pltpu.make_async_copy(mine_ref, mine_hbm, out_sems.at[1]))
    sends.append(pltpu.make_async_copy(other_ref, other_hbm, out_sems.at[2]))
    sends[1].start()
    sends[2].start()
    for send in sends:
        send.wait()


def post_kernel(
    msg_hbm, asg_ref, qd_ref, kv_ref, wq, wk, wv, wo, out_ref, mine_ref, other_ref, msg_ref, in_sems,
):
    half = lax.axis_index("head")
    offset = pl.multiple_of(half * HALF, HALF)
    away = pl.multiple_of((1 - half) * HALF, HALF)
    parts = [
        pltpu.make_async_copy(msg_hbm.at[:, head], msg_ref.at[:, head], in_sems.at[head]) for head in range(HEADS)
    ]
    for copy in parts:
        copy.start()
    onehot = onehot_rows(asg_ref[...], half * OWN_MEM)
    counts = jnp.sum(onehot, axis=1, keepdims=True)
    onehot = onehot.astype(bf16)
    for copy in parts:
        copy.wait()
    heads = range(HEADS)
    mem_pairs = [jnp.sum(msg_ref[:, head, :OWN_MEM, :].astype(f32), axis=0) for head in heads]
    pair_rows = [split_pair(qd_ref[head]) for head in heads]
    both = [dot_nt(pair_rows[head], kv_ref[head]) for head in heads]
    rows = [msg_ref[:, head, OWN_MEM:, :].astype(f32) for head in heads]
    mains = [x[:, :QROWS].reshape(OWN, LANES) for x in rows]
    extras = [x[:, QROWS:].reshape(OWN, LANES) for x in rows]
    at = HEAD_DIM
    row_max = [x[:, at : at + 1] + x[:, at + 1 : at + 2] + x[:, at + 2 : at + 3] for x in extras]
    row_sum = [x[:, at + 3 : at + 4] + x[:, at + 4 : at + 5] + x[:, at + 5 : at + 6] for x in extras]
    products = [qd_ref[head].astype(f32) * mains[head] for head in heads]
    deltas = [jnp.sum(jnp.where(low_lanes(x.shape), 0.0, x), axis=1, keepdims=True) for x in products]
    probs = [jnp.exp(both[head][:OWN] - row_max[head]) / row_sum[head] for head in heads]
    dscores = [(probs[head] * (both[head][OWN:] - deltas[head])).astype(bf16) for head in heads]
    own_grads = [dot(dscores[head], kv_ref[head]) for head in heads]
    own_pairs = [
        dot_tn(jnp.concatenate([dscores[head], probs[head].astype(bf16)], axis=0), pair_rows[head]) for head in heads
    ]
    grads = [jnp.concatenate([own_pairs[head], mem_pairs[head]], axis=0) for head in heads]
    heads_out = [x[:, HEAD_DIM:] for x in mains]
    query_grads = [((mains[head] + extras[head] + own_grads[head]) * SCALE)[:, :HEAD_DIM] for head in heads]
    key_grads = [x[:, :HEAD_DIM] for x in grads]
    value_grads = [x[:, HEAD_DIM:] for x in grads]

    def merge(parts):
        return jnp.concatenate(parts, axis=1).astype(bf16)

    heads_out = merge(heads_out)
    query_grads = merge(query_grads)
    key_grads = merge(key_grads)
    value_grads = merge(value_grads)
    own_rows = pl.ds(pl.multiple_of(half * OWN, OWN), OWN)
    for start, keep in ((away, False), (offset, True)):
        rows = pl.ds(start, HALF)
        attended = dot(heads_out, wo[:, rows])
        total = dot_nt(key_grads, wk[rows, :]) + dot_nt(value_grads, wv[rows, :])
        high, middle, low = three_parts(total[TOK:] / counts)
        spread = dot_tn(onehot, high.astype(bf16)) + dot_tn(onehot, middle.astype(bf16)) + dot_tn(onehot, low.astype(bf16))
        grad_rows = pl.ds(0, TOK)
        if keep:
            out_ref[...] = attended
            mine_ref[...] = total[:TOK] + spread
            mine_ref[own_rows, :] += dot_nt(query_grads, wq[rows, :])
        else:
            other_ref[grad_rows, :] = total[:TOK] + spread
            other_ref[own_rows, :] += dot_nt(query_grads, wq[rows, :])
            other_ref[TOK:, :] = attended


def params(vmem_bytes):
    return pltpu.CompilerParams(vmem_limit_bytes=vmem_bytes)


def vmem():
    return pl.BlockSpec(memory_space=pltpu.VMEM)


def hbm():
    return pl.BlockSpec(memory_space=pltpu.HBM)


def anywhere():
    return pl.BlockSpec(memory_space=pl.ANY)


def swap_cores(x):
    return lax.ppermute(x, "head", [(0, 1), (1, 0)])


def shards(video, assign, w_query, w_key, w_value, w_out, cotangent):
    message_shape = (SPLITS, HEADS, ROWS, LANES)
    message, query_pairs, own_pairs = pl.pallas_call(
        pre_kernel,
        out_shape=(
            jax.ShapeDtypeStruct(message_shape, bf16),
            jax.ShapeDtypeStruct((HEADS, OWN, LANES), bf16),
            jax.ShapeDtypeStruct((HEADS, TOK, LANES), bf16),
        ),
        in_specs=[anywhere()] * 7,
        out_specs=(hbm(), vmem(), vmem()),
        scratch_shapes=[
            pltpu.VMEM((TOK, D), bf16),
            pltpu.VMEM((1, TOK), jnp.int32),
            pltpu.VMEM((OWN, D), bf16),
            *[pltpu.VMEM((D, D), bf16)] * 4,
            pltpu.VMEM(message_shape, bf16),
            pltpu.SemaphoreType.DMA((3,)),
            pltpu.SemaphoreType.DMA((CHUNKS, 4)),
            pltpu.SemaphoreType.DMA((CHUNKS,)),
        ],
        compiler_params=params(FIRST_VMEM),
        name="project",
    )(video[0], assign, cotangent[0], w_query, w_key, w_value, w_out)

    received = lax.all_to_all(message.reshape(CHIPS, ROWS, LANES), "tm", 0, 0, tiled=True)
    away = swap_cores(received[:, :OWN_MEM])
    part_shape = (CHIPS, OWN_MEM, LANES)
    tail, mine, other = pl.pallas_call(
        attend_kernel,
        out_shape=(
            jax.ShapeDtypeStruct(part_shape, bf16),
            jax.ShapeDtypeStruct(part_shape, f32),
            jax.ShapeDtypeStruct(part_shape, bf16),
        ),
        in_specs=[hbm(), hbm()],
        out_specs=(hbm(), hbm(), hbm()),
        scratch_shapes=[
            pltpu.VMEM((CHIPS, ROWS, LANES), bf16),
            pltpu.VMEM(part_shape, bf16),
            pltpu.VMEM(part_shape, bf16),
            pltpu.VMEM(part_shape, f32),
            pltpu.VMEM(part_shape, bf16),
            pltpu.VMEM((LANES, KEYS), bf16),
            pltpu.VMEM((3, KEYS, QBLOCK), f32),
            pltpu.VMEM((3, KEYS, QBLOCK), f32),
            pltpu.VMEM((KEYS, LANES), f32),
            pltpu.SemaphoreType.DMA((NBLOCKS,)),
            pltpu.SemaphoreType.DMA((NBLOCKS,)),
            pltpu.SemaphoreType.DMA((3,)),
        ],
        compiler_params=params(MIDDLE_VMEM),
        name="attend",
    )(received, away)
    sums = (mine + swap_cores(other).astype(f32)).astype(bf16)
    answer = jnp.concatenate([sums, tail], axis=1)
    returned = lax.all_to_all(answer, "tm", 0, 0, tiled=True).reshape(message_shape)

    attended, mine, other = pl.pallas_call(
        post_kernel,
        out_shape=(
            jax.ShapeDtypeStruct((OWN, HALF), f32),
            jax.ShapeDtypeStruct((TOK, HALF), f32),
            jax.ShapeDtypeStruct((TOK + OWN, HALF), f32),
        ),
        in_specs=[hbm()] + [vmem()] * 7,
        out_specs=(vmem(), vmem(), vmem()),
        scratch_shapes=[pltpu.VMEM(message_shape, bf16), pltpu.SemaphoreType.DMA((HEADS,))],
        compiler_params=params(LAST_VMEM),
        name="gradients",
    )(returned, assign, query_pairs, own_pairs, w_query, w_key, w_value, w_out)
    arrived = swap_cores(other)
    video_grad = (mine + arrived[:TOK]).astype(bf16)
    first = lax.axis_index("head") == 0
    far = arrived[TOK:]
    upper = jnp.where(first, attended, far)
    lower = jnp.where(first, far, attended)
    attended = jnp.concatenate([upper, lower], axis=0).astype(bf16)
    return (attended[None], video_grad[None])


def solution(mesh):
    placed = (P("tm", None, None), P("tm", None), P(), P(), P(), P(), P("tm", None, None))
    return jax.shard_map(
        shards,
        mesh=mesh,
        in_specs=placed,
        out_specs=(P("tm", None, "head"), P("tm", None, "head")),
        check_vma=False,
    )
```

time: 143 us -> 122 us (0.85)
  blocking collectives: 104 us -> 83.7 us
  Pallas kernels: 31.2 us -> 25.7 us
  waiting for transfers between devices: 1.54 us -> 4.42 us
  other arithmetic: 0.09 us -> 1.56 us
    all_to_all x1, blocking collectives: 58.2 us -> 46.7 us  [shards(): lax.all_to_all(message.reshape(CHIPS, ROWS, LANES), 'tm', 0, 0, tiled=True)]
    all_to_all x1, blocking collectives: 45.6 us -> 37 us  [shards(): lax.all_to_all(answer, 'tm', 0, 0, tiled=True).reshape(message_shape)]
    pallas_call x3, Pallas kernels: 31.2 us -> 25.7 us  [the longest x1 12.9 us: shards(): pl.pallas_call(attend_kernel, out_shape=(jax.ShapeDtypeStruct(part_shape,...]
    ppermute x1 -> x3, waiting for transfers between devices: 1.54 us -> 4.42 us  [swap_cores(): return lax.ppermute(x, 'head', [(0, 1), (1, 0)])]
    ppermute x1 -> x3, starting transfers between devices: 4.23 us -> 5.4 us  [swap_cores(): return lax.ppermute(x, 'head', [(0, 1), (1, 0)])]
  transfers between devices with their start and end apart: 1 -> 3, of which waited for: 1 -> 3; matrix products, arithmetic and copies ran while one was open for 0% -> 0% of each run, Pallas kernels for 0% -> 0%
where the time goes in v3:
time: 122 us
  blocking collectives  83.7 us (69%)
  Pallas kernels  25.7 us (21%)
  starting transfers between devices  5.4 us (4%)
  waiting for transfers between devices  4.42 us (4%)
  other arithmetic  1.56 us (1%)
    all_to_all x1, blocking collectives, shards(): lax.all_to_all(message.reshape(CHIPS, ROWS, LANES), 'tm', 0, 0, tiled=True)  46.7 us
    all_to_all x1, blocking collectives, shards(): lax.all_to_all(answer, 'tm', 0, 0, tiled=True).reshape(message_shape)  37 us
    pallas_call x1, Pallas kernels, shards(): pl.pallas_call(attend_kernel, out_shape=(jax.ShapeDtypeStruct(part_shape,...  12.9 us
    pallas_call x1, Pallas kernels, shards(): pl.pallas_call(pre_kernel, out_shape=(jax.ShapeDtypeStruct(message_shape,...  8.13 us
    ppermute x3, starting transfers between devices, swap_cores(): return lax.ppermute(x, 'head', [(0, 1), (1, 0)])  5.4 us
    pallas_call x1, Pallas kernels, shards(): pl.pallas_call(post_kernel, out_shape=(jax.ShapeDtypeStruct((OWN, HALF),...  4.64 us
    ppermute x3, waiting for transfers between devices, swap_cores(): return lax.ppermute(x, 'head', [(0, 1), (1, 0)])  4.42 us
  transfers between devices with their start and end apart: 3, of which 3 were waited for; matrix products, arithmetic and copies ran while one was open for 0% of the time, Pallas kernels for 0%

profile of v3, /device:TPU:1, one launch (start us, length us, event | category | flops | bytes accessed | tf_op | source)
XLA Modules:
  0.0 121.6 jit_solution(9320324181671431707)
XLA Ops:
  0.6 8.1 %project.1 = (bf16[8,16,32,128]{3,2,1,0:T(8,128)(2,1)}, bf16[16,64,128]{2,1,0:T(8,128)(2,1)}, bf16[16,128,128]{2,1,0:T(8,128)(2,1)}) custom-call(bf16[128,1024]{1,0:T(8,128)(2,1)} %bitcast.12, s32[1,128]{1,0:T(1,128)} %asg_ref.1, bf16[128,1024]{1,0:T(8,128)(2,1)} %bitcast.13, bf16[1024,1024]{1,0:T(8,128)(2,1)} %wq.1, bf16[1024,1024]{1,0:T(8,128)(2,1)} %wk.1, ...), custom_call_target="tpu_custom_call" | custom-call | tf_op jit(solution)/shard_map/project/pallas_call | solution.py:365
  8.8 0.0 copy-start.5
  8.8 46.7 %all_to_all.10.msg_hbm = bf16[128,32,128]{2,1,0:T(8,128)(2,1)S(1)} all-to-all(bf16[128,32,128]{2,1,0:T(8,128)(2,1)} %bitcast.11), channel_id=1, replica_groups=mesh['tm'=128,'head'=2] {'tm'}, dimensions={0} | all-to-all | bytes 2097152 | tf_op jit(solution)/shard_map/all_to_all | solution.py:388
  55.5 0.0 copy-start.3
  55.6 2.9 %collective-permute-start = (bf16[128,16,128]{2,1,0:T(8,128)(2,1)S(1)}, bf16[128,16,128]{2,1,0:T(8,128)(2,1)S(1)}, u32[]{:S(2)}, u32[]{:S(2)}) collective-permute-start(bf16[128,16,128]{2,1,0:T(8,128)(2,1)S(1)} %slice.12), channel_id=1, source_target_pairs={{0,1},{1,0},{2,3},{3,2},{4,5},{5,4},{6,7},{7,6},{8,9},{9,8},{10,11... | collective-permute-start | bytes 1572872 | tf_op jit(solution)/shard_map/ppermute | solution.py:360
  58.4 1.5 %collective-permute-done.away_hbm = bf16[128,16,128]{2,1,0:T(8,128)(2,1)S(1)} collective-permute-done((bf16[128,16,128]{2,1,0:T(8,128)(2,1)S(1)}, bf16[128,16,128]{2,1,0:T(8,128)(2,1)S(1)}, u32[]{:S(2)}, u32[]{:S(2)}) %collective-permute-start) | collective-permute-done | bytes 524320 | tf_op jit(solution)/shard_map/ppermute | solution.py:360
  60.0 0.0 copy-start.4
  60.0 12.9 %attend.1 = (bf16[128,16,128]{2,1,0:T(8,128)(2,1)S(1)}, f32[128,16,128]{2,1,0:T(8,128)S(1)}, bf16[128,16,128]{2,1,0:T(8,128)(2,1)S(1)}) custom-call(bf16[128,32,128]{2,1,0:T(8,128)(2,1)S(1)} %all_to_all.10.msg_hbm, bf16[128,16,128]{2,1,0:T(8,128)(2,1)S(1)} %collective-permute-done.away_hbm), custom_call_target="tpu_custom_call" | custom-call | tf_op jit(solution)/shard_map/attend/pallas_call | solution.py:391
  72.9 0.5 collective-permute-start.1
  73.4 1.5 %collective-permute-done.1 = bf16[128,16,128]{2,1,0:T(8,128)(2,1)S(1)} collective-permute-done((bf16[128,16,128]{2,1,0:T(8,128)(2,1)S(1)}, bf16[128,16,128]{2,1,0:T(8,128)(2,1)S(1)}, u32[]{:S(2)}, u32[]{:S(2)}) %collective-permute-start.1) | collective-permute-done | bytes 524320 | tf_op jit(solution)/shard_map/ppermute | solution.py:360
  74.9 0.0 copy-start.2
  74.9 0.1 add_convert_fusion
  75.0 0.0 copy-start
  75.1 0.0 copy-start.1
  75.1 0.0 copy-start.6
  75.1 0.1 pad_maximum_fusion
  75.2 37.0 %all_to_all.11 = bf16[128,32,128]{2,1,0:T(8,128)(2,1)S(1)} all-to-all(bf16[128,32,128]{2,1,0:T(8,128)(2,1)S(1)} %pad_maximum_fusion), channel_id=1, replica_groups=mesh['tm'=128,'head'=2] {'tm'}, dimensions={0} | all-to-all | bytes 2097152 | tf_op jit(solution)/shard_map/all_to_all | solution.py:419
  112.1 0.0 copy-done.5
  112.1 0.0 copy-done.3
  112.1 0.0 copy-done.4
  112.1 0.0 copy-done.2
  112.1 0.0 copy-done
  112.1 0.0 copy-done.1
  112.2 0.0 copy-done.6
  112.2 4.6 %gradients.1 = (f32[64,512]{1,0:T(8,128)S(1)}, f32[128,512]{1,0:T(8,128)S(1)}, f32[192,512]{1,0:T(8,128)S(1)}) custom-call(bf16[8,16,32,128]{3,2,1,0:T(8,128)(2,1)S(1)} %bitcast.10, s32[1,128]{1,0:T(1,128)S(1)} %copy-done.6, bf16[16,64,128]{2,1,0:T(8,128)(2,1)S(1)} %copy-done.5, bf16[16,128,128]{2,1,0:T(8,128)(2,1)S(1)} %copy-done.4, ...), custom_call_target="tpu_custom_call" | custom-call | tf_op jit(solution)/shard_map/gradients/pallas_call | solution.py:421
  116.8 2.0 %collective-permute-start.2 = (f32[192,512]{1,0:T(8,128)S(1)}, f32[192,512]{1,0:T(8,128)S(1)}, u32[]{:S(2)}, u32[]{:S(2)}) collective-permute-start(f32[192,512]{1,0:T(8,128)S(1)} %get-tuple-element.18), channel_id=1, source_target_pairs={{0,1},{1,0},{2,3},{3,2},{4,5},{5,4},{6,7},{7,6},{8,9},{9,8},{10,11... | collective-permute-start | bytes 1179656 | tf_op jit(solution)/shard_map/ppermute | solution.py:360
  118.9 1.3 %collective-permute-done.2 = f32[192,512]{1,0:T(8,128)S(1)} collective-permute-done((f32[192,512]{1,0:T(8,128)S(1)}, f32[192,512]{1,0:T(8,128)S(1)}, u32[]{:S(2)}, u32[]{:S(2)}) %collective-permute-start.2) | collective-permute-done | bytes 393248 | tf_op jit(solution)/shard_map/ppermute | solution.py:360
  120.2 0.7 pad_maximum_fusion.1
  120.9 0.7 fusion.1
  (2 shorter events, 0.1 us)
Async XLA Ops:
  8.8 103.4 %copy-start.5 = (bf16[16,64,128]{2,1,0:T(8,128)(2,1)S(1)}, bf16[16,64,128]{2,1,0:T(8,128)(2,1)}, u32[]{:S(2)}) copy-start(bf16[16,64,128]{2,1,0:T(8,128)(2,1)} %get-tuple-element.15.qd_ref) | copy-start | bytes 786436
  55.5 56.6 %copy-start.3 = (bf16[1024,1024]{1,0:T(8,128)(2,1)S(1)}, bf16[1024,1024]{1,0:T(8,128)(2,1)}, u32[]{:S(2)}) copy-start(bf16[1024,1024]{1,0:T(8,128)(2,1)} %wo.1) | copy-start | bytes 6291460
  55.6 4.4 %collective-permute-start = (bf16[128,16,128]{2,1,0:T(8,128)(2,1)S(1)}, bf16[128,16,128]{2,1,0:T(8,128)(2,1)S(1)}, u32[]{:S(2)}, u32[]{:S(2)}) collective-permute-start(bf16[128,16,128]{2,1,0:T(8,128)(2,1)S(1)} %slice.12), channel_id=1, source_target_pairs={{0,1},{1,0},{2,3},{3,2},{4,5},{5,4},{6,7},{7,6},{8,9},{9,8},{10,11... | collective-permute-start | bytes 1572872 | tf_op jit(solution)/shard_map/ppermute | solution.py:360
  60.0 52.1 %copy-start.4 = (bf16[16,128,128]{2,1,0:T(8,128)(2,1)S(1)}, bf16[16,128,128]{2,1,0:T(8,128)(2,1)}, u32[]{:S(2)}) copy-start(bf16[16,128,128]{2,1,0:T(8,128)(2,1)} %get-tuple-element.16.kv_ref) | copy-start | bytes 1572868
  72.9 2.0 %collective-permute-start.1 = (bf16[128,16,128]{2,1,0:T(8,128)(2,1)S(1)}, bf16[128,16,128]{2,1,0:T(8,128)(2,1)S(1)}, u32[]{:S(2)}, u32[]{:S(2)}) collective-permute-start(bf16[128,16,128]{2,1,0:T(8,128)(2,1)S(1)} %get-tuple-element.13), channel_id=1, source_target_pairs={{0,1},{1,0},{2,3},{3,2},{4,5},{5,4},{6,7},{7,6},{8,9},{9,8},{10,11... | collective-permute-start | bytes 1572872 | tf_op jit(solution)/shard_map/ppermute | solution.py:360
  74.9 37.2 %copy-start.2 = (bf16[1024,1024]{1,0:T(8,128)(2,1)S(1)}, bf16[1024,1024]{1,0:T(8,128)(2,1)}, u32[]{:S(2)}) copy-start(bf16[1024,1024]{1,0:T(8,128)(2,1)} %wv.1) | copy-start | bytes 6291460
  75.0 37.1 %copy-start = (bf16[1024,1024]{1,0:T(8,128)(2,1)S(1)}, bf16[1024,1024]{1,0:T(8,128)(2,1)}, u32[]{:S(2)}) copy-start(bf16[1024,1024]{1,0:T(8,128)(2,1)} %wq.1) | copy-start | bytes 6291460
  75.1 37.1 %copy-start.1 = (bf16[1024,1024]{1,0:T(8,128)(2,1)S(1)}, bf16[1024,1024]{1,0:T(8,128)(2,1)}, u32[]{:S(2)}) copy-start(bf16[1024,1024]{1,0:T(8,128)(2,1)} %wk.1) | copy-start | bytes 6291460
  75.1 37.1 %copy-start.6 = (s32[1,128]{1,0:T(1,128)S(1)}, s32[1,128]{1,0:T(1,128)}, u32[]{:S(2)}) copy-start(s32[1,128]{1,0:T(1,128)} %asg_ref.1) | copy-start | bytes 1540
  116.8 3.4 %collective-permute-start.2 = (f32[192,512]{1,0:T(8,128)S(1)}, f32[192,512]{1,0:T(8,128)S(1)}, u32[]{:S(2)}, u32[]{:S(2)}) collective-permute-start(f32[192,512]{1,0:T(8,128)S(1)} %get-tuple-element.18), channel_id=1, source_target_pairs={{0,1},{1,0},{2,3},{3,2},{4,5},{5,4},{6,7},{7,6},{8,9},{9,8},{10,11... | collective-permute-start | bytes 1179656 | tf_op jit(solution)/shard_map/ppermute | solution.py:360

commit v4 on v3

v4 whole, which is shorter than its diff:
```python
import jax
import jax.numpy as jnp
from jax import lax
from jax.experimental import pallas as pl
from jax.experimental.pallas import tpu as pltpu
from jax.sharding import PartitionSpec as P

HEAD_DIM = 64
MEM = 32
TOK = 128
D = 1024
HALF = 512
HEADS = 16
CHIPS = 128
SPLITS = CHIPS // HEADS
OWN = TOK // 2
OWN_MEM = MEM // 2
QROWS = OWN // SPLITS
MEM_PAIRS = OWN_MEM // 2
QUERY_PAIRS = QROWS // 2
PAIRS = MEM_PAIRS + QUERY_PAIRS + 1
STATS_AT = MEM_PAIRS + QUERY_PAIRS
CHUNK_HEADS = 4
GROUP = 2
CHUNK = CHUNK_HEADS * HEAD_DIM
CHUNKS = HEADS // CHUNK_HEADS
LANES = 2 * HEAD_DIM
KEYS = CHIPS * MEM
BLOCK_SEGS = 16
QBLOCK = BLOCK_SEGS * QROWS
KBLOCK = BLOCK_SEGS * MEM
KHALF = KBLOCK // 2
NBLOCKS = CHIPS // BLOCK_SEGS
SCALE = 0.125
MASKED = -3e38
FIRST_VMEM = 60 * 1024 * 1024
MIDDLE_VMEM = 40 * 1024 * 1024
LAST_VMEM = 45 * 1024 * 1024
f32 = jnp.float32
bf16 = jnp.bfloat16


def dot(a, b):
    return jnp.dot(a, b, preferred_element_type=f32)


def dot_nt(a, b):
    return lax.dot_general(a, b, (((1,), (1,)), ((), ())), preferred_element_type=f32)


def dot_tn(a, b):
    return lax.dot_general(a, b, (((0,), (0,)), ((), ())), preferred_element_type=f32)


def three_parts(x):
    high = x.astype(bf16).astype(f32)
    rest = x - high
    middle = rest.astype(bf16).astype(f32)
    low = (rest - middle).astype(bf16).astype(f32)
    return high, middle, low


def low_lanes(shape):
    return lax.broadcasted_iota(jnp.int32, shape, 1) < HEAD_DIM


def split_pair(pair):
    low = low_lanes(pair.shape)
    zero = jnp.zeros_like(pair)
    return jnp.concatenate([jnp.where(low, pair, zero), jnp.where(low, zero, pair)], axis=0)


def head_cols(matrix, head):
    return matrix[:, head * HEAD_DIM : (head + 1) * HEAD_DIM]


def onehot_rows(assign_row, first):
    rows = lax.broadcasted_iota(jnp.int32, (OWN_MEM, TOK), 0) + first
    return (rows == assign_row).astype(f32)


def pre_kernel(
    tok_hbm, asg_hbm, cot_hbm, wq_hbm, wk_hbm, wv_hbm, wo_hbm, msg_hbm, qd_hbm, kv_hbm, side_hbm,
    tok_ref, asg_ref, cot_ref, wq, wk, wv, wo, msg_ref, qd_ref, kv_ref, side_ref, sems, w_sems, out_sems,
):
    half = lax.axis_index("head")
    own_rows = pl.ds(pl.multiple_of(half * OWN, OWN), OWN)
    moves = [(asg_hbm, asg_ref), (tok_hbm, tok_ref), (cot_hbm.at[own_rows, :], cot_ref)]
    copies = [pltpu.make_async_copy(source, target, sems.at[at]) for at, (source, target) in enumerate(moves)]
    weights = []
    for chunk in range(CHUNKS):
        cols = slice(chunk * CHUNK, (chunk + 1) * CHUNK)
        pairs = [
            (wk_hbm.at[:, cols], wk.at[:, cols]),
            (wv_hbm.at[:, cols], wv.at[:, cols]),
            (wq_hbm.at[:, cols], wq.at[:, cols]),
            (wo_hbm.at[cols, :], wo.at[cols, :]),
        ]
        weights.append(
            [pltpu.make_async_copy(source, target, w_sems.at[chunk, at]) for at, (source, target) in enumerate(pairs)]
        )
    for copy in copies + weights[0] + weights[1]:
        copy.start()
    copies[0].wait()
    onehot = onehot_rows(asg_ref[...], half * OWN_MEM)
    counts = jnp.sum(onehot, axis=1, keepdims=True)
    copies[1].wait()
    tokens = tok_ref[...]
    memory = (dot(onehot.astype(bf16), tokens) / counts).astype(bf16)
    rows = jnp.concatenate([memory, tokens], axis=0)
    own_tokens = tok_ref[own_rows, :]
    copies[2].wait()
    own_cotangent = cot_ref[...]
    lane = lax.broadcasted_iota(jnp.int32, (OWN, LANES), 1)
    sublane = lax.broadcasted_iota(jnp.int32, (OWN, LANES), 0)
    sends = []
    for chunk in range(CHUNKS):
        cols = slice(chunk * CHUNK, (chunk + 1) * CHUNK)
        for copy in weights[chunk]:
            copy.wait()
        if chunk + 2 < CHUNKS:
            for copy in weights[chunk + 2]:
                copy.start()
        keys = dot(rows, wk[:, cols]).astype(bf16)
        values = dot(rows, wv[:, cols]).astype(bf16)
        queries = (dot(own_tokens, wq[:, cols]).astype(bf16).astype(f32) * SCALE).astype(bf16)
        grad_out = dot_nt(own_cotangent, wo[cols, :]).astype(bf16)
        for at_head in range(CHUNK_HEADS):
            head = chunk * CHUNK_HEADS + at_head
            pair = jnp.concatenate([head_cols(keys, at_head), head_cols(values, at_head)], axis=1)
            query_pair = jnp.concatenate([head_cols(queries, at_head), head_cols(grad_out, at_head)], axis=1)
            kv_ref[head] = pair[OWN_MEM:]
            qd_ref[head] = query_pair
            mem_pairs = pair[:OWN_MEM].reshape(MEM_PAIRS, 2, LANES)
            msg_ref[:, head, :MEM_PAIRS] = jnp.broadcast_to(mem_pairs[None], (SPLITS, MEM_PAIRS, 2, LANES))
            msg_ref[:, head, MEM_PAIRS:STATS_AT] = query_pair.reshape(SPLITS, QUERY_PAIRS, 2, LANES)
        heads = slice(chunk * CHUNK_HEADS, (chunk + 1) * CHUNK_HEADS)
        sends.append(pltpu.make_async_copy(kv_ref.at[heads], kv_hbm.at[heads], out_sems.at[0, chunk]))
        sends.append(pltpu.make_async_copy(qd_ref.at[heads], qd_hbm.at[heads], out_sems.at[1, chunk]))
        sends[-2].start()
        sends[-1].start()
    for chunk in range(CHUNKS // GROUP):
        group = range(chunk * CHUNK_HEADS * GROUP, (chunk + 1) * CHUNK_HEADS * GROUP)
        query_pairs = [qd_ref[head] for head in group]
        low = low_lanes((OWN, LANES))
        scores = [dot_nt(jnp.where(low, q, jnp.zeros_like(q)), kv_ref[head]) for head, q in zip(group, query_pairs)]
        row_max = [jnp.max(x, axis=1, keepdims=True) for x in scores]
        raised = [jnp.exp(x - m) for x, m in zip(scores, row_max)]
        row_sum = [jnp.sum(x, axis=1, keepdims=True) for x in raised]
        sides = [dot((x / t).astype(bf16), kv_ref[head]) for head, x, t in zip(group, raised, row_sum)]
        for head, query_pair, top, total, side in zip(group, query_pairs, row_max, row_sum, sides):
            log_sum = top + jnp.log(total)
            products = jnp.where(low, 0.0, query_pair.astype(f32) * side)
            delta = jnp.sum(products, axis=1, keepdims=True)
            side_ref[head] = jnp.where(low, log_sum, side)
            stats = jnp.zeros((OWN, LANES), f32)
            for at, part in enumerate(three_parts(log_sum) + three_parts(delta)):
                stats = jnp.where(lane // QROWS == at, part, stats)
            stats = jnp.where(lane % QROWS == sublane % QROWS, stats, 0.0)
            stats = jnp.sum(stats.reshape(SPLITS, QROWS, LANES), axis=1, keepdims=True)
            msg_ref[:, head, STATS_AT] = jnp.broadcast_to(stats, (SPLITS, 2, LANES)).astype(bf16)
        heads = slice(group[0], group[-1] + 1)
        sends.append(pltpu.make_async_copy(msg_ref.at[:, heads], msg_hbm.at[:, heads], out_sems.at[2, chunk]))
        sends.append(pltpu.make_async_copy(side_ref.at[heads], side_hbm.at[heads], out_sems.at[3, chunk]))
        sends[-2].start()
        sends[-1].start()
    for send in sends:
        send.wait()


def attend_kernel(msg_ref, away_ref, tail_ref, mine_ref, other_ref, kv, kvt, scores, dprobs, accum):
    def segs(j):
        return slice(j * BLOCK_SEGS, (j + 1) * BLOCK_SEGS)

    def block(j):
        return slice(j * KBLOCK, (j + 1) * KBLOCK)

    def kv_block(j):
        return kv[block(j), :]

    eye = (
        lax.broadcasted_iota(jnp.int32, (LANES, LANES), 0) == lax.broadcasted_iota(jnp.int32, (LANES, LANES), 1)
    ).astype(bf16)
    visible = lax.broadcasted_iota(jnp.int32, (KBLOCK, QBLOCK), 0) % KHALF // OWN_MEM < (
        lax.broadcasted_iota(jnp.int32, (KBLOCK, QBLOCK), 1) // QROWS
    )

    def fold(op, x):
        return op(x.reshape(KBLOCK // 8, 8, QBLOCK), axis=0)

    row = lax.broadcasted_iota(jnp.int32, (2 * BLOCK_SEGS, QBLOCK), 0)
    column = lax.broadcasted_iota(jnp.int32, (2 * BLOCK_SEGS, QBLOCK), 1)
    spread = (row == column // QROWS * 2).astype(bf16)
    square_row = lax.broadcasted_iota(jnp.int32, (LANES, LANES), 0)
    square_column = lax.broadcasted_iota(jnp.int32, (LANES, LANES), 1)
    same_query = square_row % QROWS == square_column % QROWS
    gather = (
        lax.broadcasted_iota(jnp.int32, (8, LANES), 0) == lax.broadcasted_iota(jnp.int32, (8, LANES), 1) // QROWS
    ).astype(bf16)
    blocks = range(NBLOCKS)
    stats = [dot_tn(spread, msg_ref[segs(i), STATS_AT].reshape(2 * BLOCK_SEGS, LANES)) for i in blocks]
    stats = [dot_nt(gather, jnp.where(same_query, x, 0.0).astype(bf16)) for x in stats]
    state = [
        {"own_log": x[0:1] + x[1:2] + x[2:3], "own_delta": x[3:4] + x[4:5] + x[5:6]} for x in stats
    ]

    def score_stage(i):
        buf, mine = i % 3, state[i]
        kv[i * KBLOCK : i * KBLOCK + KHALF, :] = msg_ref[segs(i), :MEM_PAIRS].reshape(KHALF, LANES)
        kv[i * KBLOCK + KHALF : (i + 1) * KBLOCK, :] = away_ref[segs(i)].reshape(KHALF, LANES)
        kvt[:, block(i)] = dot_nt(eye, kv_block(i)).astype(bf16)
        query_pair = msg_ref[segs(i), MEM_PAIRS:STATS_AT].reshape(QBLOCK, LANES).astype(f32)
        mine["grad_t"] = query_pair.T[HEAD_DIM:]
        mine["pair_rows"] = split_pair(query_pair).astype(bf16)
        top = jnp.full((8, QBLOCK), MASKED, f32)
        for j in range(i + 1):
            both = dot_nt(kv_block(j), mine["pair_rows"])
            score = both[:, :QBLOCK]
            if j == i:
                score = jnp.where(visible, score, MASKED)
            scores[buf, block(j), :] = score
            dprobs[buf, block(j), :] = both[:, QBLOCK:]
            top = jnp.maximum(top, fold(jnp.max, score))
            yield
        mine["row_max"] = jnp.maximum(jnp.max(top, axis=0, keepdims=True), mine["own_log"])

    def weight_stage(i):
        buf, mine = i % 3, state[i]
        row_max = mine["row_max"]
        total = jnp.zeros((8, QBLOCK), f32)
        out = jnp.zeros((LANES, QBLOCK), f32)
        for j in range(i + 1):
            raised = jnp.exp(scores[buf, block(j), :] - row_max)
            scores[buf, block(j), :] = raised
            total = total + fold(jnp.sum, raised)
            out = out + dot(kvt[:, block(j)], raised.astype(bf16))
            yield
        own_share = jnp.exp(mine["own_log"] - row_max)
        row_sum = own_share + jnp.sum(total, axis=0, keepdims=True)
        inverse = 1.0 / row_sum
        out = out[HEAD_DIM:] * inverse
        mine.update(log_sum=row_max + jnp.log(row_sum), inverse=inverse, out=out)
        mine["delta"] = jnp.sum(mine["grad_t"] * out, axis=0, keepdims=True) + own_share * inverse * mine["own_delta"]

    def grad_stage(i):
        buf, mine = i % 3, state[i]
        grad = jnp.zeros((LANES, QBLOCK), f32)
        for j in range(i + 1):
            probs = scores[buf, block(j), :] * mine["inverse"]
            dscores = (probs * (dprobs[buf, block(j), :] - mine["delta"])).astype(bf16)
            both = jnp.concatenate([dscores, probs.astype(bf16)], axis=1)
            term = dot(both, mine["pair_rows"])
            if j < i:
                term = accum[block(j), :] + term
            if i < NBLOCKS - 1:
                accum[block(j), :] = term
            else:
                mine_ref[j * KHALF : (j + 1) * KHALF, :] = term[:KHALF]
                other_ref[segs(j)] = term[KHALF:].astype(bf16).reshape(BLOCK_SEGS, MEM_PAIRS, 2, LANES)
            grad = grad + dot(kvt[:, block(j)], dscores)
            yield
        main = jnp.concatenate([grad[:HEAD_DIM], mine["out"]], axis=0).T.astype(bf16)
        tail_ref[segs(i), :QUERY_PAIRS] = main.reshape(BLOCK_SEGS, QUERY_PAIRS, 2, LANES)

    for step in range(NBLOCKS + 2):
        running = []
        for at, stage in ((step - 2, grad_stage), (step - 1, weight_stage), (step, score_stage)):
            if 0 <= at < NBLOCKS:
                running.append(stage(at))
        while running:
            for one in list(running):
                if next(one, one) is one:
                    running.remove(one)

    stats = [jnp.zeros((LANES, LANES), f32) for _ in blocks]
    for at in range(3):
        parts = [three_parts(one["log_sum"])[at] for one in state]
        stats = [jnp.where(square_row // QROWS == at, part, x) for part, x in zip(parts, stats)]
    stats = [dot_nt(spread, jnp.where(same_query, x, 0.0).astype(bf16)) for x in stats]
    for i in blocks:
        tail_ref[segs(i), QUERY_PAIRS] = stats[i].astype(bf16).reshape(BLOCK_SEGS, 2, LANES)


def join_kernel(mine_ref, other_ref, tail_ref, out_ref):
    out_ref[:, MEM_PAIRS:] = tail_ref[...]
    for j in range(NBLOCKS):
        segs = slice(j * BLOCK_SEGS, (j + 1) * BLOCK_SEGS)
        far = other_ref[segs].reshape(KHALF, LANES).astype(f32)
        total = (mine_ref[j * KHALF : (j + 1) * KHALF, :] + far).astype(bf16)
        out_ref[segs, :MEM_PAIRS] = total.reshape(BLOCK_SEGS, MEM_PAIRS, 2, LANES)


def post_kernel(
    msg_ref, asg_ref, qd_ref, kv_ref, side_ref, wq, wk, wv, wo_hbm, out_ref, mine_ref, other_ref, wo, wo_sem,
):
    half = lax.axis_index("head")
    offset = pl.multiple_of(half * HALF, HALF)
    away = pl.multiple_of((1 - half) * HALF, HALF)
    wo_copy = pltpu.make_async_copy(wo_hbm, wo, wo_sem)
    wo_copy.start()
    onehot = onehot_rows(asg_ref[...], half * OWN_MEM)
    counts = jnp.sum(onehot, axis=1, keepdims=True)
    onehot = onehot.astype(bf16)
    heads = range(HEADS)
    def mem_sum(head):
        parts = [msg_ref[k, head, :MEM_PAIRS].reshape(OWN_MEM, LANES).astype(f32) for k in range(SPLITS)]
        return sum(parts[1:], parts[0])

    mem_pairs = [mem_sum(head) for head in heads]
    pair_rows = [split_pair(qd_ref[head]) for head in heads]
    both = [dot_nt(pair_rows[head], kv_ref[head]) for head in heads]
    returned = [msg_ref[:, head, MEM_PAIRS:STATS_AT].reshape(OWN, LANES).astype(f32) for head in heads]
    sublane = lax.broadcasted_iota(jnp.int32, (OWN, LANES), 0)
    lane = lax.broadcasted_iota(jnp.int32, (OWN, LANES), 1)
    same_query = sublane % QROWS == lane % QROWS

    def log_sum_of(head):
        stats = msg_ref[:, head, STATS_AT].astype(f32)[:, :1]
        stats = jnp.broadcast_to(stats, (SPLITS, QROWS, LANES)).reshape(OWN, LANES)
        return jnp.sum(jnp.where(same_query, stats, 0.0), axis=1, keepdims=True)

    log_sums = [log_sum_of(head) for head in heads]
    shares = [jnp.exp(side_ref[head][:, :1] - log_sums[head]) for head in heads]
    mains = [(returned[head] + shares[head] * side_ref[head]).astype(bf16).astype(f32) for head in heads]
    products = [qd_ref[head].astype(f32) * mains[head] for head in heads]
    deltas = [jnp.sum(jnp.where(low_lanes(x.shape), 0.0, x), axis=1, keepdims=True) for x in products]
    probs = [jnp.exp(both[head][:OWN] - log_sums[head]) for head in heads]
    dscores = [(probs[head] * (both[head][OWN:] - deltas[head])).astype(bf16) for head in heads]
    own_grads = [dot(dscores[head], kv_ref[head]) for head in heads]
    own_pairs = [
        dot_tn(jnp.concatenate([dscores[head], probs[head].astype(bf16)], axis=0), pair_rows[head]) for head in heads
    ]
    grads = [jnp.concatenate([own_pairs[head], mem_pairs[head]], axis=0) for head in heads]
    heads_out = [x[:, HEAD_DIM:] for x in mains]
    query_grads = [((returned[head] + own_grads[head]) * SCALE)[:, :HEAD_DIM] for head in heads]
    key_grads = [x[:, :HEAD_DIM] for x in grads]
    value_grads = [x[:, HEAD_DIM:] for x in grads]

    def merge(parts):
        return jnp.concatenate(parts, axis=1).astype(bf16)

    heads_out = merge(heads_out)
    query_grads = merge(query_grads)
    key_grads = merge(key_grads)
    value_grads = merge(value_grads)
    own_rows = pl.ds(pl.multiple_of(half * OWN, OWN), OWN)
    for start, keep in ((away, False), (offset, True)):
        rows = pl.ds(start, HALF)
        total = dot_nt(key_grads, wk[rows, :]) + dot_nt(value_grads, wv[rows, :])
        high, middle, low = three_parts(total[TOK:] / counts)
        spread = dot_tn(onehot, high.astype(bf16)) + dot_tn(onehot, middle.astype(bf16)) + dot_tn(onehot, low.astype(bf16))
        grad_rows = pl.ds(0, TOK)
        if keep:
            mine_ref[...] = total[:TOK] + spread
            mine_ref[own_rows, :] += dot_nt(query_grads, wq[rows, :])
        else:
            other_ref[grad_rows, :] = total[:TOK] + spread
            other_ref[own_rows, :] += dot_nt(query_grads, wq[rows, :])
    wo_copy.wait()
    other_ref[TOK:, :] = dot(heads_out, wo[:, pl.ds(away, HALF)])
    out_ref[...] = dot(heads_out, wo[:, pl.ds(offset, HALF)])


def finish_kernel(attended_ref, mine_ref, arrived_ref, out_ref, grad_ref):
    half = lax.axis_index("head")
    own_rows = pl.ds(pl.multiple_of(half * OWN, OWN), OWN)
    far_rows = pl.ds(pl.multiple_of((1 - half) * OWN, OWN), OWN)
    out_ref[0, own_rows, :] = attended_ref[...].astype(bf16)
    out_ref[0, far_rows, :] = arrived_ref[TOK:, :].astype(bf16)
    grad_ref[0] = (mine_ref[...] + arrived_ref[:TOK, :]).astype(bf16)


def params(vmem_bytes):
    return pltpu.CompilerParams(vmem_limit_bytes=vmem_bytes)


def vmem():
    return pl.BlockSpec(memory_space=pltpu.VMEM)


def hbm():
    return pl.BlockSpec(memory_space=pltpu.HBM)


def anywhere():
    return pl.BlockSpec(memory_space=pl.ANY)


def swap_cores(x):
    return lax.ppermute(x, "head", [(0, 1), (1, 0)])


def shards(video, assign, w_query, w_key, w_value, w_out, cotangent):
    message_shape = (SPLITS, HEADS, PAIRS, 2, LANES)
    chip_shape = (CHIPS, PAIRS, 2, LANES)
    message, query_pairs, own_pairs, own_sides = pl.pallas_call(
        pre_kernel,
        out_shape=(
            jax.ShapeDtypeStruct(message_shape, bf16),
            jax.ShapeDtypeStruct((HEADS, OWN, LANES), bf16),
            jax.ShapeDtypeStruct((HEADS, TOK, LANES), bf16),
            jax.ShapeDtypeStruct((HEADS, OWN, LANES), f32),
        ),
        in_specs=[anywhere()] * 7,
        out_specs=(hbm(), hbm(), hbm(), hbm()),
        scratch_shapes=[
            pltpu.VMEM((TOK, D), bf16),
            pltpu.VMEM((1, TOK), jnp.int32),
            pltpu.VMEM((OWN, D), bf16),
            *[pltpu.VMEM((D, D), bf16)] * 4,
            pltpu.VMEM(message_shape, bf16),
            pltpu.VMEM((HEADS, OWN, LANES), bf16),
            pltpu.VMEM((HEADS, TOK, LANES), bf16),
            pltpu.VMEM((HEADS, OWN, LANES), f32),
            pltpu.SemaphoreType.DMA((3,)),
            pltpu.SemaphoreType.DMA((CHUNKS, 4)),
            pltpu.SemaphoreType.DMA((4, CHUNKS)),
        ],
        compiler_params=params(FIRST_VMEM),
        name="project",
    )(video[0], assign, cotangent[0], w_query, w_key, w_value, w_out)

    received = lax.all_to_all(message.reshape(chip_shape), "tm", 0, 0, tiled=True)
    away = swap_cores(received[:, :MEM_PAIRS])
    part_shape = (CHIPS, MEM_PAIRS, 2, LANES)
    tail_shape = (CHIPS, PAIRS - MEM_PAIRS, 2, LANES)
    mine_shape = (CHIPS * OWN_MEM, LANES)
    tail, mine, other = pl.pallas_call(
        attend_kernel,
        out_shape=(
            jax.ShapeDtypeStruct(tail_shape, bf16),
            jax.ShapeDtypeStruct(mine_shape, f32),
            jax.ShapeDtypeStruct(part_shape, bf16),
        ),
        in_specs=[vmem(), vmem()],
        out_specs=(vmem(), vmem(), vmem()),
        scratch_shapes=[
            pltpu.VMEM((KEYS, LANES), bf16),
            pltpu.VMEM((LANES, KEYS), bf16),
            pltpu.VMEM((3, KEYS, QBLOCK), f32),
            pltpu.VMEM((3, KEYS, QBLOCK), f32),
            pltpu.VMEM((KEYS, LANES), f32),
        ],
        compiler_params=params(MIDDLE_VMEM),
        name="attend",
    )(received, away)
    answer = pl.pallas_call(
        join_kernel,
        out_shape=jax.ShapeDtypeStruct(chip_shape, bf16),
        in_specs=[vmem()] * 3,
        out_specs=vmem(),
        compiler_params=params(LAST_VMEM),
        name="join",
    )(mine, swap_cores(other), tail)
    returned = lax.all_to_all(answer, "tm", 0, 0, tiled=True).reshape(message_shape)

    attended, mine, other = pl.pallas_call(
        post_kernel,
        out_shape=(
            jax.ShapeDtypeStruct((OWN, HALF), f32),
            jax.ShapeDtypeStruct((TOK, HALF), f32),
            jax.ShapeDtypeStruct((TOK + OWN, HALF), f32),
        ),
        in_specs=[vmem()] * 8 + [anywhere()],
        out_specs=(vmem(), vmem(), vmem()),
        scratch_shapes=[pltpu.VMEM((D, D), bf16), pltpu.SemaphoreType.DMA],
        compiler_params=params(LAST_VMEM),
        name="gradients",
    )(returned, assign, query_pairs, own_pairs, own_sides, w_query, w_key, w_value, w_out)
    half_shape = jax.ShapeDtypeStruct((1, TOK, HALF), bf16)
    return pl.pallas_call(
        finish_kernel,
        out_shape=(half_shape, half_shape),
        in_specs=[vmem()] * 3,
        out_specs=(vmem(), vmem()),
        compiler_params=params(LAST_VMEM),
        name="finish",
    )(attended, mine, swap_cores(other))


def solution(mesh):
    placed = (P("tm", None, None), P("tm", None), P(), P(), P(), P(), P("tm", None, None))
    return jax.shard_map(
        shards,
        mesh=mesh,
        in_specs=placed,
        out_specs=(P("tm", None, "head"), P("tm", None, "head")),
        check_vma=False,
    )
```

time: 122 us -> 113 us (0.926)
  blocking collectives: 83.7 us -> 75 us
  other arithmetic: 1.56 us -> 0 us
  Pallas kernels: 25.7 us -> 27.1 us
    all_to_all x1, blocking collectives: 37 us -> 32.5 us  [shards(): lax.all_to_all(answer, 'tm', 0, 0, tiled=True).reshape(message_shape)]
    all_to_all x1, blocking collectives: 46.7 us -> 42.5 us  [shards(): lax.all_to_all(message.reshape(chip_shape), 'tm', 0, 0, tiled=True)]
    pallas_call x1, Pallas kernels: 4.64 us -> 6.28 us  [shards(): pl.pallas_call(post_kernel, out_shape=(jax.ShapeDtypeStruct((OWN, HALF),...]
    pallas_call x1 -> x3, Pallas kernels: 12.9 us -> 13.1 us  [the longest x1 11.7 us: shards(): pl.pallas_call(attend_kernel, out_shape=(jax.ShapeDtypeStruct(tail_shape,...]
where the time goes in v4:
time: 113 us
  blocking collectives  75 us (66%)
  Pallas kernels  27.1 us (24%)
  starting transfers between devices  5.49 us (5%)
  waiting for transfers between devices  4.42 us (4%)
    all_to_all x1, blocking collectives, shards(): lax.all_to_all(message.reshape(chip_shape), 'tm', 0, 0, tiled=True)  42.5 us
    all_to_all x1, blocking collectives, shards(): lax.all_to_all(answer, 'tm', 0, 0, tiled=True).reshape(message_shape)  32.5 us
    pallas_call x1, Pallas kernels, shards(): pl.pallas_call(attend_kernel, out_shape=(jax.ShapeDtypeStruct(tail_shape,...  11.7 us
    pallas_call x1, Pallas kernels, shards(): pl.pallas_call(pre_kernel, out_shape=(jax.ShapeDtypeStruct(message_shape,...  7.8 us
    pallas_call x1, Pallas kernels, shards(): pl.pallas_call(post_kernel, out_shape=(jax.ShapeDtypeStruct((OWN, HALF),...  6.28 us
    ppermute x3, starting transfers between devices, swap_cores(): return lax.ppermute(x, 'head', [(0, 1), (1, 0)])  5.49 us
    ppermute x3, waiting for transfers between devices, swap_cores(): return lax.ppermute(x, 'head', [(0, 1), (1, 0)])  4.42 us
  transfers between devices with their start and end apart: 3, of which 3 were waited for; matrix products, arithmetic and copies ran while one was open for 0% of the time, Pallas kernels for 0%

profile of v4, /device:TPU:1, one launch (start us, length us, event | category | flops | bytes accessed | tf_op | source)
XLA Modules:
  0.0 113.2 jit_solution(17534497701021060526)
XLA Ops:
  0.6 7.8 %project.1 = (bf16[8,16,13,2,128]{4,3,2,1,0:T(2,128)(2,1)}, bf16[16,64,128]{2,1,0:T(8,128)(2,1)}, bf16[16,128,128]{2,1,0:T(8,128)(2,1)}, f32[16,64,128]{2,1,0:T(8,128)}) custom-call(bf16[128,1024]{1,0:T(8,128)(2,1)} %bitcast.6, s32[1,128]{1,0:T(1,128)} %asg_ref.1, bf16[128,1024]{1,0:T(8,128)(2,1)} %bitcast.7, bf16[1024,1024]{1,0:T(8,128)(2,1)} %wq.1, ...), custom_call_target="tpu_custom_call" | custom-call | tf_op jit(solution)/shard_map/project/pallas_call | solution.py:396
  8.4 0.0 copy-start.4
  8.4 0.0 copy-start.5
  8.5 42.5 %all_to_all.10.msg_ref = bf16[128,13,2,128]{3,2,1,0:T(2,128)(2,1)S(1)} all-to-all(bf16[128,13,2,128]{3,2,1,0:T(2,128)(2,1)} %bitcast.5), channel_id=1, replica_groups=mesh['tm'=128,'head'=2] {'tm'}, dimensions={0} | all-to-all | bytes 1703936 | tf_op jit(solution)/shard_map/all_to_all | solution.py:423
  50.9 0.0 copy-start.2
  50.9 0.4 slice.4
  51.3 2.9 %collective-permute-start = (bf16[128,8,2,128]{3,2,1,0:T(2,128)(2,1)S(1)}, bf16[128,8,2,128]{3,2,1,0:T(2,128)(2,1)S(1)}, u32[]{:S(2)}, u32[]{:S(2)}) collective-permute-start(bf16[128,8,2,128]{3,2,1,0:T(2,128)(2,1)S(1)} %slice.4), channel_id=1, source_target_pairs={{0,1},{1,0},{2,3},{3,2},{4,5},{5,4},{6,7},{7,6},{8,9},{9,8},{10,11... | collective-permute-start | bytes 1572872 | tf_op jit(solution)/shard_map/ppermute | solution.py:390
  54.2 1.5 %collective-permute-done.away_ref = bf16[128,8,2,128]{3,2,1,0:T(2,128)(2,1)S(1)} collective-permute-done((bf16[128,8,2,128]{3,2,1,0:T(2,128)(2,1)S(1)}, bf16[128,8,2,128]{3,2,1,0:T(2,128)(2,1)S(1)}, u32[]{:S(2)}, u32[]{:S(2)}) %collective-permute-start) | collective-permute-done | bytes 524320 | tf_op jit(solution)/shard_map/ppermute | solution.py:390
  55.8 0.0 copy-start.3
  55.8 11.7 %attend.1 = (bf16[128,5,2,128]{3,2,1,0:T(2,128)(2,1)S(1)}, f32[2048,128]{1,0:T(8,128)S(1)}, bf16[128,8,2,128]{3,2,1,0:T(2,128)(2,1)S(1)}) custom-call(bf16[128,13,2,128]{3,2,1,0:T(2,128)(2,1)S(1)} %all_to_all.10.msg_ref, bf16[128,8,2,128]{3,2,1,0:T(2,128)(2,1)S(1)} %collective-permute-done.away_ref), custom_call_target="tpu_custom_call" | custom-call | tf_op jit(solution)/shard_map/attend/pallas_call | solution.py:428
  67.4 0.7 collective-permute-start.1
  68.1 1.5 %collective-permute-done.1.other_ref = bf16[128,8,2,128]{3,2,1,0:T(2,128)(2,1)S(1)} collective-permute-done((bf16[128,8,2,128]{3,2,1,0:T(2,128)(2,1)S(1)}, bf16[128,8,2,128]{3,2,1,0:T(2,128)(2,1)S(1)}, u32[]{:S(2)}, u32[]{:S(2)}) %collective-permute-start.1) | collective-permute-done | bytes 524320 | tf_op jit(solution)/shard_map/ppermute | solution.py:390
  69.7 0.0 copy-start
  69.7 0.0 copy-start.1
  69.7 0.0 copy-start.6
  69.7 0.7 join.1
  70.3 32.5 %all_to_all.11 = bf16[128,13,2,128]{3,2,1,0:T(2,128)(2,1)S(1)} all-to-all(bf16[128,13,2,128]{3,2,1,0:T(2,128)(2,1)S(1)} %join.1), channel_id=1, replica_groups=mesh['tm'=128,'head'=2] {'tm'}, dimensions={0} | all-to-all | bytes 1703936 | tf_op jit(solution)/shard_map/all_to_all | solution.py:455
  102.9 0.0 copy-done.4
  102.9 0.0 copy-done.5
  102.9 0.0 copy-done.2
  102.9 0.0 copy-done.3
  102.9 0.0 copy-done
  102.9 0.0 copy-done.1
  102.9 0.0 copy-done.6
  102.9 6.3 %gradients.1 = (f32[64,512]{1,0:T(8,128)S(1)}, f32[128,512]{1,0:T(8,128)S(1)}, f32[192,512]{1,0:T(8,128)S(1)}) custom-call(bf16[8,16,13,2,128]{4,3,2,1,0:T(2,128)(2,1)S(1)} %bitcast.4, s32[1,128]{1,0:T(1,128)S(1)} %copy-done.6, bf16[16,64,128]{2,1,0:T(8,128)(2,1)S(1)} %copy-done.5, bf16[16,128,128]{2,1,0:T(8,128)(2,1)S(1)} %copy-done.3, ...), custom_call_target="tpu_custom_call" | custom-call | tf_op jit(solution)/shard_map/gradients/pallas_call | solution.py:457
  109.2 1.9 %collective-permute-start.2 = (f32[192,512]{1,0:T(8,128)S(1)}, f32[192,512]{1,0:T(8,128)S(1)}, u32[]{:S(2)}, u32[]{:S(2)}) collective-permute-start(f32[192,512]{1,0:T(8,128)S(1)} %get-tuple-element.21), channel_id=1, source_target_pairs={{0,1},{1,0},{2,3},{3,2},{4,5},{5,4},{6,7},{7,6},{8,9},{9,8},{10,11... | collective-permute-start | bytes 1179656 | tf_op jit(solution)/shard_map/ppermute | solution.py:390
  111.1 1.3 %collective-permute-done.2.arrived_ref = f32[192,512]{1,0:T(8,128)S(1)} collective-permute-done((f32[192,512]{1,0:T(8,128)S(1)}, f32[192,512]{1,0:T(8,128)S(1)}, u32[]{:S(2)}, u32[]{:S(2)}) %collective-permute-start.2) | collective-permute-done | bytes 393248 | tf_op jit(solution)/shard_map/ppermute | solution.py:390
  112.4 0.7 finish.1
Async XLA Ops:
  8.4 94.4 %copy-start.4 = (f32[16,64,128]{2,1,0:T(8,128)S(1)}, f32[16,64,128]{2,1,0:T(8,128)}, u32[]{:S(2)}) copy-start(f32[16,64,128]{2,1,0:T(8,128)} %get-tuple-element.18.side_ref) | copy-start | bytes 1572868
  8.4 94.4 %copy-start.5 = (bf16[16,64,128]{2,1,0:T(8,128)(2,1)S(1)}, bf16[16,64,128]{2,1,0:T(8,128)(2,1)}, u32[]{:S(2)}) copy-start(bf16[16,64,128]{2,1,0:T(8,128)(2,1)} %get-tuple-element.16.qd_ref) | copy-start | bytes 786436
  50.9 52.0 %copy-start.2 = (bf16[1024,1024]{1,0:T(8,128)(2,1)S(1)}, bf16[1024,1024]{1,0:T(8,128)(2,1)}, u32[]{:S(2)}) copy-start(bf16[1024,1024]{1,0:T(8,128)(2,1)} %wv.1) | copy-start | bytes 6291460
  51.3 4.5 %collective-permute-start = (bf16[128,8,2,128]{3,2,1,0:T(2,128)(2,1)S(1)}, bf16[128,8,2,128]{3,2,1,0:T(2,128)(2,1)S(1)}, u32[]{:S(2)}, u32[]{:S(2)}) collective-permute-start(bf16[128,8,2,128]{3,2,1,0:T(2,128)(2,1)S(1)} %slice.4), channel_id=1, source_target_pairs={{0,1},{1,0},{2,3},{3,2},{4,5},{5,4},{6,7},{7,6},{8,9},{9,8},{10,11... | collective-permute-start | bytes 1572872 | tf_op jit(solution)/shard_map/ppermute | solution.py:390
  55.8 47.1 %copy-start.3 = (bf16[16,128,128]{2,1,0:T(8,128)(2,1)S(1)}, bf16[16,128,128]{2,1,0:T(8,128)(2,1)}, u32[]{:S(2)}) copy-start(bf16[16,128,128]{2,1,0:T(8,128)(2,1)} %get-tuple-element.17.kv_ref) | copy-start | bytes 1572868
  67.4 2.2 %collective-permute-start.1 = (bf16[128,8,2,128]{3,2,1,0:T(2,128)(2,1)S(1)}, bf16[128,8,2,128]{3,2,1,0:T(2,128)(2,1)S(1)}, u32[]{:S(2)}, u32[]{:S(2)}) collective-permute-start(bf16[128,8,2,128]{3,2,1,0:T(2,128)(2,1)S(1)} %get-tuple-element.14), channel_id=1, source_target_pairs={{0,1},{1,0},{2,3},{3,2},{4,5},{5,4},{6,7},{7,6},{8,9},{9,8},{10,11... | collective-permute-start | bytes 1572872 | tf_op jit(solution)/shard_map/ppermute | solution.py:390
  69.7 33.2 %copy-start = (bf16[1024,1024]{1,0:T(8,128)(2,1)S(1)}, bf16[1024,1024]{1,0:T(8,128)(2,1)}, u32[]{:S(2)}) copy-start(bf16[1024,1024]{1,0:T(8,128)(2,1)} %wq.1) | copy-start | bytes 6291460
  69.7 33.2 %copy-start.1 = (bf16[1024,1024]{1,0:T(8,128)(2,1)S(1)}, bf16[1024,1024]{1,0:T(8,128)(2,1)}, u32[]{:S(2)}) copy-start(bf16[1024,1024]{1,0:T(8,128)(2,1)} %wk.1) | copy-start | bytes 6291460
  69.7 33.3 %copy-start.6 = (s32[1,128]{1,0:T(1,128)S(1)}, s32[1,128]{1,0:T(1,128)}, u32[]{:S(2)}) copy-start(s32[1,128]{1,0:T(1,128)} %asg_ref.1) | copy-start | bytes 1540
  109.2 3.2 %collective-permute-start.2 = (f32[192,512]{1,0:T(8,128)S(1)}, f32[192,512]{1,0:T(8,128)S(1)}, u32[]{:S(2)}, u32[]{:S(2)}) collective-permute-start(f32[192,512]{1,0:T(8,128)S(1)} %get-tuple-element.21), channel_id=1, source_target_pairs={{0,1},{1,0},{2,3},{3,2},{4,5},{5,4},{6,7},{7,6},{8,9},{9,8},{10,11... | collective-permute-start | bytes 1179656 | tf_op jit(solution)/shard_map/ppermute | solution.py:390

commit v5 on v4

--- a/solution.py
+++ b/solution.py
@@ -35,7 +35,7 @@
 MASKED = -3e38
 FIRST_VMEM = 60 * 1024 * 1024
 MIDDLE_VMEM = 40 * 1024 * 1024
-LAST_VMEM = 45 * 1024 * 1024
+LAST_VMEM = 32 * 1024 * 1024
 f32 = jnp.float32
 bf16 = jnp.bfloat16
 
@@ -168,7 +168,15 @@
         send.wait()
 
 
-def attend_kernel(msg_ref, away_ref, tail_ref, mine_ref, other_ref, kv, kvt, scores, dprobs, accum):
+def attend_kernel(
+    msg_ref, away_ref, qd_hbm, own_hbm, side_hbm, tail_ref, mine_ref, other_ref, qd_ref, own_ref, side_ref,
+    kv, kvt, scores, dprobs, accum, sems,
+):
+    moves = [(qd_hbm, qd_ref), (own_hbm, own_ref), (side_hbm, side_ref)]
+    copies = [pltpu.make_async_copy(source, target, sems.at[at]) for at, (source, target) in enumerate(moves)]
+    for copy in copies:
+        copy.start()
+
     def segs(j):
         return slice(j * BLOCK_SEGS, (j + 1) * BLOCK_SEGS)
 
@@ -224,49 +232,57 @@
             yield
         mine["row_max"] = jnp.maximum(jnp.max(top, axis=0, keepdims=True), mine["own_log"])
 
-    def weight_stage(i):
-        buf, mine = i % 3, state[i]
-        row_max = mine["row_max"]
+    def middle_stage(i):
+        mine = state[i] if i < NBLOCKS else None
+        last = state[i - 1] if i > 0 else None
         total = jnp.zeros((8, QBLOCK), f32)
         out = jnp.zeros((LANES, QBLOCK), f32)
-        for j in range(i + 1):
-            raised = jnp.exp(scores[buf, block(j), :] - row_max)
-            scores[buf, block(j), :] = raised
-            total = total + fold(jnp.sum, raised)
-            out = out + dot(kvt[:, block(j)], raised.astype(bf16))
+        grad = jnp.zeros((LANES, QBLOCK), f32)
+        for j in range(min(i + 1, NBLOCKS)):
+            right = []
+            if mine is not None:
+                raised = jnp.exp(scores[i % 3, block(j), :] - mine["row_max"])
+                scores[i % 3, block(j), :] = raised
+                total = total + fold(jnp.sum, raised)
+                right.append(raised.astype(bf16))
+            if last is not None and j < i:
+                probs = scores[(i - 1) % 3, block(j), :] * last["inverse"]
+                dscores = (probs * (dprobs[(i - 1) % 3, block(j), :] - last["delta"])).astype(bf16)
+                both = jnp.concatenate([dscores, probs.astype(bf16)], axis=1)
+                term = dot(both, last["pair_rows"])
+                if j < i - 1:
+                    term = accum[block(j), :] + term
+                if i < NBLOCKS:
+                    accum[block(j), :] = term
+                else:
+                    mine_ref[j * KHALF : (j + 1) * KHALF, :] = term[:KHALF]
+                    other_ref[segs(j)] = term[KHALF:].astype(bf16).reshape(BLOCK_SEGS, MEM_PAIRS, 2, LANES)
+                right.append(dscores)
+            product = dot(kvt[:, block(j)], jnp.concatenate(right, axis=1) if len(right) > 1 else right[0])
+            if mine is not None:
+                out = out + product[:, :QBLOCK]
+            if last is not None and j < i:
+                grad = grad + product[:, -QBLOCK:]
             yield
-        own_share = jnp.exp(mine["own_log"] - row_max)
-        row_sum = own_share + jnp.sum(total, axis=0, keepdims=True)
-        inverse = 1.0 / row_sum
-        out = out[HEAD_DIM:] * inverse
-        mine.update(log_sum=row_max + jnp.log(row_sum), inverse=inverse, out=out)
-        mine["delta"] = jnp.sum(mine["grad_t"] * out, axis=0, keepdims=True) + own_share * inverse * mine["own_delta"]
-
-    def grad_stage(i):
-        buf, mine = i % 3, state[i]
-        grad = jnp.zeros((LANES, QBLOCK), f32)
-        for j in range(i + 1):
-            probs = scores[buf, block(j), :] * mine["inverse"]
-            dscores = (probs * (dprobs[buf, block(j), :] - mine["delta"])).astype(bf16)
-            both = jnp.concatenate([dscores, probs.astype(bf16)], axis=1)
-            term = dot(both, mine["pair_rows"])
-            if j < i:
-                term = accum[block(j), :] + term
-            if i < NBLOCKS - 1:
-                accum[block(j), :] = term
-            else:
-                mine_ref[j * KHALF : (j + 1) * KHALF, :] = term[:KHALF]
-                other_ref[segs(j)] = term[KHALF:].astype(bf16).reshape(BLOCK_SEGS, MEM_PAIRS, 2, LANES)
-            grad = grad + dot(kvt[:, block(j)], dscores)
-            yield
-        main = jnp.concatenate([grad[:HEAD_DIM], mine["out"]], axis=0).T.astype(bf16)
-        tail_ref[segs(i), :QUERY_PAIRS] = main.reshape(BLOCK_SEGS, QUERY_PAIRS, 2, LANES)
+        if mine is not None:
+            own_share = jnp.exp(mine["own_log"] - mine["row_max"])
+            row_sum = own_share + jnp.sum(total, axis=0, keepdims=True)
+            inverse = 1.0 / row_sum
+            out = out[HEAD_DIM:] * inverse
+            mine.update(log_sum=mine["row_max"] + jnp.log(row_sum), inverse=inverse, out=out)
+            mine["delta"] = (
+                jnp.sum(mine["grad_t"] * out, axis=0, keepdims=True) + own_share * inverse * mine["own_delta"]
+            )
+        if last is not None:
+            main = jnp.concatenate([grad[:HEAD_DIM], last["out"]], axis=0).T.astype(bf16)
+            tail_ref[segs(i - 1), :QUERY_PAIRS] = main.reshape(BLOCK_SEGS, QUERY_PAIRS, 2, LANES)
 
     for step in range(NBLOCKS + 2):
         running = []
-        for at, stage in ((step - 2, grad_stage), (step - 1, weight_stage), (step, score_stage)):
-            if 0 <= at < NBLOCKS:
-                running.append(stage(at))
+        if step > 0:
+            running.append(middle_stage(step - 1))
+        if step < NBLOCKS:
+            running.append(score_stage(step))
         while running:
             for one in list(running):
                 if next(one, one) is one:
@@ -279,6 +295,8 @@
     stats = [dot_nt(spread, jnp.where(same_query, x, 0.0).astype(bf16)) for x in stats]
     for i in blocks:
         tail_ref[segs(i), QUERY_PAIRS] = stats[i].astype(bf16).reshape(BLOCK_SEGS, 2, LANES)
+    for copy in copies:
+        copy.wait()
 
 
 def join_kernel(mine_ref, other_ref, tail_ref, out_ref):
@@ -291,13 +309,11 @@
 
 
 def post_kernel(
-    msg_ref, asg_ref, qd_ref, kv_ref, side_ref, wq, wk, wv, wo_hbm, out_ref, mine_ref, other_ref, wo, wo_sem,
+    msg_ref, asg_ref, qd_ref, kv_ref, side_ref, wq, wk, wv, wo, out_ref, mine_ref, other_ref,
 ):
     half = lax.axis_index("head")
     offset = pl.multiple_of(half * HALF, HALF)
     away = pl.multiple_of((1 - half) * HALF, HALF)
-    wo_copy = pltpu.make_async_copy(wo_hbm, wo, wo_sem)
-    wo_copy.start()
     onehot = onehot_rows(asg_ref[...], half * OWN_MEM)
     counts = jnp.sum(onehot, axis=1, keepdims=True)
     onehot = onehot.astype(bf16)
@@ -356,7 +372,6 @@
         else:
             other_ref[grad_rows, :] = total[:TOK] + spread
             other_ref[own_rows, :] += dot_nt(query_grads, wq[rows, :])
-    wo_copy.wait()
     other_ref[TOK:, :] = dot(heads_out, wo[:, pl.ds(away, HALF)])
     out_ref[...] = dot(heads_out, wo[:, pl.ds(offset, HALF)])
 
@@ -425,25 +440,28 @@
     part_shape = (CHIPS, MEM_PAIRS, 2, LANES)
     tail_shape = (CHIPS, PAIRS - MEM_PAIRS, 2, LANES)
     mine_shape = (CHIPS * OWN_MEM, LANES)
-    tail, mine, other = pl.pallas_call(
+    saved = (query_pairs, own_pairs, own_sides)
+    tail, mine, other, *saved = pl.pallas_call(
         attend_kernel,
         out_shape=(
             jax.ShapeDtypeStruct(tail_shape, bf16),
             jax.ShapeDtypeStruct(mine_shape, f32),
             jax.ShapeDtypeStruct(part_shape, bf16),
+            *[jax.ShapeDtypeStruct(one.shape, one.dtype) for one in saved],
         ),
-        in_specs=[vmem(), vmem()],
-        out_specs=(vmem(), vmem(), vmem()),
+        in_specs=[vmem(), vmem()] + [anywhere()] * 3,
+        out_specs=(vmem(),) * 6,
         scratch_shapes=[
             pltpu.VMEM((KEYS, LANES), bf16),
             pltpu.VMEM((LANES, KEYS), bf16),
             pltpu.VMEM((3, KEYS, QBLOCK), f32),
             pltpu.VMEM((3, KEYS, QBLOCK), f32),
             pltpu.VMEM((KEYS, LANES), f32),
+            pltpu.SemaphoreType.DMA((3,)),
         ],
         compiler_params=params(MIDDLE_VMEM),
         name="attend",
-    )(received, away)
+    )(received, away, *saved)
     answer = pl.pallas_call(
         join_kernel,
         out_shape=jax.ShapeDtypeStruct(chip_shape, bf16),
@@ -461,12 +479,11 @@
             jax.ShapeDtypeStruct((TOK, HALF), f32),
             jax.ShapeDtypeStruct((TOK + OWN, HALF), f32),
         ),
-        in_specs=[vmem()] * 8 + [anywhere()],
+        in_specs=[vmem()] * 9,
         out_specs=(vmem(), vmem(), vmem()),
-        scratch_shapes=[pltpu.VMEM((D, D), bf16), pltpu.SemaphoreType.DMA],
         compiler_params=params(LAST_VMEM),
         name="gradients",
-    )(returned, assign, query_pairs, own_pairs, own_sides, w_query, w_key, w_value, w_out)
+    )(returned, assign, *saved, w_query, w_key, w_value, w_out)
     half_shape = jax.ShapeDtypeStruct((1, TOK, HALF), bf16)
     return pl.pallas_call(
         finish_kernel,

time: 113 us -> 112 us (level)
  Pallas kernels: 27.1 us -> 25.6 us
    pallas_call x1, Pallas kernels: 6.28 us -> 4.76 us  [shards(): pl.pallas_call(post_kernel, out_shape=(jax.ShapeDtypeStruct((OWN, HALF),...]
where the time goes in v5:
time: 112 us
  blocking collectives  75.1 us (67%)
  Pallas kernels  25.6 us (23%)
  starting transfers between devices  5.49 us (5%)
  waiting for transfers between devices  4.42 us (4%)
    all_to_all x1, blocking collectives, shards(): lax.all_to_all(message.reshape(chip_shape), 'tm', 0, 0, tiled=True)  42.6 us
    all_to_all x1, blocking collectives, shards(): lax.all_to_all(answer, 'tm', 0, 0, tiled=True).reshape(message_shape)  32.5 us
    pallas_call x1, Pallas kernels, shards(): pl.pallas_call(attend_kernel, out_shape=(jax.ShapeDtypeStruct(tail_shape,...  11.6 us
    pallas_call x1, Pallas kernels, shards(): pl.pallas_call(pre_kernel, out_shape=(jax.ShapeDtypeStruct(message_shape,...  7.77 us
    ppermute x3, starting transfers between devices, swap_cores(): return lax.ppermute(x, 'head', [(0, 1), (1, 0)])  5.49 us
    pallas_call x1, Pallas kernels, shards(): pl.pallas_call(post_kernel, out_shape=(jax.ShapeDtypeStruct((OWN, HALF),...  4.76 us
    ppermute x3, waiting for transfers between devices, swap_cores(): return lax.ppermute(x, 'head', [(0, 1), (1, 0)])  4.42 us
  transfers between devices with their start and end apart: 3, of which 3 were waited for; matrix products, arithmetic and copies ran while one was open for 0% of the time, Pallas kernels for 0%

profile of v5, /device:TPU:1, one launch (start us, length us, event | category | flops | bytes accessed | tf_op | source)
XLA Modules:
  0.0 111.7 jit_solution(7484210327625765944)
XLA Ops:
  0.6 7.8 %project.1 = (bf16[8,16,13,2,128]{4,3,2,1,0:T(2,128)(2,1)}, bf16[16,64,128]{2,1,0:T(8,128)(2,1)}, bf16[16,128,128]{2,1,0:T(8,128)(2,1)}, f32[16,64,128]{2,1,0:T(8,128)}) custom-call(bf16[128,1024]{1,0:T(8,128)(2,1)} %bitcast.6, s32[1,128]{1,0:T(1,128)} %asg_ref.1, bf16[128,1024]{1,0:T(8,128)(2,1)} %bitcast.7, bf16[1024,1024]{1,0:T(8,128)(2,1)} %wq.1, ...), custom_call_target="tpu_custom_call" | custom-call | tf_op jit(solution)/shard_map/project/pallas_call | solution.py:411
  8.4 0.0 copy-start.4
  8.4 0.0 copy-start.5
  8.4 0.0 copy-start.6
  8.4 0.0 copy-start.3
  8.4 42.6 %all_to_all.10.msg_ref = bf16[128,13,2,128]{3,2,1,0:T(2,128)(2,1)S(1)} all-to-all(bf16[128,13,2,128]{3,2,1,0:T(2,128)(2,1)} %bitcast.5), channel_id=1, replica_groups=mesh['tm'=128,'head'=2] {'tm'}, dimensions={0} | all-to-all | bytes 1703936 | tf_op jit(solution)/shard_map/all_to_all | solution.py:438
  51.0 0.4 slice.4
  51.4 2.9 %collective-permute-start = (bf16[128,8,2,128]{3,2,1,0:T(2,128)(2,1)S(1)}, bf16[128,8,2,128]{3,2,1,0:T(2,128)(2,1)S(1)}, u32[]{:S(2)}, u32[]{:S(2)}) collective-permute-start(bf16[128,8,2,128]{3,2,1,0:T(2,128)(2,1)S(1)} %slice.4), channel_id=1, source_target_pairs={{0,1},{1,0},{2,3},{3,2},{4,5},{5,4},{6,7},{7,6},{8,9},{9,8},{10,11... | collective-permute-start | bytes 1572872 | tf_op jit(solution)/shard_map/ppermute | solution.py:405
  54.4 1.5 %collective-permute-done.away_ref = bf16[128,8,2,128]{3,2,1,0:T(2,128)(2,1)S(1)} collective-permute-done((bf16[128,8,2,128]{3,2,1,0:T(2,128)(2,1)S(1)}, bf16[128,8,2,128]{3,2,1,0:T(2,128)(2,1)S(1)}, u32[]{:S(2)}, u32[]{:S(2)}) %collective-permute-start) | collective-permute-done | bytes 524320 | tf_op jit(solution)/shard_map/ppermute | solution.py:405
  55.9 0.0 copy-done.4
  55.9 0.0 copy-done.5
  55.9 0.0 copy-done.6
  55.9 0.0 copy-start.2
  55.9 11.6 %attend.1 = (bf16[128,5,2,128]{3,2,1,0:T(2,128)(2,1)S(1)}, f32[2048,128]{1,0:T(8,128)S(1)}, bf16[128,8,2,128]{3,2,1,0:T(2,128)(2,1)S(1)}, bf16[16,64,128]{2,1,0:...) custom-call(bf16[128,13,2,128]{3,2,1,0:T(2,128)(2,1)S(1)} %all_to_all.10.msg_ref, ...), custom_call_target="tpu_custom_call" | custom-call | tf_op jit(solution)/shard_map/attend/pallas_call | solution.py:444
  67.5 0.7 collective-permute-start.1
  68.2 1.5 %collective-permute-done.1.other_ref = bf16[128,8,2,128]{3,2,1,0:T(2,128)(2,1)S(1)} collective-permute-done((bf16[128,8,2,128]{3,2,1,0:T(2,128)(2,1)S(1)}, bf16[128,8,2,128]{3,2,1,0:T(2,128)(2,1)S(1)}, u32[]{:S(2)}, u32[]{:S(2)}) %collective-permute-start.1) | collective-permute-done | bytes 524320 | tf_op jit(solution)/shard_map/ppermute | solution.py:405
  69.7 0.0 copy-start
  69.7 0.0 copy-start.1
  69.8 0.0 copy-start.7
  69.8 0.7 join.1
  70.4 32.5 %all_to_all.11 = bf16[128,13,2,128]{3,2,1,0:T(2,128)(2,1)S(1)} all-to-all(bf16[128,13,2,128]{3,2,1,0:T(2,128)(2,1)S(1)} %join.1), channel_id=1, replica_groups=mesh['tm'=128,'head'=2] {'tm'}, dimensions={0} | all-to-all | bytes 1703936 | tf_op jit(solution)/shard_map/all_to_all | solution.py:473
  103.0 0.0 copy-done.3
  103.0 0.0 copy-done.2
  103.0 0.0 copy-done
  103.0 0.0 copy-done.1
  103.0 0.0 copy-done.7
  103.0 4.8 %gradients.1 = (f32[64,512]{1,0:T(8,128)S(1)}, f32[128,512]{1,0:T(8,128)S(1)}, f32[192,512]{1,0:T(8,128)S(1)}) custom-call(bf16[8,16,13,2,128]{4,3,2,1,0:T(2,128)(2,1)S(1)} %bitcast.4, s32[1,128]{1,0:T(1,128)S(1)} %copy-done.7, bf16[16,64,128]{2,1,0:T(8,128)(2,1)S(1)} %get-tuple-element.22.qd_ref, bf16[16,128,128]{2,1,0:T(8,128)(2,1)S(1)} %get-tuple-element.23.kv_ref, ...), custom_call_target="tpu_custom_call" | custom-call | tf_op jit(solution)/shard_map/gradients/pallas_call | solution.py:475
  107.8 1.9 %collective-permute-start.2 = (f32[192,512]{1,0:T(8,128)S(1)}, f32[192,512]{1,0:T(8,128)S(1)}, u32[]{:S(2)}, u32[]{:S(2)}) collective-permute-start(f32[192,512]{1,0:T(8,128)S(1)} %get-tuple-element.27), channel_id=1, source_target_pairs={{0,1},{1,0},{2,3},{3,2},{4,5},{5,4},{6,7},{7,6},{8,9},{9,8},{10,11... | collective-permute-start | bytes 1179656 | tf_op jit(solution)/shard_map/ppermute | solution.py:405
  109.6 1.3 %collective-permute-done.2.arrived_ref = f32[192,512]{1,0:T(8,128)S(1)} collective-permute-done((f32[192,512]{1,0:T(8,128)S(1)}, f32[192,512]{1,0:T(8,128)S(1)}, u32[]{:S(2)}, u32[]{:S(2)}) %collective-permute-start.2) | collective-permute-done | bytes 393248 | tf_op jit(solution)/shard_map/ppermute | solution.py:405
  111.0 0.7 finish.1
Async XLA Ops:
  8.4 47.5 %copy-start.4 = (bf16[16,128,128]{2,1,0:T(8,128)(2,1)S(1)}, bf16[16,128,128]{2,1,0:T(8,128)(2,1)}, u32[]{:S(2)}) copy-start(bf16[16,128,128]{2,1,0:T(8,128)(2,1)} %get-tuple-element.17.own_hbm) | copy-start | bytes 1572868
  8.4 47.5 %copy-start.5 = (f32[16,64,128]{2,1,0:T(8,128)S(1)}, f32[16,64,128]{2,1,0:T(8,128)}, u32[]{:S(2)}) copy-start(f32[16,64,128]{2,1,0:T(8,128)} %get-tuple-element.18.side_hbm) | copy-start | bytes 1572868
  8.4 47.5 %copy-start.6 = (bf16[16,64,128]{2,1,0:T(8,128)(2,1)S(1)}, bf16[16,64,128]{2,1,0:T(8,128)(2,1)}, u32[]{:S(2)}) copy-start(bf16[16,64,128]{2,1,0:T(8,128)(2,1)} %get-tuple-element.16.qd_hbm) | copy-start | bytes 786436
  8.4 94.5 %copy-start.3 = (bf16[1024,1024]{1,0:T(8,128)(2,1)S(1)}, bf16[1024,1024]{1,0:T(8,128)(2,1)}, u32[]{:S(2)}) copy-start(bf16[1024,1024]{1,0:T(8,128)(2,1)} %wo.1) | copy-start | bytes 6291460
  51.4 4.5 %collective-permute-start = (bf16[128,8,2,128]{3,2,1,0:T(2,128)(2,1)S(1)}, bf16[128,8,2,128]{3,2,1,0:T(2,128)(2,1)S(1)}, u32[]{:S(2)}, u32[]{:S(2)}) collective-permute-start(bf16[128,8,2,128]{3,2,1,0:T(2,128)(2,1)S(1)} %slice.4), channel_id=1, source_target_pairs={{0,1},{1,0},{2,3},{3,2},{4,5},{5,4},{6,7},{7,6},{8,9},{9,8},{10,11... | collective-permute-start | bytes 1572872 | tf_op jit(solution)/shard_map/ppermute | solution.py:405
  55.9 47.1 %copy-start.2 = (bf16[1024,1024]{1,0:T(8,128)(2,1)S(1)}, bf16[1024,1024]{1,0:T(8,128)(2,1)}, u32[]{:S(2)}) copy-start(bf16[1024,1024]{1,0:T(8,128)(2,1)} %wv.1) | copy-start | bytes 6291460
  67.5 2.2 %collective-permute-start.1 = (bf16[128,8,2,128]{3,2,1,0:T(2,128)(2,1)S(1)}, bf16[128,8,2,128]{3,2,1,0:T(2,128)(2,1)S(1)}, u32[]{:S(2)}, u32[]{:S(2)}) collective-permute-start(bf16[128,8,2,128]{3,2,1,0:T(2,128)(2,1)S(1)} %get-tuple-element.20), channel_id=1, source_target_pairs={{0,1},{1,0},{2,3},{3,2},{4,5},{5,4},{6,7},{7,6},{8,9},{9,8},{10,11... | collective-permute-start | bytes 1572872 | tf_op jit(solution)/shard_map/ppermute | solution.py:405
  69.7 33.2 %copy-start = (bf16[1024,1024]{1,0:T(8,128)(2,1)S(1)}, bf16[1024,1024]{1,0:T(8,128)(2,1)}, u32[]{:S(2)}) copy-start(bf16[1024,1024]{1,0:T(8,128)(2,1)} %wq.1) | copy-start | bytes 6291460
  69.7 33.2 %copy-start.1 = (bf16[1024,1024]{1,0:T(8,128)(2,1)S(1)}, bf16[1024,1024]{1,0:T(8,128)(2,1)}, u32[]{:S(2)}) copy-start(bf16[1024,1024]{1,0:T(8,128)(2,1)} %wk.1) | copy-start | bytes 6291460
  69.8 33.3 %copy-start.7 = (s32[1,128]{1,0:T(1,128)S(1)}, s32[1,128]{1,0:T(1,128)}, u32[]{:S(2)}) copy-start(s32[1,128]{1,0:T(1,128)} %asg_ref.1) | copy-start | bytes 1540
  107.8 3.2 %collective-permute-start.2 = (f32[192,512]{1,0:T(8,128)S(1)}, f32[192,512]{1,0:T(8,128)S(1)}, u32[]{:S(2)}, u32[]{:S(2)}) collective-permute-start(f32[192,512]{1,0:T(8,128)S(1)} %get-tuple-element.27), channel_id=1, source_target_pairs={{0,1},{1,0},{2,3},{3,2},{4,5},{5,4},{6,7},{7,6},{8,9},{9,8},{10,11... | collective-permute-start | bytes 1179656 | tf_op jit(solution)/shard_map/ppermute | solution.py:405

commit v6 on v5

--- a/solution.py
+++ b/solution.py
@@ -149,12 +149,11 @@
         row_sum = [jnp.sum(x, axis=1, keepdims=True) for x in raised]
         sides = [dot((x / t).astype(bf16), kv_ref[head]) for head, x, t in zip(group, raised, row_sum)]
         for head, query_pair, top, total, side in zip(group, query_pairs, row_max, row_sum, sides):
-            log_sum = top + jnp.log(total)
             products = jnp.where(low, 0.0, query_pair.astype(f32) * side)
             delta = jnp.sum(products, axis=1, keepdims=True)
-            side_ref[head] = jnp.where(low, log_sum, side)
+            side_ref[head] = jnp.where(lane == 0, top, jnp.where(low, total, side))
             stats = jnp.zeros((OWN, LANES), f32)
-            for at, part in enumerate(three_parts(log_sum) + three_parts(delta)):
+            for at, part in enumerate(three_parts(top) + three_parts(total) + three_parts(delta)):
                 stats = jnp.where(lane // QROWS == at, part, stats)
             stats = jnp.where(lane % QROWS == sublane % QROWS, stats, 0.0)
             stats = jnp.sum(stats.reshape(SPLITS, QROWS, LANES), axis=1, keepdims=True)
@@ -203,13 +202,18 @@
     square_column = lax.broadcasted_iota(jnp.int32, (LANES, LANES), 1)
     same_query = square_row % QROWS == square_column % QROWS
     gather = (
-        lax.broadcasted_iota(jnp.int32, (8, LANES), 0) == lax.broadcasted_iota(jnp.int32, (8, LANES), 1) // QROWS
+        lax.broadcasted_iota(jnp.int32, (16, LANES), 0) == lax.broadcasted_iota(jnp.int32, (16, LANES), 1) // QROWS
     ).astype(bf16)
     blocks = range(NBLOCKS)
     stats = [dot_tn(spread, msg_ref[segs(i), STATS_AT].reshape(2 * BLOCK_SEGS, LANES)) for i in blocks]
     stats = [dot_nt(gather, jnp.where(same_query, x, 0.0).astype(bf16)) for x in stats]
     state = [
-        {"own_log": x[0:1] + x[1:2] + x[2:3], "own_delta": x[3:4] + x[4:5] + x[5:6]} for x in stats
+        {
+            "own_max": x[0:1] + x[1:2] + x[2:3],
+            "own_sum": x[3:4] + x[4:5] + x[5:6],
+            "own_delta": x[6:7] + x[7:8] + x[8:9],
+        }
+        for x in stats
     ]
 
     def score_stage(i):
@@ -230,7 +234,7 @@
             dprobs[buf, block(j), :] = both[:, QBLOCK:]
             top = jnp.maximum(top, fold(jnp.max, score))
             yield
-        mine["row_max"] = jnp.maximum(jnp.max(top, axis=0, keepdims=True), mine["own_log"])
+        mine["row_max"] = jnp.maximum(jnp.max(top, axis=0, keepdims=True), mine["own_max"])
 
     def middle_stage(i):
         mine = state[i] if i < NBLOCKS else None
@@ -265,11 +269,11 @@
                 grad = grad + product[:, -QBLOCK:]
             yield
         if mine is not None:
-            own_share = jnp.exp(mine["own_log"] - mine["row_max"])
+            own_share = mine["own_sum"] * jnp.exp(mine["own_max"] - mine["row_max"])
             row_sum = own_share + jnp.sum(total, axis=0, keepdims=True)
             inverse = 1.0 / row_sum
             out = out[HEAD_DIM:] * inverse
-            mine.update(log_sum=mine["row_max"] + jnp.log(row_sum), inverse=inverse, out=out)
+            mine.update(row_sum=row_sum, inverse=inverse, out=out)
             mine["delta"] = (
                 jnp.sum(mine["grad_t"] * out, axis=0, keepdims=True) + own_share * inverse * mine["own_delta"]
             )
@@ -289,8 +293,9 @@
                     running.remove(one)
 
     stats = [jnp.zeros((LANES, LANES), f32) for _ in blocks]
-    for at in range(3):
-        parts = [three_parts(one["log_sum"])[at] for one in state]
+    sent = [three_parts(one["row_max"]) + three_parts(one["row_sum"]) for one in state]
+    for at in range(6):
+        parts = [one[at] for one in sent]
         stats = [jnp.where(square_row // QROWS == at, part, x) for part, x in zip(parts, stats)]
     stats = [dot_nt(spread, jnp.where(same_query, x, 0.0).astype(bf16)) for x in stats]
     for i in blocks:
@@ -330,17 +335,25 @@
     lane = lax.broadcasted_iota(jnp.int32, (OWN, LANES), 1)
     same_query = sublane % QROWS == lane % QROWS
 
-    def log_sum_of(head):
+    part = lax.broadcasted_iota(jnp.int32, (LANES, 2 * LANES), 0) // QROWS
+    wanted = lax.broadcasted_iota(jnp.int32, (LANES, 2 * LANES), 1) // LANES
+    pick = (part // 3 == wanted).astype(bf16)
+
+    def stats_of(head):
         stats = msg_ref[:, head, STATS_AT].astype(f32)[:, :1]
         stats = jnp.broadcast_to(stats, (SPLITS, QROWS, LANES)).reshape(OWN, LANES)
-        return jnp.sum(jnp.where(same_query, stats, 0.0), axis=1, keepdims=True)
-
-    log_sums = [log_sum_of(head) for head in heads]
-    shares = [jnp.exp(side_ref[head][:, :1] - log_sums[head]) for head in heads]
+        return dot(jnp.where(same_query, stats, 0.0).astype(bf16), pick)
+
+    stats = [stats_of(head) for head in heads]
+    row_max = [x[:, :LANES] for x in stats]
+    inverse = [1.0 / x[:, LANES:] for x in stats]
+    shares = [
+        side_ref[head][:, 1:2] * jnp.exp(side_ref[head][:, :1] - row_max[head]) * inverse[head] for head in heads
+    ]
     mains = [(returned[head] + shares[head] * side_ref[head]).astype(bf16).astype(f32) for head in heads]
     products = [qd_ref[head].astype(f32) * mains[head] for head in heads]
     deltas = [jnp.sum(jnp.where(low_lanes(x.shape), 0.0, x), axis=1, keepdims=True) for x in products]
-    probs = [jnp.exp(both[head][:OWN] - log_sums[head]) for head in heads]
+    probs = [jnp.exp(both[head][:OWN] - row_max[head]) * inverse[head] for head in heads]
     dscores = [(probs[head] * (both[head][OWN:] - deltas[head])).astype(bf16) for head in heads]
     own_grads = [dot(dscores[head], kv_ref[head]) for head in heads]
     own_pairs = [

time: 112 us -> 112 us (level)
  no operation moved by 1% of the time
where the time goes in v6:
time: 112 us
  blocking collectives  75.1 us (67%)
  Pallas kernels  26 us (23%)
  starting transfers between devices  5.5 us (5%)
  waiting for transfers between devices  4.42 us (4%)
    all_to_all x1, blocking collectives, shards(): lax.all_to_all(message.reshape(chip_shape), 'tm', 0, 0, tiled=True)  42.6 us
    all_to_all x1, blocking collectives, shards(): lax.all_to_all(answer, 'tm', 0, 0, tiled=True).reshape(message_shape)  32.5 us
    pallas_call x1, Pallas kernels, shards(): pl.pallas_call(attend_kernel, out_shape=(jax.ShapeDtypeStruct(tail_shape,...  11.6 us
    pallas_call x1, Pallas kernels, shards(): pl.pallas_call(pre_kernel, out_shape=(jax.ShapeDtypeStruct(message_shape,...  7.84 us
    ppermute x3, starting transfers between devices, swap_cores(): return lax.ppermute(x, 'head', [(0, 1), (1, 0)])  5.5 us
    pallas_call x1, Pallas kernels, shards(): pl.pallas_call(post_kernel, out_shape=(jax.ShapeDtypeStruct((OWN, HALF),...  5.09 us
    ppermute x3, waiting for transfers between devices, swap_cores(): return lax.ppermute(x, 'head', [(0, 1), (1, 0)])  4.42 us
  transfers between devices with their start and end apart: 3, of which 3 were waited for; matrix products, arithmetic and copies ran while one was open for 0% of the time, Pallas kernels for 0%

profile of v6, /device:TPU:1, one launch (start us, length us, event | category | flops | bytes accessed | tf_op | source)
XLA Modules:
  0.0 112.2 jit_solution(578675216292007275)
XLA Ops:
  0.6 7.8 %project.1 = (bf16[8,16,13,2,128]{4,3,2,1,0:T(2,128)(2,1)}, bf16[16,64,128]{2,1,0:T(8,128)(2,1)}, bf16[16,128,128]{2,1,0:T(8,128)(2,1)}, f32[16,64,128]{2,1,0:T(8,128)}) custom-call(bf16[128,1024]{1,0:T(8,128)(2,1)} %bitcast.6, s32[1,128]{1,0:T(1,128)} %asg_ref.1, bf16[128,1024]{1,0:T(8,128)(2,1)} %bitcast.7, bf16[1024,1024]{1,0:T(8,128)(2,1)} %wq.1, ...), custom_call_target="tpu_custom_call" | custom-call | tf_op jit(solution)/shard_map/project/pallas_call | solution.py:424
  8.5 0.0 copy-start.4
  8.5 0.0 copy-start.5
  8.5 0.0 copy-start.6
  8.5 0.0 copy-start.3
  8.5 42.6 %all_to_all.10.msg_ref = bf16[128,13,2,128]{3,2,1,0:T(2,128)(2,1)S(1)} all-to-all(bf16[128,13,2,128]{3,2,1,0:T(2,128)(2,1)} %bitcast.5), channel_id=1, replica_groups=mesh['tm'=128,'head'=2] {'tm'}, dimensions={0} | all-to-all | bytes 1703936 | tf_op jit(solution)/shard_map/all_to_all | solution.py:451
  51.1 0.4 slice.4
  51.5 2.9 %collective-permute-start = (bf16[128,8,2,128]{3,2,1,0:T(2,128)(2,1)S(1)}, bf16[128,8,2,128]{3,2,1,0:T(2,128)(2,1)S(1)}, u32[]{:S(2)}, u32[]{:S(2)}) collective-permute-start(bf16[128,8,2,128]{3,2,1,0:T(2,128)(2,1)S(1)} %slice.4), channel_id=1, source_target_pairs={{0,1},{1,0},{2,3},{3,2},{4,5},{5,4},{6,7},{7,6},{8,9},{9,8},{10,11... | collective-permute-start | bytes 1572872 | tf_op jit(solution)/shard_map/ppermute | solution.py:418
  54.4 1.5 %collective-permute-done.away_ref = bf16[128,8,2,128]{3,2,1,0:T(2,128)(2,1)S(1)} collective-permute-done((bf16[128,8,2,128]{3,2,1,0:T(2,128)(2,1)S(1)}, bf16[128,8,2,128]{3,2,1,0:T(2,128)(2,1)S(1)}, u32[]{:S(2)}, u32[]{:S(2)}) %collective-permute-start) | collective-permute-done | bytes 524320 | tf_op jit(solution)/shard_map/ppermute | solution.py:418
  56.0 0.0 copy-done.4
  56.0 0.0 copy-done.5
  56.0 0.0 copy-done.6
  56.0 0.0 copy-start.2
  56.0 11.6 %attend.1 = (bf16[128,5,2,128]{3,2,1,0:T(2,128)(2,1)S(1)}, f32[2048,128]{1,0:T(8,128)S(1)}, bf16[128,8,2,128]{3,2,1,0:T(2,128)(2,1)S(1)}, bf16[16,64,128]{2,1,0:...) custom-call(bf16[128,13,2,128]{3,2,1,0:T(2,128)(2,1)S(1)} %all_to_all.10.msg_ref, ...), custom_call_target="tpu_custom_call" | custom-call | tf_op jit(solution)/shard_map/attend/pallas_call | solution.py:457
  67.6 0.7 collective-permute-start.1
  68.3 1.5 %collective-permute-done.1.other_ref = bf16[128,8,2,128]{3,2,1,0:T(2,128)(2,1)S(1)} collective-permute-done((bf16[128,8,2,128]{3,2,1,0:T(2,128)(2,1)S(1)}, bf16[128,8,2,128]{3,2,1,0:T(2,128)(2,1)S(1)}, u32[]{:S(2)}, u32[]{:S(2)}) %collective-permute-start.1) | collective-permute-done | bytes 524320 | tf_op jit(solution)/shard_map/ppermute | solution.py:418
  69.8 0.0 copy-start
  69.9 0.0 copy-start.1
  69.9 0.0 copy-start.7
  69.9 0.7 join.1
  70.5 32.5 %all_to_all.11 = bf16[128,13,2,128]{3,2,1,0:T(2,128)(2,1)S(1)} all-to-all(bf16[128,13,2,128]{3,2,1,0:T(2,128)(2,1)S(1)} %join.1), channel_id=1, replica_groups=mesh['tm'=128,'head'=2] {'tm'}, dimensions={0} | all-to-all | bytes 1703936 | tf_op jit(solution)/shard_map/all_to_all | solution.py:486
  103.1 0.0 copy-done.3
  103.1 0.0 copy-done.2
  103.1 0.0 copy-done
  103.1 0.0 copy-done.1
  103.1 0.0 copy-done.7
  103.1 5.1 %gradients.1 = (f32[64,512]{1,0:T(8,128)S(1)}, f32[128,512]{1,0:T(8,128)S(1)}, f32[192,512]{1,0:T(8,128)S(1)}) custom-call(bf16[8,16,13,2,128]{4,3,2,1,0:T(2,128)(2,1)S(1)} %bitcast.4, s32[1,128]{1,0:T(1,128)S(1)} %copy-done.7, bf16[16,64,128]{2,1,0:T(8,128)(2,1)S(1)} %get-tuple-element.22.qd_ref, bf16[16,128,128]{2,1,0:T(8,128)(2,1)S(1)} %get-tuple-element.23.kv_ref, ...), custom_call_target="tpu_custom_call" | custom-call | tf_op jit(solution)/shard_map/gradients/pallas_call | solution.py:488
  108.2 1.9 %collective-permute-start.2 = (f32[192,512]{1,0:T(8,128)S(1)}, f32[192,512]{1,0:T(8,128)S(1)}, u32[]{:S(2)}, u32[]{:S(2)}) collective-permute-start(f32[192,512]{1,0:T(8,128)S(1)} %get-tuple-element.27), channel_id=1, source_target_pairs={{0,1},{1,0},{2,3},{3,2},{4,5},{5,4},{6,7},{7,6},{8,9},{9,8},{10,11... | collective-permute-start | bytes 1179656 | tf_op jit(solution)/shard_map/ppermute | solution.py:418
  110.1 1.3 %collective-permute-done.2.arrived_ref = f32[192,512]{1,0:T(8,128)S(1)} collective-permute-done((f32[192,512]{1,0:T(8,128)S(1)}, f32[192,512]{1,0:T(8,128)S(1)}, u32[]{:S(2)}, u32[]{:S(2)}) %collective-permute-start.2) | collective-permute-done | bytes 393248 | tf_op jit(solution)/shard_map/ppermute | solution.py:418
  111.4 0.7 finish.1
Async XLA Ops:
  8.5 47.5 %copy-start.4 = (bf16[16,128,128]{2,1,0:T(8,128)(2,1)S(1)}, bf16[16,128,128]{2,1,0:T(8,128)(2,1)}, u32[]{:S(2)}) copy-start(bf16[16,128,128]{2,1,0:T(8,128)(2,1)} %get-tuple-element.17.own_hbm) | copy-start | bytes 1572868
  8.5 47.5 %copy-start.5 = (f32[16,64,128]{2,1,0:T(8,128)S(1)}, f32[16,64,128]{2,1,0:T(8,128)}, u32[]{:S(2)}) copy-start(f32[16,64,128]{2,1,0:T(8,128)} %get-tuple-element.18.side_hbm) | copy-start | bytes 1572868
  8.5 47.5 %copy-start.6 = (bf16[16,64,128]{2,1,0:T(8,128)(2,1)S(1)}, bf16[16,64,128]{2,1,0:T(8,128)(2,1)}, u32[]{:S(2)}) copy-start(bf16[16,64,128]{2,1,0:T(8,128)(2,1)} %get-tuple-element.16.qd_hbm) | copy-start | bytes 786436
  8.5 94.6 %copy-start.3 = (bf16[1024,1024]{1,0:T(8,128)(2,1)S(1)}, bf16[1024,1024]{1,0:T(8,128)(2,1)}, u32[]{:S(2)}) copy-start(bf16[1024,1024]{1,0:T(8,128)(2,1)} %wo.1) | copy-start | bytes 6291460
  51.5 4.5 %collective-permute-start = (bf16[128,8,2,128]{3,2,1,0:T(2,128)(2,1)S(1)}, bf16[128,8,2,128]{3,2,1,0:T(2,128)(2,1)S(1)}, u32[]{:S(2)}, u32[]{:S(2)}) collective-permute-start(bf16[128,8,2,128]{3,2,1,0:T(2,128)(2,1)S(1)} %slice.4), channel_id=1, source_target_pairs={{0,1},{1,0},{2,3},{3,2},{4,5},{5,4},{6,7},{7,6},{8,9},{9,8},{10,11... | collective-permute-start | bytes 1572872 | tf_op jit(solution)/shard_map/ppermute | solution.py:418
  56.0 47.1 %copy-start.2 = (bf16[1024,1024]{1,0:T(8,128)(2,1)S(1)}, bf16[1024,1024]{1,0:T(8,128)(2,1)}, u32[]{:S(2)}) copy-start(bf16[1024,1024]{1,0:T(8,128)(2,1)} %wv.1) | copy-start | bytes 6291460
  67.6 2.2 %collective-permute-start.1 = (bf16[128,8,2,128]{3,2,1,0:T(2,128)(2,1)S(1)}, bf16[128,8,2,128]{3,2,1,0:T(2,128)(2,1)S(1)}, u32[]{:S(2)}, u32[]{:S(2)}) collective-permute-start(bf16[128,8,2,128]{3,2,1,0:T(2,128)(2,1)S(1)} %get-tuple-element.20), channel_id=1, source_target_pairs={{0,1},{1,0},{2,3},{3,2},{4,5},{5,4},{6,7},{7,6},{8,9},{9,8},{10,11... | collective-permute-start | bytes 1572872 | tf_op jit(solution)/shard_map/ppermute | solution.py:418
  69.8 33.2 %copy-start = (bf16[1024,1024]{1,0:T(8,128)(2,1)S(1)}, bf16[1024,1024]{1,0:T(8,128)(2,1)}, u32[]{:S(2)}) copy-start(bf16[1024,1024]{1,0:T(8,128)(2,1)} %wq.1) | copy-start | bytes 6291460
  69.9 33.2 %copy-start.1 = (bf16[1024,1024]{1,0:T(8,128)(2,1)S(1)}, bf16[1024,1024]{1,0:T(8,128)(2,1)}, u32[]{:S(2)}) copy-start(bf16[1024,1024]{1,0:T(8,128)(2,1)} %wk.1) | copy-start | bytes 6291460
  69.9 33.3 %copy-start.7 = (s32[1,128]{1,0:T(1,128)S(1)}, s32[1,128]{1,0:T(1,128)}, u32[]{:S(2)}) copy-start(s32[1,128]{1,0:T(1,128)} %asg_ref.1) | copy-start | bytes 1540
  108.2 3.2 %collective-permute-start.2 = (f32[192,512]{1,0:T(8,128)S(1)}, f32[192,512]{1,0:T(8,128)S(1)}, u32[]{:S(2)}, u32[]{:S(2)}) collective-permute-start(f32[192,512]{1,0:T(8,128)S(1)} %get-tuple-element.27), channel_id=1, source_target_pairs={{0,1},{1,0},{2,3},{3,2},{4,5},{5,4},{6,7},{7,6},{8,9},{9,8},{10,11... | collective-permute-start | bytes 1179656 | tf_op jit(solution)/shard_map/ppermute | solution.py:418

commit v7 on v6

--- a/solution.py
+++ b/solution.py
@@ -314,7 +314,7 @@
 
 
 def post_kernel(
-    msg_ref, asg_ref, qd_ref, kv_ref, side_ref, wq, wk, wv, wo, out_ref, mine_ref, other_ref,
+    msg_ref, asg_ref, qd_ref, kv_ref, side_ref, wq, wk, wv, wo, out_ref, mine_ref, other_ref, far,
 ):
     half = lax.axis_index("head")
     offset = pl.multiple_of(half * HALF, HALF)
@@ -378,14 +378,14 @@
         total = dot_nt(key_grads, wk[rows, :]) + dot_nt(value_grads, wv[rows, :])
         high, middle, low = three_parts(total[TOK:] / counts)
         spread = dot_tn(onehot, high.astype(bf16)) + dot_tn(onehot, middle.astype(bf16)) + dot_tn(onehot, low.astype(bf16))
-        grad_rows = pl.ds(0, TOK)
         if keep:
             mine_ref[...] = total[:TOK] + spread
             mine_ref[own_rows, :] += dot_nt(query_grads, wq[rows, :])
         else:
-            other_ref[grad_rows, :] = total[:TOK] + spread
-            other_ref[own_rows, :] += dot_nt(query_grads, wq[rows, :])
-    other_ref[TOK:, :] = dot(heads_out, wo[:, pl.ds(away, HALF)])
+            far[...] = total[:TOK] + spread
+            far[own_rows, :] += dot_nt(query_grads, wq[rows, :])
+    other_ref[:TOK, :] = far[...].astype(bf16)
+    other_ref[TOK:, :] = dot(heads_out, wo[:, pl.ds(away, HALF)]).astype(bf16)
     out_ref[...] = dot(heads_out, wo[:, pl.ds(offset, HALF)])
 
 
@@ -394,8 +394,8 @@
     own_rows = pl.ds(pl.multiple_of(half * OWN, OWN), OWN)
     far_rows = pl.ds(pl.multiple_of((1 - half) * OWN, OWN), OWN)
     out_ref[0, own_rows, :] = attended_ref[...].astype(bf16)
-    out_ref[0, far_rows, :] = arrived_ref[TOK:, :].astype(bf16)
-    grad_ref[0] = (mine_ref[...] + arrived_ref[:TOK, :]).astype(bf16)
+    out_ref[0, far_rows, :] = arrived_ref[TOK:, :]
+    grad_ref[0] = (mine_ref[...] + arrived_ref[:TOK, :].astype(f32)).astype(bf16)
 
 
 def params(vmem_bytes):
@@ -490,10 +490,11 @@
         out_shape=(
             jax.ShapeDtypeStruct((OWN, HALF), f32),
             jax.ShapeDtypeStruct((TOK, HALF), f32),
-            jax.ShapeDtypeStruct((TOK + OWN, HALF), f32),
+            jax.ShapeDtypeStruct((TOK + OWN, HALF), bf16),
         ),
         in_specs=[vmem()] * 9,
         out_specs=(vmem(), vmem(), vmem()),
+        scratch_shapes=[pltpu.VMEM((TOK, HALF), f32)],
         compiler_params=params(LAST_VMEM),
         name="gradients",
     )(returned, assign, *saved, w_query, w_key, w_value, w_out)

time: 112 us -> 112 us (level)
  no operation moved by 1% of the time
where the time goes in v7:
time: 112 us
  blocking collectives  75.1 us (67%)
  Pallas kernels  26 us (23%)
  starting transfers between devices  5.5 us (5%)
  waiting for transfers between devices  4.14 us (4%)
    all_to_all x1, blocking collectives, shards(): lax.all_to_all(message.reshape(chip_shape), 'tm', 0, 0, tiled=True)  42.6 us
    all_to_all x1, blocking collectives, shards(): lax.all_to_all(answer, 'tm', 0, 0, tiled=True).reshape(message_shape)  32.5 us
    pallas_call x1, Pallas kernels, shards(): pl.pallas_call(attend_kernel, out_shape=(jax.ShapeDtypeStruct(tail_shape,...  11.6 us
    pallas_call x1, Pallas kernels, shards(): pl.pallas_call(pre_kernel, out_shape=(jax.ShapeDtypeStruct(message_shape,...  7.84 us
    ppermute x3, starting transfers between devices, swap_cores(): return lax.ppermute(x, 'head', [(0, 1), (1, 0)])  5.5 us
    pallas_call x1, Pallas kernels, shards(): pl.pallas_call(post_kernel, out_shape=(jax.ShapeDtypeStruct((OWN, HALF),...  5.11 us
    ppermute x3, waiting for transfers between devices, swap_cores(): return lax.ppermute(x, 'head', [(0, 1), (1, 0)])  4.14 us
  transfers between devices with their start and end apart: 3, of which 3 were waited for; matrix products, arithmetic and copies ran while one was open for 0% of the time, Pallas kernels for 0%

profile of v7, /device:TPU:1, one launch (start us, length us, event | category | flops | bytes accessed | tf_op | source)
XLA Modules:
  0.0 111.9 jit_solution(7398464720417964190)
XLA Ops:
  0.6 7.8 %project.1 = (bf16[8,16,13,2,128]{4,3,2,1,0:T(2,128)(2,1)}, bf16[16,64,128]{2,1,0:T(8,128)(2,1)}, bf16[16,128,128]{2,1,0:T(8,128)(2,1)}, f32[16,64,128]{2,1,0:T(8,128)}) custom-call(bf16[128,1024]{1,0:T(8,128)(2,1)} %bitcast.6, s32[1,128]{1,0:T(1,128)} %asg_ref.1, bf16[128,1024]{1,0:T(8,128)(2,1)} %bitcast.7, bf16[1024,1024]{1,0:T(8,128)(2,1)} %wq.1, ...), custom_call_target="tpu_custom_call" | custom-call | tf_op jit(solution)/shard_map/project/pallas_call | solution.py:424
  8.5 0.0 copy-start.4
  8.5 0.0 copy-start.5
  8.5 0.0 copy-start.6
  8.5 0.0 copy-start.3
  8.5 42.6 %all_to_all.10.msg_ref = bf16[128,13,2,128]{3,2,1,0:T(2,128)(2,1)S(1)} all-to-all(bf16[128,13,2,128]{3,2,1,0:T(2,128)(2,1)} %bitcast.5), channel_id=1, replica_groups=mesh['tm'=128,'head'=2] {'tm'}, dimensions={0} | all-to-all | bytes 1703936 | tf_op jit(solution)/shard_map/all_to_all | solution.py:451
  51.1 0.4 slice.4
  51.5 2.9 %collective-permute-start = (bf16[128,8,2,128]{3,2,1,0:T(2,128)(2,1)S(1)}, bf16[128,8,2,128]{3,2,1,0:T(2,128)(2,1)S(1)}, u32[]{:S(2)}, u32[]{:S(2)}) collective-permute-start(bf16[128,8,2,128]{3,2,1,0:T(2,128)(2,1)S(1)} %slice.4), channel_id=1, source_target_pairs={{0,1},{1,0},{2,3},{3,2},{4,5},{5,4},{6,7},{7,6},{8,9},{9,8},{10,11... | collective-permute-start | bytes 1572872 | tf_op jit(solution)/shard_map/ppermute | solution.py:418
  54.4 1.5 %collective-permute-done.away_ref = bf16[128,8,2,128]{3,2,1,0:T(2,128)(2,1)S(1)} collective-permute-done((bf16[128,8,2,128]{3,2,1,0:T(2,128)(2,1)S(1)}, bf16[128,8,2,128]{3,2,1,0:T(2,128)(2,1)S(1)}, u32[]{:S(2)}, u32[]{:S(2)}) %collective-permute-start) | collective-permute-done | bytes 524320 | tf_op jit(solution)/shard_map/ppermute | solution.py:418
  56.0 0.0 copy-done.4
  56.0 0.0 copy-done.5
  56.0 0.0 copy-done.6
  56.0 0.0 copy-start.2
  56.0 11.6 %attend.1 = (bf16[128,5,2,128]{3,2,1,0:T(2,128)(2,1)S(1)}, f32[2048,128]{1,0:T(8,128)S(1)}, bf16[128,8,2,128]{3,2,1,0:T(2,128)(2,1)S(1)}, bf16[16,64,128]{2,1,0:...) custom-call(bf16[128,13,2,128]{3,2,1,0:T(2,128)(2,1)S(1)} %all_to_all.10.msg_ref, ...), custom_call_target="tpu_custom_call" | custom-call | tf_op jit(solution)/shard_map/attend/pallas_call | solution.py:457
  67.6 0.7 collective-permute-start.1
  68.3 1.5 %collective-permute-done.1.other_ref = bf16[128,8,2,128]{3,2,1,0:T(2,128)(2,1)S(1)} collective-permute-done((bf16[128,8,2,128]{3,2,1,0:T(2,128)(2,1)S(1)}, bf16[128,8,2,128]{3,2,1,0:T(2,128)(2,1)S(1)}, u32[]{:S(2)}, u32[]{:S(2)}) %collective-permute-start.1) | collective-permute-done | bytes 524320 | tf_op jit(solution)/shard_map/ppermute | solution.py:418
  69.8 0.0 copy-start
  69.9 0.0 copy-start.1
  69.9 0.0 copy-start.7
  69.9 0.7 join.1
  70.5 32.5 %all_to_all.11 = bf16[128,13,2,128]{3,2,1,0:T(2,128)(2,1)S(1)} all-to-all(bf16[128,13,2,128]{3,2,1,0:T(2,128)(2,1)S(1)} %join.1), channel_id=1, replica_groups=mesh['tm'=128,'head'=2] {'tm'}, dimensions={0} | all-to-all | bytes 1703936 | tf_op jit(solution)/shard_map/all_to_all | solution.py:486
  103.1 0.0 copy-done.3
  103.1 0.0 copy-done.2
  103.1 0.0 copy-done
  103.1 0.0 copy-done.1
  103.1 0.0 copy-done.7
  103.1 5.1 %gradients.1 = (f32[64,512]{1,0:T(8,128)S(1)}, f32[128,512]{1,0:T(8,128)S(1)}, bf16[192,512]{1,0:T(8,128)(2,1)S(1)}) custom-call(bf16[8,16,13,2,128]{4,3,2,1,0:T(2,128)(2,1)S(1)} %bitcast.4, s32[1,128]{1,0:T(1,128)S(1)} %copy-done.7, bf16[16,64,128]{2,1,0:T(8,128)(2,1)S(1)} %get-tuple-element.22.qd_ref, bf16[16,128,128]{2,1,0:T(8,128)(2,1)S(1)} %get-tuple-element.23.kv_ref, ...), custom_call_target="tpu_custom_call" | custom-call | tf_op jit(solution)/shard_map/gradients/pallas_call | solution.py:488
  108.2 1.9 %collective-permute-start.2 = (bf16[192,512]{1,0:T(8,128)(2,1)S(1)}, bf16[192,512]{1,0:T(8,128)(2,1)S(1)}, u32[]{:S(2)}, u32[]{:S(2)}) collective-permute-start(bf16[192,512]{1,0:T(8,128)(2,1)S(1)} %get-tuple-element.27), channel_id=1, source_target_pairs={{0,1},{1,0},{2,3},{3,2},{4,5},{5,4},{6,7},{7,6},{8,9},{9,8},{10,11... | collective-permute-start | bytes 589832 | tf_op jit(solution)/shard_map/ppermute | solution.py:418
  110.1 1.1 collective-permute-done.2.arrived_ref
  111.2 0.7 finish.1
Async XLA Ops:
  8.5 47.5 %copy-start.4 = (bf16[16,128,128]{2,1,0:T(8,128)(2,1)S(1)}, bf16[16,128,128]{2,1,0:T(8,128)(2,1)}, u32[]{:S(2)}) copy-start(bf16[16,128,128]{2,1,0:T(8,128)(2,1)} %get-tuple-element.17.own_hbm) | copy-start | bytes 1572868
  8.5 47.5 %copy-start.5 = (f32[16,64,128]{2,1,0:T(8,128)S(1)}, f32[16,64,128]{2,1,0:T(8,128)}, u32[]{:S(2)}) copy-start(f32[16,64,128]{2,1,0:T(8,128)} %get-tuple-element.18.side_hbm) | copy-start | bytes 1572868
  8.5 47.5 %copy-start.6 = (bf16[16,64,128]{2,1,0:T(8,128)(2,1)S(1)}, bf16[16,64,128]{2,1,0:T(8,128)(2,1)}, u32[]{:S(2)}) copy-start(bf16[16,64,128]{2,1,0:T(8,128)(2,1)} %get-tuple-element.16.qd_hbm) | copy-start | bytes 786436
  8.5 94.6 %copy-start.3 = (bf16[1024,1024]{1,0:T(8,128)(2,1)S(1)}, bf16[1024,1024]{1,0:T(8,128)(2,1)}, u32[]{:S(2)}) copy-start(bf16[1024,1024]{1,0:T(8,128)(2,1)} %wo.1) | copy-start | bytes 6291460
  51.5 4.5 %collective-permute-start = (bf16[128,8,2,128]{3,2,1,0:T(2,128)(2,1)S(1)}, bf16[128,8,2,128]{3,2,1,0:T(2,128)(2,1)S(1)}, u32[]{:S(2)}, u32[]{:S(2)}) collective-permute-start(bf16[128,8,2,128]{3,2,1,0:T(2,128)(2,1)S(1)} %slice.4), channel_id=1, source_target_pairs={{0,1},{1,0},{2,3},{3,2},{4,5},{5,4},{6,7},{7,6},{8,9},{9,8},{10,11... | collective-permute-start | bytes 1572872 | tf_op jit(solution)/shard_map/ppermute | solution.py:418
  56.0 47.1 %copy-start.2 = (bf16[1024,1024]{1,0:T(8,128)(2,1)S(1)}, bf16[1024,1024]{1,0:T(8,128)(2,1)}, u32[]{:S(2)}) copy-start(bf16[1024,1024]{1,0:T(8,128)(2,1)} %wv.1) | copy-start | bytes 6291460
  67.6 2.2 %collective-permute-start.1 = (bf16[128,8,2,128]{3,2,1,0:T(2,128)(2,1)S(1)}, bf16[128,8,2,128]{3,2,1,0:T(2,128)(2,1)S(1)}, u32[]{:S(2)}, u32[]{:S(2)}) collective-permute-start(bf16[128,8,2,128]{3,2,1,0:T(2,128)(2,1)S(1)} %get-tuple-element.20), channel_id=1, source_target_pairs={{0,1},{1,0},{2,3},{3,2},{4,5},{5,4},{6,7},{7,6},{8,9},{9,8},{10,11... | collective-permute-start | bytes 1572872 | tf_op jit(solution)/shard_map/ppermute | solution.py:418
  69.8 33.2 %copy-start = (bf16[1024,1024]{1,0:T(8,128)(2,1)S(1)}, bf16[1024,1024]{1,0:T(8,128)(2,1)}, u32[]{:S(2)}) copy-start(bf16[1024,1024]{1,0:T(8,128)(2,1)} %wq.1) | copy-start | bytes 6291460
  69.9 33.2 %copy-start.1 = (bf16[1024,1024]{1,0:T(8,128)(2,1)S(1)}, bf16[1024,1024]{1,0:T(8,128)(2,1)}, u32[]{:S(2)}) copy-start(bf16[1024,1024]{1,0:T(8,128)(2,1)} %wk.1) | copy-start | bytes 6291460
  69.9 33.3 %copy-start.7 = (s32[1,128]{1,0:T(1,128)S(1)}, s32[1,128]{1,0:T(1,128)}, u32[]{:S(2)}) copy-start(s32[1,128]{1,0:T(1,128)} %asg_ref.1) | copy-start | bytes 1540
  108.2 2.9 %collective-permute-start.2 = (bf16[192,512]{1,0:T(8,128)(2,1)S(1)}, bf16[192,512]{1,0:T(8,128)(2,1)S(1)}, u32[]{:S(2)}, u32[]{:S(2)}) collective-permute-start(bf16[192,512]{1,0:T(8,128)(2,1)S(1)} %get-tuple-element.27), channel_id=1, source_target_pairs={{0,1},{1,0},{2,3},{3,2},{4,5},{5,4},{6,7},{7,6},{8,9},{9,8},{10,11... | collective-permute-start | bytes 589832 | tf_op jit(solution)/shard_map/ppermute | solution.py:418
